TPU v7x, 128 devices: a whole 4x4x4 slice. The times are simulated.
128 devices in a mesh: gx: 8 (over z, core), gy: 4 (over x), gz: 4 (over y).
Axes of the slice: x: 4, y: 4, z: 4, core: 2. Of those that a mesh axis runs over, the one named last changes fastest.
Arguments:
- fields: bfloat16 [131072, 4, 512], P(('gx', 'gy', 'gz')), may hold values from -16 to 16
- jacobian: bfloat16 [131072, 512], P(('gx', 'gy', 'gz')), may hold values from 0.25 to 4
- home_slot: int32 [131072], P(('gx', 'gy', 'gz')), may hold values from 0 to 131071, as said below
Outputs:
- mid_level: float32 [4, 64, 256, 512], P(None, 'gx', 'gy', 'gz')
- coarse_level: float32 [4, 32, 128, 256], P(None, 'gx', 'gy', 'gz')
Inputs may be any that keep to these rules, and one draw needn't show every extreme that they name: home_slot is a permutation of the lattice slots. Slot s lies in the brick of device s // 1024 in the order gx, gy, gz (gx slowest). Each element's brick is the holder's own or one whose brick coordinates differ from the holder's by one in exactly one direction, without wrap-around. One device sends at most 16 elements to any other brick, and in every draw some device sends exactly 16 to a neighbour along gx.
All inputs are finite; a program needn't handle non-finite values.
Results may differ from a plain program's by a relative error of at most 0.0033.
Values may be sent and summed in bfloat16 or wider, within the bound.
No kernel may reach another device: no remote copies, remote signals or barrier semaphores. Data moves between devices by JAX's collectives and lax.ppermute only.
A program may use at most 192 MiB of HBM per device.

v0:
```python
import jax
import jax.numpy as jnp
import numpy as np
from jax import lax
from jax.sharding import PartitionSpec as P

EX = 2
EY = 16
EZ = 32
CAP = 16


GLL_NODES = np.array(
    [
        -1.0,
        -0.8717401485096066,
        -0.5917001814331423,
        -0.2092992179024789,
        0.2092992179024789,
        0.5917001814331423,
        0.8717401485096066,
        1.0,
    ]
)


def shifted(x, axis, by):
    size = lax.axis_size(axis)
    pairs = [(i, i + by) for i in range(size) if 0 <= i + by < size]
    return lax.ppermute(x, axis, pairs)


def extended(block, sides, width):
    for axis, dim in sides:
        count = lax.axis_size(axis)
        forward = [(i, i + 1) for i in range(count - 1)]
        backward = [(target, source) for source, target in forward]
        low = lax.ppermute(
            lax.slice_in_dim(block, block.shape[dim] - width, None, axis=dim), axis, forward
        )
        high = lax.ppermute(lax.slice_in_dim(block, 0, width, axis=dim), axis, backward)
        block = jnp.concatenate([low, block, high], axis=dim)
    return block


def gll_basis():
    targets = -1.0 + (2.0 * np.arange(8) + 1.0) / 8.0
    basis_table = np.ones((8, 8))
    for node_index in range(8):
        for other_index in range(8):
            if other_index != node_index:
                basis_table[:, node_index] *= (targets - GLL_NODES[other_index]) / (
                    GLL_NODES[node_index] - GLL_NODES[other_index]
                )
    return basis_table


def plain_sinc(points):
    return np.sin(np.pi * points) / (np.pi * points)


def lanczos_taps():
    offsets = np.arange(8) - 3.5
    sample_values = plain_sinc(offsets / 2.0) * plain_sinc(offsets / 4.0)
    return sample_values / np.sum(sample_values)


def band_table(in_length, out_length):
    filter_weight_vector = lanczos_taps()
    table = np.zeros((in_length, out_length))
    for column in range(out_length):
        table[2 * column : 2 * column + 8, column] = filter_weight_vector
    return jnp.asarray(table, jnp.float32)


def pass_depth(volume_block, first_level):
    depth_in = volume_block.shape[3]
    table_z = band_table(depth_in, (depth_in - 6) // 2)
    if first_level:
        return jnp.einsum(
            "fabc,cz->fabz",
            volume_block,
            table_z.astype(jnp.bfloat16),
            preferred_element_type=jnp.float32,
        )
    return jnp.einsum("fabc,cz->fabz", volume_block, table_z, precision=lax.Precision.HIGHEST)


def pass_width(volume_block):
    width_in = volume_block.shape[2]
    table_y = band_table(width_in, (width_in - 6) // 2)
    return jnp.einsum("fabz,by->fayz", volume_block, table_y, precision=lax.Precision.HIGHEST)


def pass_length(volume_block):
    length_in = volume_block.shape[1]
    table_x = band_table(length_in, (length_in - 6) // 2)
    return jnp.einsum("fayz,ax->fxyz", volume_block, table_x, precision=lax.Precision.HIGHEST)


def filter_level(volume_block, first_level):
    return pass_length(pass_width(pass_depth(volume_block, first_level)))


def interp_tables():
    basis_table = gll_basis()
    kron_table = np.kron(basis_table, np.kron(basis_table, basis_table)).T
    full_table = jnp.asarray(kron_table, jnp.float32)
    high_part = full_table.astype(jnp.bfloat16)
    low_part = (full_table - high_part.astype(jnp.float32)).astype(jnp.bfloat16)
    return (high_part, low_part)


def place_rows(brick_sum, arrived, arrived_tags, elem_count):
    row_ids = jnp.arange(elem_count, dtype=jnp.int32)
    selector = (row_ids[:, None] == (arrived_tags - 1)[None, :]).astype(jnp.bfloat16)
    arrived_flat = arrived.reshape(arrived.shape[0], 2048)
    return brick_sum + jnp.dot(selector, arrived_flat, preferred_element_type=jnp.float32)


def running_count(lower_ones, selected):
    return (
        jnp.dot(
            lower_ones, selected.astype(jnp.bfloat16), preferred_element_type=jnp.float32
        ).astype(jnp.int32)
        - 1
    )


def pack_rows(uniform_flat, selected, place, capacity, lower_ones):
    ranking = running_count(lower_ones, selected)
    slot_ids = jnp.arange(capacity, dtype=jnp.int32)
    picker = (slot_ids[:, None] == ranking[None, :]) & selected[None, :]
    outgoing = jnp.dot(
        picker.astype(jnp.bfloat16), uniform_flat, preferred_element_type=jnp.float32
    )
    outgoing = outgoing.astype(jnp.bfloat16).reshape(capacity, 4, 512)
    slot_tags = jnp.sum(jnp.where(picker, (place + 1)[None, :], 0), 1)
    return (outgoing, slot_tags)


def body(fields, jacobian, home_slot):
    elem_count = fields.shape[0]
    size_y = lax.axis_size("gy")
    size_z = lax.axis_size("gz")
    index_x = lax.axis_index("gx")
    index_y = lax.axis_index("gy")
    index_z = lax.axis_index("gz")
    my_device = (index_x * size_y + index_y) * size_z + index_z
    high_part, low_part = interp_tables()
    flat_rows = fields.reshape(elem_count * 4, 512)
    sample_values = jnp.dot(flat_rows, high_part, preferred_element_type=jnp.float32) + jnp.dot(
        flat_rows, low_part, preferred_element_type=jnp.float32
    )
    uniform = (
        sample_values.reshape(elem_count, 4, 512) * jacobian.astype(jnp.float32)[:, None, :]
    ).astype(jnp.bfloat16)
    uniform_flat = uniform.reshape(elem_count, 2048)
    target = home_slot // elem_count
    place = home_slot % elem_count
    stays = target == my_device
    row_ids = jnp.arange(elem_count, dtype=jnp.int32)
    keeper = ((row_ids[:, None] == place[None, :]) & stays[None, :]).astype(jnp.bfloat16)
    brick_sum = jnp.dot(keeper, uniform_flat, preferred_element_type=jnp.float32)
    lower_ones = (row_ids[:, None] >= row_ids[None, :]).astype(jnp.bfloat16)
    target_x = target // (size_y * size_z)
    target_y = target // size_z % size_y
    target_z = target % size_z
    for offset in (1, -1):
        outgoing, slot_tags = pack_rows(
            uniform_flat, target_x == index_x + offset, place, CAP, lower_ones
        )
        arrived, arrived_tags = shifted((outgoing, slot_tags), "gx", offset)
        brick_sum = place_rows(brick_sum, arrived, arrived_tags, elem_count)
    for offset in (1, -1):
        outgoing, slot_tags = pack_rows(
            uniform_flat, target_y == index_y + offset, place, CAP, lower_ones
        )
        arrived, arrived_tags = shifted((outgoing, slot_tags), "gy", offset)
        brick_sum = place_rows(brick_sum, arrived, arrived_tags, elem_count)
    for offset in (1, -1):
        outgoing, slot_tags = pack_rows(
            uniform_flat, target_z == index_z + offset, place, CAP, lower_ones
        )
        arrived, arrived_tags = shifted((outgoing, slot_tags), "gz", offset)
        brick_sum = place_rows(brick_sum, arrived, arrived_tags, elem_count)
    brick = brick_sum.astype(jnp.bfloat16)
    volume_block = brick.reshape(EX, EY, EZ, 4, 8, 8, 8)
    volume_block = volume_block.transpose(3, 0, 4, 1, 5, 2, 6).reshape(4, EX * 8, EY * 8, EZ * 8)
    padded = extended(volume_block, (("gx", 1), ("gy", 2), ("gz", 3)), 3)
    mid_level = filter_level(padded, True)
    padded_mid = extended(mid_level, (("gx", 1), ("gy", 2), ("gz", 3)), 3)
    coarse_level = filter_level(padded_mid, False)
    return (mid_level, coarse_level)


def solution(mesh):
    placed = (P(("gx", "gy", "gz"), None, None), P(("gx", "gy", "gz"), None), P(("gx", "gy", "gz")))
    return jax.shard_map(
        body,
        mesh=mesh,
        in_specs=placed,
        out_specs=(P(None, "gx", "gy", "gz"), P(None, "gx", "gy", "gz")),
        check_vma=False,
    )
```

profile of v0, /device:TPU:32, one launch (start us, length us, event | category | flops | bytes accessed | tf_op | source)
XLA Modules:
  0.0 475.0 jit_solution(9394739755878628094)
XLA Ops:
  5.9 1.9 collective-permute-start.2
  7.9 3.4 collective-permute-start.4
  12.6 4.5 collective-permute-start.8
  17.1 6.9 %reshape.77 = bf16[4096,512]{1,0:T(8,128)(2,1)} reshape(bf16[1024,4,512]{2,1,0:T(4,128)(2,1)} %param.10) | data formatting | bytes 8388608 | tf_op jit(solution)/shard_map/reshape | solution.py:151
  24.0 4.7 fusion.77
  28.8 5.7 %add_bitcast_fusion = f32[4096,512]{0,1:T(8,128)} fusion(f32[512,4096]{1,0:T(8,128)S(1)} %fusion.77, bf16[512,512]{1,0:T(8,128)(2,1)S(1)} %copy-done.8, bf16[4096,512]{1,0:T(8,128)(2,1)S(1)} %copy-done.1), kind=kOutput, calls=%fused_computation.10 | convolution fusion | flops 2149580800 | bytes 21495808 | tf_op jit(solution)/shard_map/dot_general | solution.py:152
  34.5 9.0 %copy.35 = f32[4096,512]{1,0:T(8,128)} copy(f32[4096,512]{0,1:T(8,128)} %add_bitcast_fusion) | data formatting | bytes 16777216 | tf_op jit(solution)/shard_map/add | solution.py:152
  43.5 11.2 %reshape.78 = f32[1024,2048]{1,0:T(8,128)} reshape(f32[4096,512]{1,0:T(8,128)} %copy.35) | data formatting | bytes 16777216 | tf_op jit(solution)/shard_map/reshape | solution.py:156
  54.6 4.4 mul.19
  59.0 10.7 %copy.56 = f32[128,8,4,512]{3,1,2,0:T(8,128)} copy(f32[128,8,4,512]{3,2,1,0:T(4,128)} %bitcast.83) | data formatting | bytes 16777216
  69.8 7.2 %multiply_convert_fusion = bf16[1024,2048]{1,0:T(8,128)(2,1)S(1)} fusion(f32[1024,2048]{1,0:T(8,128)} %reshape.78, f32[1024,2048]{1,0:T(8,128)} %bitcast.82), kind=kLoop, calls=%fused_computation.12 | loop fusion | flops 4194304 | bytes 20971520 | tf_op jit(solution)/shard_map/convert_element_type | solution.py:157
  81.2 9.1 %fusion.17 = f32[1024,2048]{1,0:T(8,128)} fusion(bf16[1024,2048]{1,0:T(8,128)(2,1)} %copy-done, s32[1024]{0:T(1024)S(1)} %get-tuple-element.32, pred[1024]{0:T(1024)(128)(4,1)S(1)} %get-tuple-element.16), kind=kOutput, calls=%fused_computation.24 | convolution fusion | flops 4297064448 | bytes 12588032 | tf_op jit(solution)/shard_map/dot_general | solution.py:164
  90.3 1.9 collective-permute-start
  92.3 3.9 collective-permute-start.1
  96.2 1.9 collective-permute-start.3
  98.2 4.5 collective-permute-start.5
  104.1 3.5 collective-permute-start.9
  109.5 4.3 collective-permute-done.11
  113.7 4.5 fusion.33
  118.2 4.5 fusion.32
  122.7 4.5 fusion.31
  127.2 4.5 fusion.30
  131.7 4.5 fusion.29
  136.1 19.0 %add_convert_fusion = bf16[1024,2048]{1,0:T(8,128)(2,1)} fusion(f32[1024,2048]{1,0:T(8,128)} %fusion.33, f32[1024,2048]{1,0:T(8,128)} %fusion.32, f32[1024,2048]{1,0:T(8,128)} %fusion.31, f32[1024,2048]{1,0:T(8,128)} %fusion.30, f32[1024,2048]{1,0:T(8,128)} %fusion.17, f32[1024,2048]{1,0:T(8,128)} %fusion.29, bf16[16,2048]{1,0:T(8,128)(2,1)S(1)} %bitcast.87, ...), kind=kOutput, calls=%fused_computation.11 | convolution fusion | flops 81805312 | bytes 54591552 | tf_op jit(solution)/shard_map/dot_general | solution.py:118
  155.1 6.4 %copy.36 = bf16[1024,2048]{0,1:T(8,128)(2,1)} copy(bf16[1024,2048]{1,0:T(8,128)(2,1)} %add_convert_fusion) | data formatting | bytes 8388608 | tf_op jit(solution)/shard_map/convert_element_type | solution.py:187
  161.6 20.3 %reshape.91 = bf16[2,16,32,4,8,8,8]{2,1,0,6,5,4,3:T(8,128)(2,1)} reshape(bf16[1024,2048]{0,1:T(8,128)(2,1)} %copy.36) | data formatting | bytes 8388608 | tf_op jit(solution)/shard_map/reshape | solution.py:188
  181.8 55.5 %copy.37 = bf16[4,2,8,16,8,32,8]{6,5,4,3,2,1,0:T(8,128)(2,1)} copy(bf16[4,2,8,16,8,32,8]{5,3,1,6,4,2,0:T(8,128)(2,1)} %bitcast.81) | data formatting | bytes 8388608 | tf_op jit(solution)/shard_map/transpose | solution.py:189
  237.4 92.6 %reshape.92 = bf16[4,16,128,256]{3,2,1,0:T(8,128)(2,1)} reshape(bf16[4,2,8,16,8,32,8]{6,5,4,3,2,1,0:T(8,128)(2,1)} %copy.37) | data formatting | bytes 8388608 | tf_op jit(solution)/shard_map/reshape | solution.py:189
  330.0 1.6 fusion.74
  331.7 2.1 collective-permute-start.12
  333.7 3.6 collective-permute-start.13
  337.4 7.7 %collective-permute-done.12 = bf16[4,3,128,256]{3,2,1,0:T(8,128)(2,1)S(1)} collective-permute-done((bf16[4,3,128,256]{3,2,1,0:T(8,128)(2,1)S(1)}, bf16[4,3,128,256]{3,2,1,0:T(8,128)(2,1)S(1)}, u32[]{:S(2)}, u32[]{:S(2)}) %collective-permute-start.12) | collective-permute-done | bytes 786464 | tf_op jit(solution)/shard_map/ppermute | solution.py:38
  345.5 1.4 collective-permute-done.13
  347.1 4.6 collective-permute-start.14
  353.0 2.7 collective-permute-done.14
  355.7 4.7 collective-permute-done.15
  360.4 4.0 pad_maximum_fusion
  364.4 3.0 fusion.72
  367.4 4.4 copy.38
  371.9 4.1 collective-permute-start.16
  376.0 3.9 copy.39
  381.2 3.1 copy.40
  384.3 3.5 collective-permute-done.17
  387.8 3.8 copy.41
  391.5 10.2 %fusion = f32[4,22,134,128]{3,2,1,0:T(8,128)S(1)} fusion(bf16[262,128,1,1]{1,0,3,2:T(8,128)(2,1)S(1)} %copy-done.15, bf16[4,22,134,3]{3,2,1,0:T(8,128)(2,1)} %copy.41, bf16[4,22,3,256]{3,2,1,0:T(4,128)(2,1)S(1)} %collective-permute-done.15, bf16[4,22,128,256]{3,2,1,0:T(8,128)(2,1)} %copy-done.3, bf16[4,22,3,256]{3,2,1,0:T(4,128)(2,1)S(1)} %collective-permute-done.14, ...), kind=kOutput, calls=%fused_computation | convolution fusion | flops 821808064 | bytes 12283584 | tf_op jit(solution)/shard_map/fabc,cz->fabz/dot_general | solution.py:80
  401.7 5.3 %convolution_bitcast_fusion = f32[4,22,64,128]{3,2,1,0:T(8,128)S(1)} fusion(f32[4,22,134,128]{3,2,1,0:T(8,128)S(1)} %fusion, f32[134,64,1,1]{0,1,3,2:T(8,128)S(1)} %copy-done.9), kind=kOutput, calls=%fused_computation.38 | convolution fusion | flops 1159200768 | bytes 8955392 | tf_op jit(solution)/shard_map/fabz,by->fayz/dot_general | solution.py:92
  407.1 3.7 fusion.25
  411.0 1.9 collective-permute-start.18
  412.9 3.6 collective-permute-start.19
  416.6 4.9 %collective-permute-done.18 = f32[4,3,64,128]{3,1,2,0:T(4,128)S(1)} collective-permute-done((f32[4,3,64,128]{3,1,2,0:T(4,128)S(1)}, f32[4,3,64,128]{3,1,2,0:T(4,128)S(1)}, u32[]{:S(2)}, u32[]{:S(2)}) %collective-permute-start.18) | collective-permute-done | bytes 393248 | tf_op jit(solution)/shard_map/ppermute | solution.py:38
  421.5 1.8 collective-permute-done.19
  423.3 3.6 collective-permute-start.20
  429.1 4.7 collective-permute-done.21
  434.3 2.2 fusion.75
  436.5 3.3 copy.43
  439.8 2.2 collective-permute-start.22
  442.0 1.8 copy.44
  446.2 2.0 copy.45
  448.2 2.4 collective-permute-done.23
  450.5 3.2 copy.46
  453.8 5.8 %pad_maximum_fusion.1 = f32[4,14,70,134]{3,1,2,0:T(8,128)S(1)} fusion(f32[4,14,70,3]{3,1,2,0:T(8,128)} %copy.46, f32[4,14,3,128]{3,1,2,0:T(8,128)S(1)} %collective-permute-done.21, f32[4,3,64,128]{3,1,2,0:T(4,128)} %copy-done.5, f32[4,8,64,128]{3,1,2,0:T(8,128)S(1)} %fusion.25, f32[4,3,64,128]{3,1,2,0:T(4,128)} %copy-done.4, ...), kind=kLoop, calls=%fused_computation.14 | loop fusion | flops 3151680 | bytes 4202240 | tf_op jit(solution)/shard_map/concatenate | solution.py:42
  459.6 7.9 %fusion.19 = f32[4,14,70,64]{2,3,1,0:T(8,128)S(1)} fusion(f32[134,64,1,1]{0,1,3,2:T(8,128)S(1)} %copy-done.10, f32[4,14,70,134]{3,1,2,0:T(8,128)S(1)} %pad_maximum_fusion.1), kind=kOutput, calls=%fused_computation.25 | convolution fusion | flops 403415040 | bytes 3138944 | tf_op jit(solution)/shard_map/fabc,cz->fabz/dot_general | solution.py:86
  467.5 5.1 %convolution_bitcast_fusion.1 = f32[4,14,32,64]{3,2,1,0:T(8,128)S(1)} fusion(f32[4,14,70,64]{2,3,1,0:T(8,128)S(1)} %fusion.19, f32[70,32,1,1]{0,1,3,2:T(8,128)S(1)} %copy-done.11), kind=kOutput, calls=%fused_computation.40 | convolution fusion | flops 96337920 | bytes 1471232 | tf_op jit(solution)/shard_map/fabz,by->fayz/dot_general | solution.py:92
  472.6 1.4 convolution_bitcast_fusion.2
  (107 shorter events, 23.0 us)
Async XLA Ops:
  0.6 3.7 copy-start.12
  3.9 20.1 %copy-start.7 = (bf16[512,512]{1,0:T(8,128)(2,1)S(1)}, bf16[512,512]{1,0:T(8,128)(2,1)}, u32[]{:S(2)}) copy-start(bf16[512,512]{1,0:T(8,128)(2,1)} %constant.111) | copy-start | bytes 1572868
  4.6 85.7 %collective-permute-start.10 = (s32[16]{0:T(128)S(1)}, s32[16]{0:T(128)S(1)}, u32[]{:S(2)}, u32[]{:S(2)}) collective-permute-start(s32[16]{0:T(128)S(1)} %get-tuple-element.10), channel_id=1, source_target_pairs={{1,0},{2,1},{3,2},{5,4},{6,5},{7,6},{9,8},{10,9},{11,10},{13,12},{... | collective-permute-start | bytes 200 | tf_op jit(solution)/shard_map/ppermute | solution.py:30
  5.9 86.3 %collective-permute-start.2 = (s32[16]{0:T(128)S(1)}, s32[16]{0:T(128)S(1)}, u32[]{:S(2)}, u32[]{:S(2)}) collective-permute-start(s32[16]{0:T(128)S(1)} %get-tuple-element.11), channel_id=1, source_target_pairs={{16,0},{32,16},{48,32},{64,48},{80,64},{96,80},{112,96},{17,1},{33... | collective-permute-start | bytes 200 | tf_op jit(solution)/shard_map/ppermute | solution.py:30
  7.9 88.4 %collective-permute-start.4 = (s32[16]{0:T(128)S(1)}, s32[16]{0:T(128)S(1)}, u32[]{:S(2)}, u32[]{:S(2)}) collective-permute-start(s32[16]{0:T(128)S(1)} %get-tuple-element.12), channel_id=1, source_target_pairs={{0,4},{4,8},{8,12},{1,5},{5,9},{9,13},{2,6},{6,10},{10,14},{3,7},{... | collective-permute-start | bytes 200 | tf_op jit(solution)/shard_map/ppermute | solution.py:30
  11.3 86.9 %collective-permute-start.6 = (s32[16]{0:T(128)S(1)}, s32[16]{0:T(128)S(1)}, u32[]{:S(2)}, u32[]{:S(2)}) collective-permute-start(s32[16]{0:T(128)S(1)} %get-tuple-element.13), channel_id=1, source_target_pairs={{4,0},{8,4},{12,8},{5,1},{9,5},{13,9},{6,2},{10,6},{14,10},{7,3},{... | collective-permute-start | bytes 200 | tf_op jit(solution)/shard_map/ppermute | solution.py:30
  12.6 90.2 %collective-permute-start.8 = (s32[16]{0:T(128)S(1)}, s32[16]{0:T(128)S(1)}, u32[]{:S(2)}, u32[]{:S(2)}) collective-permute-start(s32[16]{0:T(128)S(1)} %get-tuple-element.14), channel_id=1, source_target_pairs={{0,1},{1,2},{2,3},{4,5},{5,6},{6,7},{8,9},{9,10},{10,11},{12,13},{... | collective-permute-start | bytes 200 | tf_op jit(solution)/shard_map/ppermute | solution.py:30
  24.0 4.8 %copy-start.1 = (bf16[4096,512]{1,0:T(8,128)(2,1)S(1)}, bf16[4096,512]{1,0:T(8,128)(2,1)}, u32[]{:S(2)}) copy-start(bf16[4096,512]{1,0:T(8,128)(2,1)} %reshape.77) | copy-start | bytes 12582916
  24.0 4.8 %copy-start.8 = (bf16[512,512]{1,0:T(8,128)(2,1)S(1)}, bf16[512,512]{1,0:T(8,128)(2,1)}, u32[]{:S(2)}) copy-start(bf16[512,512]{1,0:T(8,128)(2,1)} %constant.114) | copy-start | bytes 1572868
  43.5 11.2 %copy-start.6 = (bf16[1024,512]{1,0:T(8,128)(2,1)S(1)}, bf16[1024,512]{1,0:T(8,128)(2,1)}, u32[]{:S(2)}) copy-start(bf16[1024,512]{1,0:T(8,128)(2,1)} %param.11) | copy-start | bytes 3145732
  77.0 3.3 copy-start
  90.3 13.7 %collective-permute-start = (s32[16]{0:T(128)S(1)}, s32[16]{0:T(128)S(1)}, u32[]{:S(2)}, u32[]{:S(2)}) collective-permute-start(s32[16]{0:T(128)S(1)} %get-tuple-element.15), channel_id=1, source_target_pairs={{0,16},{16,32},{32,48},{48,64},{64,80},{80,96},{96,112},{1,17},{17... | collective-permute-start | bytes 200 | tf_op jit(solution)/shard_map/ppermute | solution.py:30
  92.3 15.3 %collective-permute-start.1 = (bf16[16,4,512]{2,1,0:T(4,128)(2,1)S(1)}, bf16[16,4,512]{2,1,0:T(4,128)(2,1)S(1)}, u32[]{:S(2)}, u32[]{:S(2)}) collective-permute-start(bf16[16,4,512]{2,1,0:T(4,128)(2,1)S(1)} %reshape.79), channel_id=1, source_target_pairs={{0,16},{16,32},{32,48},{48,64},{64,80},{80,96},{96,112},{1,17},{17... | collective-permute-start | bytes 196616 | tf_op jit(solution)/shard_map/ppermute | solution.py:30
  96.2 12.7 %collective-permute-start.3 = (bf16[16,4,512]{2,1,0:T(4,128)(2,1)S(1)}, bf16[16,4,512]{2,1,0:T(4,128)(2,1)S(1)}, u32[]{:S(2)}, u32[]{:S(2)}) collective-permute-start(bf16[16,4,512]{2,1,0:T(4,128)(2,1)S(1)} %reshape.81), channel_id=1, source_target_pairs={{16,0},{32,16},{48,32},{64,48},{80,64},{96,80},{112,96},{17,1},{33... | collective-permute-start | bytes 196616 | tf_op jit(solution)/shard_map/ppermute | solution.py:30
  98.2 10.8 %collective-permute-start.5 = (bf16[16,4,512]{2,1,0:T(4,128)(2,1)S(1)}, bf16[16,4,512]{2,1,0:T(4,128)(2,1)S(1)}, u32[]{:S(2)}, u32[]{:S(2)}) collective-permute-start(bf16[16,4,512]{2,1,0:T(4,128)(2,1)S(1)} %reshape.83), channel_id=1, source_target_pairs={{0,4},{4,8},{8,12},{1,5},{5,9},{9,13},{2,6},{6,10},{10,14},{3,7},{... | collective-permute-start | bytes 196616 | tf_op jit(solution)/shard_map/ppermute | solution.py:30
  102.7 6.2 %collective-permute-start.7 = (bf16[16,4,512]{2,1,0:T(4,128)(2,1)S(1)}, bf16[16,4,512]{2,1,0:T(4,128)(2,1)S(1)}, u32[]{:S(2)}, u32[]{:S(2)}) collective-permute-start(bf16[16,4,512]{2,1,0:T(4,128)(2,1)S(1)} %reshape.85), channel_id=1, source_target_pairs={{4,0},{8,4},{12,8},{5,1},{9,5},{13,9},{6,2},{10,6},{14,10},{7,3},{... | collective-permute-start | bytes 196616 | tf_op jit(solution)/shard_map/ppermute | solution.py:30
  104.1 5.4 %collective-permute-start.9 = (bf16[16,4,512]{2,1,0:T(4,128)(2,1)S(1)}, bf16[16,4,512]{2,1,0:T(4,128)(2,1)S(1)}, u32[]{:S(2)}, u32[]{:S(2)}) collective-permute-start(bf16[16,4,512]{2,1,0:T(4,128)(2,1)S(1)} %reshape.87), channel_id=1, source_target_pairs={{0,1},{1,2},{2,3},{4,5},{5,6},{6,7},{8,9},{9,10},{10,11},{12,13},{... | collective-permute-start | bytes 196616 | tf_op jit(solution)/shard_map/ppermute | solution.py:30
  107.6 6.2 %collective-permute-start.11 = (bf16[16,4,512]{2,1,0:T(4,128)(2,1)S(1)}, bf16[16,4,512]{2,1,0:T(4,128)(2,1)S(1)}, u32[]{:S(2)}, u32[]{:S(2)}) collective-permute-start(bf16[16,4,512]{2,1,0:T(4,128)(2,1)S(1)} %reshape.89), channel_id=1, source_target_pairs={{1,0},{2,1},{3,2},{5,4},{6,5},{7,6},{9,8},{10,9},{11,10},{13,12},{... | collective-permute-start | bytes 196616 | tf_op jit(solution)/shard_map/ppermute | solution.py:30
  330.0 15.1 %copy-start.2 = (bf16[4,16,128,256]{3,2,1,0:T(8,128)(2,1)S(1)}, bf16[4,16,128,256]{3,2,1,0:T(8,128)(2,1)}, u32[]{:S(2)}) copy-start(bf16[4,16,128,256]{3,2,1,0:T(8,128)(2,1)} %reshape.92) | copy-start | bytes 12582916
  331.7 13.4 %collective-permute-start.12 = (bf16[4,3,128,256]{3,2,1,0:T(8,128)(2,1)S(1)}, bf16[4,3,128,256]{3,2,1,0:T(8,128)(2,1)S(1)}, u32[]{:S(2)}, u32[]{:S(2)}) collective-permute-start(bf16[4,3,128,256]{3,2,1,0:T(8,128)(2,1)S(1)} %get-tuple-element.25), channel_id=1, source_target_pairs={{0,16},{16,32},{32,48},{48,64},{64,80},{80,96},{96,112},{1,17},{17... | collective-permute-start | bytes 2359304 | tf_op jit(solution)/shard_map/ppermute | solution.py:38
  333.7 13.1 %collective-permute-start.13 = (bf16[4,3,128,256]{3,2,1,0:T(8,128)(2,1)S(1)}, bf16[4,3,128,256]{3,2,1,0:T(8,128)(2,1)S(1)}, u32[]{:S(2)}, u32[]{:S(2)}) collective-permute-start(bf16[4,3,128,256]{3,2,1,0:T(8,128)(2,1)S(1)} %get-tuple-element.24), channel_id=1, source_target_pairs={{16,0},{32,16},{48,32},{64,48},{80,64},{96,80},{112,96},{17,1},{33... | collective-permute-start | bytes 2359304 | tf_op jit(solution)/shard_map/ppermute | solution.py:41
  346.9 17.5 %copy-start.3 = (bf16[4,22,128,256]{3,2,1,0:T(8,128)(2,1)}, bf16[4,22,128,256]{3,2,1,0:T(8,128)(2,1)S(1)}, u32[]{:S(2)}) copy-start(bf16[4,22,128,256]{3,2,1,0:T(8,128)(2,1)S(1)} %constant_dynamic-update-slice_fusion) | copy-start | bytes 17301508
  347.1 8.6 %collective-permute-start.14 = (bf16[4,22,3,256]{3,2,1,0:T(4,128)(2,1)S(1)}, bf16[4,22,3,256]{3,2,1,0:T(4,128)(2,1)S(1)}, u32[]{:S(2)}, u32[]{:S(2)}) collective-permute-start(bf16[4,22,3,256]{3,2,1,0:T(4,128)(2,1)S(1)} %get-tuple-element.22), channel_id=1, source_target_pairs={{0,4},{4,8},{8,12},{1,5},{5,9},{9,13},{2,6},{6,10},{10,14},{3,7},{... | collective-permute-start | bytes 405512 | tf_op jit(solution)/shard_map/ppermute | solution.py:38
  351.7 8.7 %collective-permute-start.15 = (bf16[4,22,3,256]{3,2,1,0:T(4,128)(2,1)S(1)}, bf16[4,22,3,256]{3,2,1,0:T(4,128)(2,1)S(1)}, u32[]{:S(2)}, u32[]{:S(2)}) collective-permute-start(bf16[4,22,3,256]{3,2,1,0:T(4,128)(2,1)S(1)} %get-tuple-element.23), channel_id=1, source_target_pairs={{4,0},{8,4},{12,8},{5,1},{9,5},{13,9},{6,2},{10,6},{14,10},{7,3},{... | collective-permute-start | bytes 405512 | tf_op jit(solution)/shard_map/ppermute | solution.py:41
  371.9 9.3 %collective-permute-start.16 = (bf16[4,22,134,3]{2,0,3,1:T(4,128)(2,1)}, bf16[4,22,134,3]{2,0,3,1:T(4,128)(2,1)}, u32[]{:S(2)}, u32[]{:S(2)}) collective-permute-start(bf16[4,22,134,3]{2,0,3,1:T(4,128)(2,1)} %copy.38), channel_id=1, source_target_pairs={{0,1},{1,2},{2,3},{4,5},{5,6},{6,7},{8,9},{9,10},{10,11},{12,13},{... | collective-permute-start | bytes 212264 | tf_op jit(solution)/shard_map/ppermute | solution.py:38
  376.0 15.5 %copy-start.15 = (bf16[262,128,1,1]{1,0,3,2:T(8,128)(2,1)S(1)}, bf16[262,128,1,1]{1,0,3,2:T(8,128)(2,1)}, u32[]{:S(2)}) copy-start(bf16[262,128,1,1]{1,0,3,2:T(8,128)(2,1)} %constant.116) | copy-start | bytes 201220
  379.9 7.9 %collective-permute-start.17 = (bf16[4,22,134,3]{2,0,3,1:T(4,128)(2,1)}, bf16[4,22,134,3]{2,0,3,1:T(4,128)(2,1)}, u32[]{:S(2)}, u32[]{:S(2)}) collective-permute-start(bf16[4,22,134,3]{2,0,3,1:T(4,128)(2,1)} %copy.39), channel_id=1, source_target_pairs={{1,0},{2,1},{3,2},{5,4},{6,5},{7,6},{9,8},{10,9},{11,10},{13,12},{... | collective-permute-start | bytes 212264 | tf_op jit(solution)/shard_map/ppermute | solution.py:41
  391.5 10.2 %copy-start.9 = (f32[134,64,1,1]{0,1,3,2:T(8,128)S(1)}, f32[134,64,1,1]{0,1,3,2:T(8,128)}, u32[]{:S(2)}) copy-start(f32[134,64,1,1]{0,1,3,2:T(8,128)} %constant.117) | copy-start | bytes 102916
  401.7 5.4 %copy-start.13 = (f32[22,8,1,1]{0,1,3,2:T(8,128)S(1)}, f32[22,8,1,1]{0,1,3,2:T(8,128)}, u32[]{:S(2)}) copy-start(f32[22,8,1,1]{0,1,3,2:T(8,128)} %constant.118) | copy-start | bytes 2116
  411.0 10.5 %collective-permute-start.18 = (f32[4,3,64,128]{3,1,2,0:T(4,128)S(1)}, f32[4,3,64,128]{3,1,2,0:T(4,128)S(1)}, u32[]{:S(2)}, u32[]{:S(2)}) collective-permute-start(f32[4,3,64,128]{3,1,2,0:T(4,128)S(1)} %get-tuple-element.30), channel_id=1, source_target_pairs={{0,16},{16,32},{32,48},{48,64},{64,80},{80,96},{96,112},{1,17},{17... | collective-permute-start | bytes 1179656 | tf_op jit(solution)/shard_map/ppermute | solution.py:38
  412.9 10.3 %collective-permute-start.19 = (f32[4,3,64,128]{3,1,2,0:T(4,128)S(1)}, f32[4,3,64,128]{3,1,2,0:T(4,128)S(1)}, u32[]{:S(2)}, u32[]{:S(2)}) collective-permute-start(f32[4,3,64,128]{3,1,2,0:T(4,128)S(1)} %get-tuple-element.31), channel_id=1, source_target_pairs={{16,0},{32,16},{48,32},{64,48},{80,64},{96,80},{112,96},{17,1},{33... | collective-permute-start | bytes 1179656 | tf_op jit(solution)/shard_map/ppermute | solution.py:41
  421.5 12.4 %copy-start.4 = (f32[4,3,64,128]{3,1,2,0:T(4,128)}, f32[4,3,64,128]{3,1,2,0:T(4,128)S(1)}, u32[]{:S(2)}) copy-start(f32[4,3,64,128]{3,1,2,0:T(4,128)S(1)} %collective-permute-done.18) | copy-start | bytes 1179652
  423.2 10.6 %copy-start.5 = (f32[4,3,64,128]{3,1,2,0:T(4,128)}, f32[4,3,64,128]{3,1,2,0:T(4,128)S(1)}, u32[]{:S(2)}) copy-start(f32[4,3,64,128]{3,1,2,0:T(4,128)S(1)} %collective-permute-done.19) | copy-start | bytes 1179652
  423.3 5.9 %collective-permute-start.20 = (f32[4,14,3,128]{3,1,2,0:T(8,128)S(1)}, f32[4,14,3,128]{3,1,2,0:T(8,128)S(1)}, u32[]{:S(2)}, u32[]{:S(2)}) collective-permute-start(f32[4,14,3,128]{3,1,2,0:T(8,128)S(1)} %get-tuple-element.28), channel_id=1, source_target_pairs={{0,4},{4,8},{8,12},{1,5},{5,9},{9,13},{2,6},{6,10},{10,14},{3,7},{... | collective-permute-start | bytes 258056 | tf_op jit(solution)/shard_map/ppermute | solution.py:38
  426.9 7.0 %collective-permute-start.21 = (f32[4,14,3,128]{3,1,2,0:T(8,128)S(1)}, f32[4,14,3,128]{3,1,2,0:T(8,128)S(1)}, u32[]{:S(2)}, u32[]{:S(2)}) collective-permute-start(f32[4,14,3,128]{3,1,2,0:T(8,128)S(1)} %get-tuple-element.29), channel_id=1, source_target_pairs={{4,0},{8,4},{12,8},{5,1},{9,5},{13,9},{6,2},{10,6},{14,10},{7,3},{... | collective-permute-start | bytes 258056 | tf_op jit(solution)/shard_map/ppermute | solution.py:41
  439.8 6.4 %collective-permute-start.22 = (f32[4,14,70,3]{2,0,3,1:T(4,128)}, f32[4,14,70,3]{2,0,3,1:T(4,128)}, u32[]{:S(2)}, u32[]{:S(2)}) collective-permute-start(f32[4,14,70,3]{2,0,3,1:T(4,128)} %copy.43), channel_id=1, source_target_pairs={{0,1},{1,2},{2,3},{4,5},{5,6},{6,7},{8,9},{9,10},{10,11},{12,13},{... | collective-permute-start | bytes 141128 | tf_op jit(solution)/shard_map/ppermute | solution.py:38
  443.8 6.8 %collective-permute-start.23 = (f32[4,14,70,3]{2,0,3,1:T(4,128)}, f32[4,14,70,3]{2,0,3,1:T(4,128)}, u32[]{:S(2)}, u32[]{:S(2)}) collective-permute-start(f32[4,14,70,3]{2,0,3,1:T(4,128)} %copy.44), channel_id=1, source_target_pairs={{1,0},{2,1},{3,2},{5,4},{6,5},{7,6},{9,8},{10,9},{11,10},{13,12},{... | collective-permute-start | bytes 141128 | tf_op jit(solution)/shard_map/ppermute | solution.py:41
  453.8 5.8 %copy-start.10 = (f32[134,64,1,1]{0,1,3,2:T(8,128)S(1)}, f32[134,64,1,1]{0,1,3,2:T(8,128)}, u32[]{:S(2)}) copy-start(f32[134,64,1,1]{0,1,3,2:T(8,128)} %constant.117) | copy-start | bytes 102916
  459.6 7.9 %copy-start.11 = (f32[70,32,1,1]{0,1,3,2:T(8,128)S(1)}, f32[70,32,1,1]{0,1,3,2:T(8,128)}, u32[]{:S(2)}) copy-start(f32[70,32,1,1]{0,1,3,2:T(8,128)} %constant.119) | copy-start | bytes 26884
  459.6 13.0 %copy-start.14 = (f32[14,4,1,1]{0,1,3,2:T(4,128)S(1)}, f32[14,4,1,1]{0,1,3,2:T(4,128)}, u32[]{:S(2)}) copy-start(f32[14,4,1,1]{0,1,3,2:T(4,128)} %constant.120) | copy-start | bytes 676
where the time goes:
time: 485 us; the launch traced here: 475 us
  local copies, waits for them, and re-layouts  252 us (52%)
  matrix products  101 us (21%)
  starting transfers between devices  61.7 us (13%)
  waiting for transfers between devices  39.5 us (8%)
  other arithmetic  18.6 us (4%)
    reshape x1, local copies, waits for them, and re-layouts, body(): volume_block.transpose(3, 0, 4, 1, 5, 2, 6)  92.6 us
    transpose x1, local copies, waits for them, and re-layouts, body(): volume_block.transpose(3, 0, 4, 1, 5, 2, 6)  55.5 us
    dot_general x6, matrix products, place_rows(): jnp.dot(selector, arrived_flat, preferred_element_type=jnp.float32)  41.4 us
    ppermute x12, starting transfers between devices, shifted(): return lax.ppermute(x, axis, pairs)  30.8 us
    reshape x1, local copies, waits for them, and re-layouts, body(): volume_block = brick.reshape(EX, EY, EZ, 4, 8, 8, 8)  20.3 us
    ppermute x6, waiting for transfers between devices, extended(): lax.ppermute(lax.slice_in_dim(block, 0, width, axis=dim), axis, backward)  18.5 us
    ppermute x6, starting transfers between devices, extended(): lax.ppermute(lax.slice_in_dim(block, block.shape[dim] - width, None, axis...  18.4 us
    ppermute x6, waiting for transfers between devices, extended(): lax.ppermute(lax.slice_in_dim(block, block.shape[dim] - width, None, axis...  16.3 us
  transfers between devices with their start and end apart: 24, of which 12 were waited for; matrix products, arithmetic and copies ran while one was open for 18% of the time, Pallas kernels for 0%

commit v1 on v0

v1 whole, which is shorter than its diff:
```python
import jax
import jax.numpy as jnp
import numpy as np
from jax import lax
from jax.experimental import pallas as pl
from jax.experimental.pallas import tpu as pltpu
from jax.sharding import PartitionSpec as P

F32 = jnp.float32
BF16 = jnp.bfloat16
MIB = 1024 * 1024

GLL_NODES = np.array(
    [
        -1.0,
        -0.8717401485096066,
        -0.5917001814331423,
        -0.2092992179024789,
        0.2092992179024789,
        0.5917001814331423,
        0.8717401485096066,
        1.0,
    ]
)

SHIFTS = (("gx", 1), ("gx", -1), ("gy", 1), ("gy", -1), ("gz", 1), ("gz", -1))
STEPS = (16, -16, 4, -4, 1, -1)
PAYLOAD = 336


def gll_basis():
    targets = -1.0 + (2.0 * np.arange(8) + 1.0) / 8.0
    table = np.ones((8, 8))
    for node in range(8):
        for other in range(8):
            if other != node:
                table[:, node] *= (targets - GLL_NODES[other]) / (
                    GLL_NODES[node] - GLL_NODES[other]
                )
    return table


def plain_sinc(points):
    return np.sin(np.pi * points) / (np.pi * points)


def lanczos_taps():
    offsets = np.arange(8) - 3.5
    values = plain_sinc(offsets / 2.0) * plain_sinc(offsets / 4.0)
    return values / np.sum(values)


TAPS = [float(v) for v in lanczos_taps()]


def bf16_of(table):
    return np.asarray(table, np.float32).astype(jnp.bfloat16)


def interp_table():
    basis = gll_basis()
    table = np.einsum("ia,jb,kc->kijabc", basis, basis, basis).reshape(512, 512)
    return bf16_of(table)


def point_order():
    table = np.zeros((8, 8, 8, 8, 8, 8))
    for i in range(8):
        for j in range(8):
            for k in range(8):
                table[k, i, j, i, j, k] = 1.0
    return bf16_of(table.reshape(512, 512))


def depth_tables():
    taps = lanczos_taps()
    low = taps.astype(np.float32).astype(jnp.bfloat16).astype(np.float64)
    first = np.zeros((256, 132))
    for column in range(132):
        for tap in range(8):
            z = 2 * (column - 2) - 3 + tap
            if 0 <= z < 256:
                first[z, column] = low[tap]
    second = np.zeros((132, 70))
    for column in range(70):
        for tap in range(8):
            z = 2 * (column - 3) - 3 + tap + 2
            if 0 <= z < 132:
                second[z, column] = taps[tap]
    out = []
    for place in range(3):
        mid = first.copy()
        if place == 0:
            mid[:, :2] = 0.0
        if place == 2:
            mid[:, 130:] = 0.0
        both = mid @ second
        if place == 0:
            both[:, :3] = 0.0
        if place == 2:
            both[:, 67:] = 0.0
        columns = np.zeros((256, 256))
        columns[:, :128] = mid[:, 2:130]
        columns[:, 128:192] = both[:, 3:67]
        columns[:, 192:194] = mid[:, :2]
        columns[:, 194:196] = mid[:, 130:]
        columns[:, 196:199] = both[:, :3]
        columns[:, 199:202] = both[:, 67:]
        out.append(columns.reshape(32, 8, 256).transpose(1, 0, 2).reshape(256, 256))
    return bf16_of(np.stack(out))


def nt(a, b):
    return lax.dot_general(a, b, (((1,), (1,)), ((), ())), preferred_element_type=F32)


def nn(a, b):
    return lax.dot_general(a, b, (((1,), (0,)), ((), ())), preferred_element_type=F32)


def tn(a, b):
    return lax.dot_general(a, b, (((0,), (0,)), ((), ())), preferred_element_type=F32)


def pack_kernel(coords, home, jac, utri, fields, *rest):
    outs = rest[:6]
    picker, index_v, index_s, sem_index, sem_rows = rest[6:]
    me = coords[3]
    slots = home[...]
    diff = (slots >> 10) - me
    tag = (slots & 1023) + 1
    masks = jnp.concatenate([jnp.where(diff == step, 1.0, 0.0) for step in STEPS], axis=0)
    counts = nn(masks.astype(BF16), utri[...])
    row = lax.broadcasted_iota(jnp.int32, (8, 128), 0)
    slot_id = lax.broadcasted_iota(jnp.int32, (16, 128), 0).astype(F32)
    for d in range(6):
        count = counts[d * 8 : d * 8 + 8]
        total = jnp.broadcast_to(count[:, 127:128], (8, 128))
        rank = count - 1.0
        for r in range(7):
            rank = rank + jnp.where(row > r, jnp.broadcast_to(total[r : r + 1], (8, 128)), 0.0)
        rank = jnp.where(masks[d * 8 : d * 8 + 8] > 0.5, rank, -1.0)
        for r in range(8):
            hit = jnp.broadcast_to(rank[r : r + 1], (16, 128)) == slot_id
            picker[d * 16 : d * 16 + 16, r * 128 : r * 128 + 128] = jnp.where(
                hit, 1.0, 0.0
            ).astype(BF16)
    picker[96:128, :] = jnp.zeros((32, 1024), BF16)
    lane = lax.broadcasted_iota(jnp.int32, (8, 128), 1)
    pieces = []
    for r in range(8):
        own_tag = jnp.broadcast_to(tag[r : r + 1], (8, 128))
        elem = lane + r * 128
        value = jnp.where(
            row == 0,
            elem >> 5,
            jnp.where(row == 1, elem & 31, jnp.where(row == 2, own_tag >> 5, own_tag & 31)),
        )
        pieces.append(value.astype(F32).astype(BF16))
    values = jnp.concatenate(pieces, axis=1)
    found = nt(values, picker[...])
    index = found[0:1] * 32.0 + found[1:2]
    index_v[...] = jnp.broadcast_to(index, (8, 128)).astype(jnp.int32)
    copy_index = pltpu.make_async_copy(index_v, index_s, sem_index)
    copy_index.start()
    copy_index.wait()
    copies = []
    for d in range(6):
        for s in range(16):
            start = pl.multiple_of(index_s[0, d * 16 + s] * 16, 16)
            copy = pltpu.make_async_copy(
                fields.at[pl.ds(start, 16)], outs[d].at[pl.ds(s * 16, 16)], sem_rows.at[d]
            )
            copy.start()
    jac_rows = nn(picker[...], jac[...]).astype(BF16)
    tag_lane = lax.broadcasted_iota(jnp.int32, (16, 128), 1)
    tag_row = lax.broadcasted_iota(jnp.int32, (16, 128), 0)
    tag_hi = jnp.broadcast_to(found[2:3], (16, 128))
    tag_lo = jnp.broadcast_to(found[3:4], (16, 128))
    both = jnp.where(tag_row == 0, tag_hi, jnp.where(tag_row == 1, tag_lo, 0.0))
    for d in range(6):
        for c in range(4):
            outs[d][256 + c * 16 : 272 + c * 16, :] = jac_rows[
                d * 16 : d * 16 + 16, c * 128 : c * 128 + 128
            ]
        outs[d][320:336, :] = jnp.where((tag_lane >> 4) == d, both, 0.0).astype(BF16)
    for d in range(6):
        pltpu.make_async_copy(
            fields.at[pl.ds(0, 256)], outs[d].at[pl.ds(0, 256)], sem_rows.at[d]
        ).wait()


def pack(coords, home, jac, fields_rows):
    utri = np.triu(np.ones((128, 128)))
    vmem = pl.BlockSpec(memory_space=pltpu.VMEM)
    return pl.pallas_call(
        pack_kernel,
        out_shape=[jax.ShapeDtypeStruct((PAYLOAD, 128), BF16)] * 6,
        in_specs=[
            pl.BlockSpec(memory_space=pltpu.SMEM),
            vmem,
            vmem,
            vmem,
            pl.BlockSpec(memory_space=pl.ANY),
        ],
        out_specs=[vmem] * 6,
        scratch_shapes=[
            pltpu.VMEM((128, 1024), BF16),
            pltpu.VMEM((8, 128), jnp.int32),
            pltpu.SMEM((8, 128), jnp.int32),
            pltpu.SemaphoreType.DMA,
            pltpu.SemaphoreType.DMA((6,)),
        ],
        compiler_params=pltpu.CompilerParams(vmem_limit_bytes=16 * MIB),
        name="pack",
    )(coords, home, jac, jnp.asarray(bf16_of(utri)), fields_rows)


def own_kernel(coords, home_s, home_row, fields, jac, table, order, out, rows, jac_t):
    n = pl.program_id(0)

    @pl.when(n == 0)
    def _():
        me = coords[3]

        def clear(e, carry):
            rows[pl.ds(pl.multiple_of(e * 256, 256), 256), :] = jnp.zeros((256, 128), F32)
            return carry

        lax.fori_loop(0, 64, clear, 0)

        def place(e, carry):
            for u in range(8):
                elem = e * 8 + u
                slot = home_s[elem]
                spot = jnp.where((slot >> 10) == me, slot & 1023, 1024)
                rows[pl.ds(pl.multiple_of(spot * 16, 16), 16), :] = fields[
                    pl.ds(pl.multiple_of(elem * 16, 16), 16), :
                ].astype(F32)
            return carry

        lax.fori_loop(0, 128, place, 0)
        slots = home_row[...]
        spot = jnp.where((slots >> 10) == me, slots & 1023, -1)
        ordered = nt(order[...], jac[...]).astype(BF16)
        for c in range(4):
            ids = lax.broadcasted_iota(jnp.int32, (256, 1024), 0) + c * 256
            hit = jnp.where(ids == jnp.broadcast_to(spot, (256, 1024)), 1.0, 0.0).astype(BF16)
            jac_t[:, c * 256 : c * 256 + 256] = nt(ordered, hit)

    base = n * 4096
    for f in range(4):
        pieces = [
            rows[pl.ds(base + c * 4 + f, 256, stride=16), :].astype(BF16) for c in range(4)
        ]
        values = nt(table[...], jnp.concatenate(pieces, axis=1))
        out[f * 512 : f * 512 + 512, :] = (
            values * jac_t[:, pl.ds(pl.multiple_of(n * 256, 256), 256)]
        ).astype(BF16)


def own_elements(coords, home_slot, home_row, fields_rows, jac):
    whole = lambda *shape: pl.BlockSpec(shape, lambda n: (0,) * len(shape))
    smem = pl.BlockSpec(memory_space=pltpu.SMEM)
    return pl.pallas_call(
        own_kernel,
        grid=(4,),
        out_shape=jax.ShapeDtypeStruct((2048, 1024), BF16),
        in_specs=[
            smem,
            smem,
            whole(1, 1024),
            whole(16384, 128),
            whole(1024, 512),
            whole(512, 512),
            whole(512, 512),
        ],
        out_specs=pl.BlockSpec((2048, 256), lambda n: (0, n)),
        scratch_shapes=[
            pltpu.VMEM((1025 * 16, 128), F32),
            pltpu.VMEM((512, 1024), F32),
        ],
        compiler_params=pltpu.CompilerParams(vmem_limit_bytes=48 * MIB),
        cost_estimate=pl.CostEstimate(
            flops=6_000_000_000, bytes_accessed=10_000_000, transcendentals=0
        ),
        name="own_elements",
    )(
        coords,
        home_slot,
        home_row,
        fields_rows,
        jac,
        jnp.asarray(interp_table()),
        jnp.asarray(point_order()),
    )


def halve(values, outputs, shift):
    results = []
    for o in range(outputs):
        total = None
        for tap in range(8):
            at = 2 * o + tap - shift
            if 0 <= at < len(values):
                term = TAPS[tap] * values[at]
                total = term if total is None else total + term
        results.append(total)
    return results


def filter_kernel(
    coords, ut0, ut1, a0, a1, a2, a3, a4, a5, table, order, depth,
    main_a, edge_a, main_c, edge_c, to_low, to_high,
    raw, arrived, rhs, lhs, wide, ya, yb, mb, yc, pbz, pcz,
):
    t = pl.program_id(0)
    arrays = (a0, a1, a2, a3, a4, a5)
    one = lambda flag: jnp.where(flag, 1.0, 0.0)
    x_low = one(coords[0] > 0)
    x_high = one(coords[0] < 7)
    y_low = one(coords[1] > 0)
    y_high = one(coords[1] < 3)

    @pl.when(t == 0)
    def _():
        raw[1536:2048, :] = jnp.zeros((512, 128), F32)
        for d in range(6):
            raw[d * 256 : d * 256 + 256, :] = arrays[d][0:256, :].astype(F32)
        jac = jnp.concatenate(
            [
                jnp.concatenate(
                    [arrays[d][256 + c * 16 : 272 + c * 16, :] for c in range(4)], axis=1
                )
                for d in range(6)
            ]
            + [jnp.zeros((32, 512), BF16)],
            axis=0,
        )
        jac_t = nt(order[...], jac)
        for f in range(4):
            pieces = [
                raw[pl.ds(c * 4 + f, 128, stride=16), :].astype(BF16) for c in range(4)
            ]
            values = nt(table[...], jnp.concatenate(pieces, axis=1))
            arrived[f * 512 : f * 512 + 512, :] = (values * jac_t).astype(BF16)
        rhs[...] = jnp.zeros((1024, 1024), BF16)
        for k in range(8):
            block = depth[k * 32 : k * 32 + 32, :]
            for e in range(4):
                rhs[k * 128 + e * 32 : k * 128 + e * 32 + 32, e * 256 : e * 256 + 256] = block

        def pads(q, carry):
            zero = jnp.zeros((24, 128), F32)
            base = pl.multiple_of(q * 176, 8)
            for ref in (ya, yb):
                ref[pl.ds(base, 24), :] = zero
                ref[pl.ds(base + 152, 24), :] = zero
            return carry

        lax.fori_loop(0, 48, pads, 0)

        def more_pads(q, carry):
            zero = jnp.zeros((16, 128), F32)
            base = pl.multiple_of(q * 112, 8)
            yc[pl.ds(base, 16), :] = zero
            yc[pl.ds(base + 96, 16), :] = zero
            return carry

        lax.fori_loop(0, 40, more_pads, 0)

    tags = jnp.zeros((8, 128), F32)
    for d in range(6):
        tags = tags + arrays[d][320:336, :].astype(F32)[0:8]
    spot = (tags[0:1] * 32.0 + tags[1:2]).astype(jnp.int32) - 1
    for ex, ut in ((0, ut0), (1, ut1)):
        ids = lax.broadcasted_iota(jnp.int32, (128, 128), 0) + (ex * 512 + t * 128)
        hit = jnp.where(ids == jnp.broadcast_to(spot, (128, 128)), 1.0, 0.0).astype(BF16)
        for f in range(4):
            part = nt(arrived[f * 512 : f * 512 + 512, :], hit)
            total = (part + ut[f * 512 : f * 512 + 512, :].astype(F32)).astype(BF16)
            for k in range(8):
                lhs[ex * 256 + f * 64 : ex * 256 + f * 64 + 64, k * 128 : k * 128 + 128] = total[
                    k * 64 : k * 64 + 64
                ]
    for c in range(4):
        wide[:, c * 256 : c * 256 + 256] = nn(lhs[...], rhs[:, c * 256 : c * 256 + 256])

    for f in range(4):
        for column in range(8):
            ref = (ya, yb)[column % 2]
            values = [
                wide[
                    ex * 256 + f * 64 + i * 8 : ex * 256 + f * 64 + i * 8 + 8,
                    column * 128 : column * 128 + 128,
                ]
                for ex in range(2)
                for i in range(8)
            ]
            results = halve(values, 12, 7)
            for o in range(12):
                value = results[o]
                if o < 2:
                    value = value * x_low
                if o >= 10:
                    value = value * x_high
                at = (f * 12 + o) * 176 + 24 + (column // 2) * 8 + t * 32
                ref[pl.ds(pl.multiple_of(at, 8), 8), :] = value

    @pl.when(t == 3)
    def _():
        def along_y(ref, base, count):
            total = None
            for tap in range(8):
                term = TAPS[tap] * ref[pl.ds(base + 5 + tap, count, stride=2), :]
                total = term if total is None else total + term
            low = total[0:8] * y_low
            high = total[count - 8 : count] * y_high
            return low, total[8 : count - 8], high

        def first(q, carry):
            low, middle, high = along_y(ya, q * 176, 80)
            edge_a[pl.ds(pl.multiple_of(q * 16, 16), 8), :] = low
            edge_a[pl.ds(pl.multiple_of(q * 16 + 8, 8), 8), :] = high
            main_a[pl.ds(pl.multiple_of(q * 64, 64), 64), :] = middle
            low, middle, high = along_y(yb, q * 176, 80)
            base = pl.multiple_of(q * 80, 16)
            mb[pl.ds(base, 8), :] = low
            mb[pl.ds(base + 8, 64), :] = middle
            mb[pl.ds(base + 72, 8), :] = high
            pbz[pl.ds(pl.multiple_of(q * 16, 16), 16), :] = jnp.concatenate(
                [low, high], axis=0
            ).astype(BF16)
            pbz[pl.ds(pl.multiple_of(768 + q * 64, 64), 64), :] = middle.astype(BF16)
            return carry

        lax.fori_loop(0, 48, first, 0)

        def along_x(v, carry):
            for f in range(4):
                values = [
                    mb[pl.ds(pl.multiple_of((f * 12 + o) * 80 + v * 8, 8), 8), :]
                    for o in range(12)
                ]
                results = halve(values, 10, 7)
                for o in range(10):
                    value = results[o]
                    if o < 3:
                        value = value * x_low
                    if o >= 7:
                        value = value * x_high
                    at = (f * 10 + o) * 112 + 16 + v * 8
                    yc[pl.ds(pl.multiple_of(at, 8), 8), :] = value
            return carry

        lax.fori_loop(0, 10, along_x, 0)

        def second(q, carry):
            low, middle, high = along_y(yc, q * 112, 48)
            edge_c[pl.ds(pl.multiple_of(q * 16, 16), 8), :] = low
            edge_c[pl.ds(pl.multiple_of(q * 16 + 8, 8), 8), :] = high
            main_c[pl.ds(pl.multiple_of(q * 32, 32), 32), :] = middle
            pcz[pl.ds(pl.multiple_of(q * 16, 16), 16), :] = jnp.concatenate(
                [low, high], axis=0
            ).astype(BF16)
            pcz[pl.ds(pl.multiple_of(640 + q * 32, 32), 32), :] = middle.astype(BF16)
            return carry

        lax.fori_loop(0, 40, second, 0)
        row = lax.broadcasted_iota(jnp.int32, (16, 128), 0)
        lane = lax.broadcasted_iota(jnp.int32, (16, 128), 1)
        pick = lambda count, first_lane: jnp.where(
            (row < count) & (lane == row + first_lane), 1.0, 0.0
        ).astype(BF16)
        for ref, at_mid, at_coarse in ((to_low, 64, 68), (to_high, 66, 71)):
            ref[:, 0:3840] = nt(pick(2, at_mid), pbz[...])[0:8].astype(BF16)
            ref[:, 3840:5760] = nt(pick(3, at_coarse), pcz[...])[0:8].astype(BF16)


def filters(coords, uniform_t, arrived):
    whole = lambda *shape: pl.BlockSpec(shape, lambda t: (0,) * len(shape))
    smem = pl.BlockSpec(memory_space=pltpu.SMEM)
    iz = coords[2]
    place = jnp.where(iz == 0, 0, jnp.where(iz == 3, 2, 1))
    depth = lax.dynamic_index_in_dim(jnp.asarray(depth_tables()), place, 0, keepdims=False)
    return pl.pallas_call(
        filter_kernel,
        grid=(4,),
        out_shape=[
            jax.ShapeDtypeStruct((48 * 64, 128), F32),
            jax.ShapeDtypeStruct((48 * 16, 128), F32),
            jax.ShapeDtypeStruct((40 * 32, 128), F32),
            jax.ShapeDtypeStruct((40 * 16, 128), F32),
            jax.ShapeDtypeStruct((8, 5760), BF16),
            jax.ShapeDtypeStruct((8, 5760), BF16),
        ],
        in_specs=[
            smem,
            pl.BlockSpec((2048, 128), lambda t: (0, t)),
            pl.BlockSpec((2048, 128), lambda t: (0, t + 4)),
        ]
        + [whole(PAYLOAD, 128)] * 6
        + [whole(512, 512), whole(512, 512), whole(256, 256)],
        out_specs=[
            whole(48 * 64, 128),
            whole(48 * 16, 128),
            whole(40 * 32, 128),
            whole(40 * 16, 128),
            whole(8, 5760),
            whole(8, 5760),
        ],
        scratch_shapes=[
            pltpu.VMEM((2048, 128), F32),
            pltpu.VMEM((2048, 128), BF16),
            pltpu.VMEM((1024, 1024), BF16),
            pltpu.VMEM((512, 1024), BF16),
            pltpu.VMEM((512, 1024), F32),
            pltpu.VMEM((48 * 176, 128), F32),
            pltpu.VMEM((48 * 176, 128), F32),
            pltpu.VMEM((48 * 80, 128), F32),
            pltpu.VMEM((40 * 112, 128), F32),
            pltpu.VMEM((3840, 128), BF16),
            pltpu.VMEM((1920, 128), BF16),
        ],
        compiler_params=pltpu.CompilerParams(vmem_limit_bytes=56 * MIB),
        name="filters",
    )(
        coords,
        uniform_t,
        uniform_t,
        *arrived,
        jnp.asarray(interp_table()),
        jnp.asarray(point_order()),
        depth,
    )


def depth_spread(first_lane_high, count):
    table = np.zeros((16, 128))
    for r in range(count):
        table[r, r] = 1.0
        table[8 + r, first_lane_high + r] = 1.0
    return bf16_of(table)


def y_edges_kernel(edge_a, edge_c, from_low, from_high, spread_a, spread_c,
                   to_low, to_high, sa, sc):
    lanes = jnp.concatenate([from_low[:, 0:768], from_high[:, 0:768]], axis=0)
    sa[...] = edge_a[...] + tn(lanes, spread_a[...])
    lanes = jnp.concatenate([from_low[:, 3840:4480], from_high[:, 3840:4480]], axis=0)
    sc[...] = edge_c[...] + tn(lanes, spread_c[...])
    for ref, ra, rc in ((to_low, 6, 5), (to_high, 8, 8)):
        for r in range(2):
            ref[r * 48 : r * 48 + 48, :] = sa[pl.ds(ra + r, 48, stride=16), :].astype(BF16)
        tail = [sc[pl.ds(rc + r, 40, stride=16), :] for r in range(3)] + [jnp.zeros((8, 128), F32)]
        ref[96:224, :] = jnp.concatenate(tail, axis=0).astype(BF16)


def vmem_call(kernel, out_shape, scratch, name, *operands, **options):
    vmem = pl.BlockSpec(memory_space=pltpu.VMEM)
    single = not isinstance(out_shape, list)
    return pl.pallas_call(
        kernel,
        out_shape=out_shape,
        in_specs=[vmem] * len(operands),
        out_specs=vmem if single else [vmem] * len(out_shape),
        scratch_shapes=scratch,
        compiler_params=pltpu.CompilerParams(vmem_limit_bytes=32 * MIB),
        name=name,
        **options,
    )(*operands)


def x_edges_kernel(main_a, main_c, zl, zh, yl, yh, spread_a, spread_c,
                   sa, sc, to_low, to_high, fl, fh):
    lanes = jnp.concatenate([zl[:, 768:3840], zh[:, 768:3840]], axis=0)
    sa[...] = main_a[...] + tn(lanes, spread_a[...])
    lanes = jnp.concatenate([zl[:, 4480:5760], zh[:, 4480:5760]], axis=0)
    sc[...] = main_c[...] + tn(lanes, spread_c[...])
    fl[...] = yl[...].astype(F32)
    fh[...] = yh[...].astype(F32)
    for r in range(2):
        sa[pl.ds(r, 48, stride=64), :] += fl[r * 48 : r * 48 + 48, :]
        sa[pl.ds(62 + r, 48, stride=64), :] += fh[r * 48 : r * 48 + 48, :]
    for r in range(3):
        sc[pl.ds(r, 40, stride=32), :] += fl[96 + r * 40 : 136 + r * 40, :]
        sc[pl.ds(29 + r, 40, stride=32), :] += fh[96 + r * 40 : 136 + r * 40, :]
    for ref, xa, xc in ((to_low, 0, 0), (to_high, 10, 7)):
        for f in range(4):
            ref[f * 128 : f * 128 + 128, :] = sa[
                (f * 12 + xa) * 64 : (f * 12 + xa) * 64 + 128, :
            ].astype(BF16)
            ref[512 + f * 96 : 608 + f * 96, :] = sc[
                (f * 10 + xc) * 32 : (f * 10 + xc) * 32 + 96, :
            ].astype(BF16)


def final_kernel(sa, sc, xl, xh, mid, coarse):
    for f in range(4):
        for x in range(8):
            base = (f * 12 + x + 2) * 64
            value = sa[base : base + 64, :]
            if x < 2:
                value = value + xl[f * 128 + x * 64 : f * 128 + x * 64 + 64, :].astype(F32)
            if x >= 6:
                at = f * 128 + (x - 6) * 64
                value = value + xh[at : at + 64, :].astype(F32)
            mid[f, x] = value
        for x in range(4):
            base = (f * 10 + x + 3) * 32
            value = sc[base : base + 32, :]
            if x < 3:
                at = 512 + f * 96 + x * 32
                value = value + xl[at : at + 32, :].astype(F32)
            if x >= 1:
                at = 512 + f * 96 + (x - 1) * 32
                value = value + xh[at : at + 32, :].astype(F32)
            coarse[f, x] = value[:, 0:64]


def shifted(x, axis, by):
    size = lax.axis_size(axis)
    return lax.ppermute(x, axis, [(i, (i + by) % size) for i in range(size)])


def local_views(fields, home_slot):
    fields_rows = fields.reshape(1024, 4, 4, 128).transpose(0, 2, 1, 3).reshape(16384, 128)
    return fields_rows, home_slot.reshape(8, 128), home_slot.reshape(1, 1024)


def body(fields, jacobian, home_slot):
    ix, iy, iz = (lax.axis_index(axis) for axis in ("gx", "gy", "gz"))
    me = (ix * lax.axis_size("gy") + iy) * lax.axis_size("gz") + iz
    coords = jnp.stack([ix, iy, iz, me]).astype(jnp.int32)
    fields_rows, home_tile, home_row = local_views(fields, home_slot)
    payloads = pack(coords, home_tile, jacobian, fields_rows)
    arrived = [shifted(p, axis, by) for p, (axis, by) in zip(payloads, SHIFTS)]
    uniform_t = own_elements(coords, home_slot, home_row, fields_rows, jacobian)
    main_a, edge_a, main_c, edge_c, z_low, z_high = filters(coords, uniform_t, arrived)
    from_z_low = shifted(z_high, "gz", 1)
    from_z_high = shifted(z_low, "gz", -1)
    spread_a = jnp.asarray(depth_spread(126, 2))
    spread_c = jnp.asarray(depth_spread(61, 3))
    y_low, y_high = vmem_call(
        y_edges_kernel,
        [jax.ShapeDtypeStruct((224, 128), BF16)] * 2,
        [pltpu.VMEM((768, 128), F32), pltpu.VMEM((640, 128), F32)],
        "y_edges",
        edge_a, edge_c, from_z_low, from_z_high, spread_a, spread_c,
    )
    from_y_low = shifted(y_high, "gy", 1)
    from_y_high = shifted(y_low, "gy", -1)
    sum_a, sum_c, x_low, x_high = vmem_call(
        x_edges_kernel,
        [
            jax.ShapeDtypeStruct((48 * 64, 128), F32),
            jax.ShapeDtypeStruct((40 * 32, 128), F32),
            jax.ShapeDtypeStruct((896, 128), BF16),
            jax.ShapeDtypeStruct((896, 128), BF16),
        ],
        [pltpu.VMEM((224, 128), F32), pltpu.VMEM((224, 128), F32)],
        "x_edges",
        main_a, main_c, from_z_low, from_z_high, from_y_low, from_y_high, spread_a, spread_c,
    )
    from_x_low = shifted(x_high, "gx", 1)
    from_x_high = shifted(x_low, "gx", -1)
    mid, coarse = vmem_call(
        final_kernel,
        [
            jax.ShapeDtypeStruct((4, 8, 64, 128), F32),
            jax.ShapeDtypeStruct((4, 4, 32, 64), F32),
        ],
        [],
        "final",
        sum_a, sum_c, from_x_low, from_x_high,
    )
    return mid, coarse


def solution(mesh):
    placed = (P(("gx", "gy", "gz"), None, None), P(("gx", "gy", "gz"), None), P(("gx", "gy", "gz")))
    return jax.shard_map(
        body,
        mesh=mesh,
        in_specs=placed,
        out_specs=(P(None, "gx", "gy", "gz"), P(None, "gx", "gy", "gz")),
        check_vma=False,
    )
```

time: 485 us -> 80.2 us (0.17)
  the two profiles are of different devices: /device:TPU:32 before, /device:TPU:30 now
where the time goes in v1:
time: 80.2 us; the launch traced here: 79.5 us
  Pallas kernels  37 us (46%)
  waiting for transfers between devices  15.3 us (19%)
  starting transfers between devices  14.7 us (18%)
  local copies, waits for them, and re-layouts  11.6 us (14%)
    pallas_call x1, Pallas kernels, filters(): pl.pallas_call(filter_kernel, grid=(4,), out_shape=[jax.ShapeDtypeStruct(...  18.3 us
    ppermute x12, waiting for transfers between devices, shifted(): return lax.ppermute(x, axis, [(i, (i + by) % size) for i in range(size)])  15.3 us
    ppermute x12, starting transfers between devices, shifted(): return lax.ppermute(x, axis, [(i, (i + by) % size) for i in range(size)])  14.7 us
    pallas_call x1, Pallas kernels, own_elements(): pl.pallas_call(own_kernel, grid=(4,), out_shape=jax.ShapeDtypeStruct((204...  13.5 us
    unnamed x42, local copies, waits for them, and re-layouts  9.99 us
    pallas_call x1, Pallas kernels, pack(): pl.pallas_call(pack_kernel, out_shape=[jax.ShapeDtypeStruct((PAYLOAD, 128...  3.03 us
    pallas_call x3, Pallas kernels, vmem_call(): pl.pallas_call(kernel, out_shape=out_shape, in_specs=[vmem] * len(operand...  2.17 us
  transfers between devices with their start and end apart: 12, of which 6 were waited for; matrix products, arithmetic and copies ran while one was open for 2% of the time, Pallas kernels for 17%

profile of v1, /device:TPU:30, one launch (start us, length us, event | category | flops | bytes accessed | tf_op | source)
XLA Modules:
  0.0 79.5 jit_solution(9277854030308009214)
XLA Ops:
  0.6 0.0 copy-start.14
  0.7 0.1 pad_add_fusion.coords
  0.7 0.0 copy-start.12
  0.7 0.0 copy-start
  0.7 2.2 %copy-done = bf16[1024,4,512]{2,1,0:T(4,128)(2,1)S(1)} copy-done((bf16[1024,4,512]{2,1,0:T(4,128)(2,1)S(1)}, bf16[1024,4,512]{2,1,0:T(4,128)(2,1)}, u32[]{:S(2)}) %copy-start) | copy-done | bytes 4194328
  2.9 0.0 copy-start.2
  2.9 1.2 %copy-done.2 = bf16[1024,512]{1,0:T(8,128)(2,1)S(1)} copy-done((bf16[1024,512]{1,0:T(8,128)(2,1)S(1)}, bf16[1024,512]{1,0:T(8,128)(2,1)}, u32[]{:S(2)}) %copy-start.2) | copy-done | bytes 1048600
  4.1 0.0 copy-start.9
  4.2 0.8 copy-done.9
  4.9 0.7 copy-done.13
  5.6 0.0 copy-start.3
  5.6 0.0 copy-start.5
  5.6 3.0 %pack.1 = (bf16[336,128]{1,0:T(8,128)(2,1)S(1)}, bf16[336,128]{1,0:T(8,128)(2,1)S(1)}, bf16[336,128]{1,0:T(8,128)(2,1)S(1)}, bf16[336,128]{1,0:T(8,128)(2,1)S(1)...) custom-call(s32[4]{0:T(128)S(1)} %pad_add_fusion.coords, s32[8,128]{1,0:T(8,128)S(1)} %bitcast.15, ...), custom_call_target="tpu_custom_call" | custom-call | tf_op jit(solution)/shard_map/pack/pallas_call | solution.py:196
  8.6 0.0 collective-permute-start
  8.7 3.5 %collective-permute-start.1 = (bf16[336,128]{1,0:T(8,128)(2,1)S(1)}, bf16[336,128]{1,0:T(8,128)(2,1)S(1)}, u32[]{:S(2)}, u32[]{:S(2)}) collective-permute-start(bf16[336,128]{1,0:T(8,128)(2,1)S(1)} %get-tuple-element.21), channel_id=1, source_target_pairs={{0,112},{16,0},{32,16},{48,32},{64,48},{80,64},{96,80},{112,96},{1... | collective-permute-start | bytes 258056 | tf_op jit(solution)/shard_map/ppermute | solution.py:623
  12.2 0.5 collective-permute-start.2
  12.6 1.5 %collective-permute-start.3 = (bf16[336,128]{1,0:T(8,128)(2,1)S(1)}, bf16[336,128]{1,0:T(8,128)(2,1)S(1)}, u32[]{:S(2)}, u32[]{:S(2)}) collective-permute-start(bf16[336,128]{1,0:T(8,128)(2,1)S(1)} %get-tuple-element.23), channel_id=1, source_target_pairs={{0,12},{4,0},{8,4},{12,8},{1,13},{5,1},{9,5},{13,9},{2,14},{6,2},{... | collective-permute-start | bytes 258056 | tf_op jit(solution)/shard_map/ppermute | solution.py:623
  14.2 0.2 collective-permute-start.4
  14.4 0.0 copy-done.14
  14.4 0.0 copy-done.3
  14.4 0.0 copy-done.5
  14.4 0.0 copy-done.6
  14.4 13.5 %own_elements.1.ut0.ut1 = bf16[2048,1024]{1,0:T(8,128)(2,1)} custom-call(s32[4]{0:T(128)S(1)} %pad_add_fusion.coords, s32[1024]{0:T(1024)S(1)} %copy-done.14, s32[1,1024]{1,0:T(1,128)S(1)} %bitcast.16, bf16[16384,128]{1,0:T(8,128)(2,1)} %bitcast.13, bf16[1024,512]{1,0:T(8,128)(2,1)S(1)} %copy-done.3, bf16[512,512]{1,0:T(8,128)(2,1)S(1)} %copy-done.6, ...), custom_call_target="tpu_custom_call" | custom-call | flops 6000000000 | bytes 10000000 | tf_op jit(solution)/shard_map/own_elements/pallas_call | solution.py:265
  27.9 0.0 copy-done.12
  28.0 0.0 collective-permute-done.a0
  28.0 1.9 %collective-permute-start.5 = (bf16[336,128]{1,0:T(8,128)(2,1)S(1)}, bf16[336,128]{1,0:T(8,128)(2,1)S(1)}, u32[]{:S(2)}, u32[]{:S(2)}) collective-permute-start(bf16[336,128]{1,0:T(8,128)(2,1)S(1)} %get-tuple-element.25), channel_id=1, source_target_pairs={{0,3},{1,0},{2,1},{3,2},{4,7},{5,4},{6,5},{7,6},{8,11},{9,8},{10,9... | collective-permute-start | bytes 258056 | tf_op jit(solution)/shard_map/ppermute | solution.py:623
  29.8 1.6 %dynamic-slice_bitcast_fusion.depth = bf16[256,256]{1,0:T(8,128)(2,1)} fusion(bf16[3,256,256]{2,1,0:T(8,128)(2,1)} %constant.43.clone, s32[]{:T(128)S(6)} %select_n.11), kind=kLoop, calls=%fused_computation | loop fusion | bytes 262148 | tf_op jit(solution)/shard_map/jit(dynamic_index_in_dim)/squeeze | solution.py:485
  31.4 0.0 collective-permute-done.1.a1
  31.4 0.0 collective-permute-done.2.a2
  31.4 0.0 copy-start.17
  31.4 0.0 collective-permute-done.3.a3
  31.4 0.0 copy-start.18
  31.5 0.0 collective-permute-done.4.a4
  31.5 0.0 copy-start.19
  31.5 2.2 %collective-permute-done.5.a5 = bf16[336,128]{1,0:T(8,128)(2,1)S(1)} collective-permute-done((bf16[336,128]{1,0:T(8,128)(2,1)S(1)}, bf16[336,128]{1,0:T(8,128)(2,1)S(1)}, u32[]{:S(2)}, u32[]{:S(2)}) %collective-permute-start.5) | collective-permute-done | bytes 86048 | tf_op jit(solution)/shard_map/ppermute | solution.py:623
  33.7 0.0 copy-done.15
  33.7 0.0 copy-done.16
  33.7 0.0 copy-done.17
  33.7 0.0 copy-done.18
  33.7 0.0 copy-done.19
  33.8 0.0 copy-start.20
  33.8 0.6 copy-done.20
  34.4 18.3 %filters.1 = (f32[3072,128]{1,0:T(8,128)}, f32[768,128]{1,0:T(8,128)}, f32[1280,128]{1,0:T(8,128)}, f32[640,128]{1,0:T(8,128)}, bf16[8,5760]{1,0:T(8,128)(2,1)}, /*index=5*/bf16[8,5760]{1,0:T(8,128)(2,1)}) custom-call(s32[4]{0:T(128)} %copy-done.12, bf16[2048,1024]{1,0:T(8,128)(2,1)} %own_elements.1.ut0.ut1, bf16[2048,1024]{1,0:T(8,128)(2,1)} %own_elements.1.ut0.ut1, ...), custom_call_target="tpu_custom_call" | custom-call | tf_op jit(solution)/shard_map/filters/pallas_call | solution.py:486
  52.7 0.4 collective-permute-start.6
  53.1 1.7 %collective-permute-start.7 = (bf16[8,5760]{1,0:T(8,128)(2,1)}, bf16[8,5760]{1,0:T(8,128)(2,1)S(1)}, u32[]{:S(2)}, u32[]{:S(2)}) collective-permute-start(bf16[8,5760]{1,0:T(8,128)(2,1)} %get-tuple-element.29), channel_id=1, source_target_pairs={{0,3},{1,0},{2,1},{3,2},{4,7},{5,4},{6,5},{7,6},{8,11},{9,8},{10,9... | collective-permute-start | bytes 276488 | tf_op jit(solution)/shard_map/ppermute | solution.py:623
  54.7 2.7 %collective-permute-done.6.from_low.zl = bf16[8,5760]{1,0:T(8,128)(2,1)S(1)} collective-permute-done((bf16[8,5760]{1,0:T(8,128)(2,1)}, bf16[8,5760]{1,0:T(8,128)(2,1)S(1)}, u32[]{:S(2)}, u32[]{:S(2)}) %collective-permute-start.6) | collective-permute-done | bytes 92192 | tf_op jit(solution)/shard_map/ppermute | solution.py:623
  57.5 1.6 %collective-permute-done.7.from_high.zh = bf16[8,5760]{1,0:T(8,128)(2,1)S(1)} collective-permute-done((bf16[8,5760]{1,0:T(8,128)(2,1)}, bf16[8,5760]{1,0:T(8,128)(2,1)S(1)}, u32[]{:S(2)}, u32[]{:S(2)}) %collective-permute-start.7) | collective-permute-done | bytes 92192 | tf_op jit(solution)/shard_map/ppermute | solution.py:623
  59.1 0.0 copy-done.10
  59.1 0.0 copy-done.11
  59.1 1.0 %copy-done.7 = f32[768,128]{1,0:T(8,128)S(1)} copy-done((f32[768,128]{1,0:T(8,128)S(1)}, f32[768,128]{1,0:T(8,128)}, u32[]{:S(2)}) %copy-start.7) | copy-done | bytes 393240
  60.1 1.0 %copy-done.8 = f32[640,128]{1,0:T(8,128)S(1)} copy-done((f32[640,128]{1,0:T(8,128)S(1)}, f32[640,128]{1,0:T(8,128)}, u32[]{:S(2)}) %copy-start.8) | copy-done | bytes 327704
  61.0 0.3 y_edges.1
  61.4 1.8 %collective-permute-start.8 = (bf16[224,128]{1,0:T(8,128)(2,1)S(1)}, bf16[224,128]{1,0:T(8,128)(2,1)S(1)}, u32[]{:S(2)}, u32[]{:S(2)}) collective-permute-start(bf16[224,128]{1,0:T(8,128)(2,1)S(1)} %get-tuple-element.32), channel_id=1, source_target_pairs={{0,4},{4,8},{8,12},{12,0},{1,5},{5,9},{9,13},{13,1},{2,6},{6,10},{... | collective-permute-start | bytes 172040 | tf_op jit(solution)/shard_map/ppermute | solution.py:623
  63.1 0.3 collective-permute-start.9
  63.5 2.2 %collective-permute-done.8.yl = bf16[224,128]{1,0:T(8,128)(2,1)S(1)} collective-permute-done((bf16[224,128]{1,0:T(8,128)(2,1)S(1)}, bf16[224,128]{1,0:T(8,128)(2,1)S(1)}, u32[]{:S(2)}, u32[]{:S(2)}) %collective-permute-start.8) | collective-permute-done | bytes 57376 | tf_op jit(solution)/shard_map/ppermute | solution.py:623
  65.6 2.9 %collective-permute-done.9.yh = bf16[224,128]{1,0:T(8,128)(2,1)S(1)} collective-permute-done((bf16[224,128]{1,0:T(8,128)(2,1)S(1)}, bf16[224,128]{1,0:T(8,128)(2,1)S(1)}, u32[]{:S(2)}, u32[]{:S(2)}) %collective-permute-start.9) | collective-permute-done | bytes 57376 | tf_op jit(solution)/shard_map/ppermute | solution.py:623
  68.5 1.4 %copy-done.1 = f32[3072,128]{1,0:T(8,128)S(1)} copy-done((f32[3072,128]{1,0:T(8,128)S(1)}, f32[3072,128]{1,0:T(8,128)}, u32[]{:S(2)}) %copy-start.1) | copy-done | bytes 1572888
  69.9 1.1 %copy-done.4 = f32[1280,128]{1,0:T(8,128)S(1)} copy-done((f32[1280,128]{1,0:T(8,128)S(1)}, f32[1280,128]{1,0:T(8,128)}, u32[]{:S(2)}) %copy-start.4) | copy-done | bytes 655384
  71.0 0.7 x_edges.1
  71.7 0.0 collective-permute-start.10
  71.7 2.9 %collective-permute-start.11 = (bf16[896,128]{1,0:T(8,128)(2,1)S(1)}, bf16[896,128]{1,0:T(8,128)(2,1)S(1)}, u32[]{:S(2)}, u32[]{:S(2)}) collective-permute-start(bf16[896,128]{1,0:T(8,128)(2,1)S(1)} %get-tuple-element.37), channel_id=1, source_target_pairs={{0,112},{16,0},{32,16},{48,32},{64,48},{80,64},{96,80},{112,96},{1... | collective-permute-start | bytes 688136 | tf_op jit(solution)/shard_map/ppermute | solution.py:623
  74.7 3.7 %collective-permute-done.10.xl = bf16[896,128]{1,0:T(8,128)(2,1)S(1)} collective-permute-done((bf16[896,128]{1,0:T(8,128)(2,1)S(1)}, bf16[896,128]{1,0:T(8,128)(2,1)S(1)}, u32[]{:S(2)}, u32[]{:S(2)}) %collective-permute-start.10) | collective-permute-done | bytes 229408 | tf_op jit(solution)/shard_map/ppermute | solution.py:623
  78.4 0.0 collective-permute-done.11.xh
  78.4 1.1 %final.1 = (f32[4,8,64,128]{3,2,1,0:T(8,128)}, f32[4,4,32,64]{3,2,1,0:T(8,128)}) custom-call(f32[3072,128]{1,0:T(8,128)S(1)} %get-tuple-element.34.sa, f32[1280,128]{1,0:T(8,128)S(1)} %get-tuple-element.35.sc, bf16[896,128]{1,0:T(8,128)(2,1)S(1)} %collective-permute-done.10.xl, bf16[896,128]{1,0:T(8,128)(2,1)S(1)} %collective-permute-done.11.xh), custom_call_target="tpu_custom_call" | custom-call | tf_op jit(solution)/shard_map/final/pallas_call | solution.py:562
  (10 shorter events, 0.0 us)
Async XLA Ops:
  0.6 13.8 %copy-start.14 = (s32[1024]{0:T(1024)S(1)}, s32[1024]{0:T(1024)}, u32[]{:S(2)}) copy-start(s32[1024]{0:T(1024)} %home_s.1) | copy-start | bytes 12292
  0.7 27.2 %copy-start.12 = (s32[4]{0:T(128)}, s32[4]{0:T(128)S(1)}, u32[]{:S(2)}) copy-start(s32[4]{0:T(128)S(1)} %pad_add_fusion.coords) | copy-start | bytes 52
  0.7 2.2 %copy-start = (bf16[1024,4,512]{2,1,0:T(4,128)(2,1)S(1)}, bf16[1024,4,512]{2,1,0:T(4,128)(2,1)}, u32[]{:S(2)}) copy-start(bf16[1024,4,512]{2,1,0:T(4,128)(2,1)} %param.11) | copy-start | bytes 12582916
  2.9 1.2 %copy-start.2 = (bf16[1024,512]{1,0:T(8,128)(2,1)S(1)}, bf16[1024,512]{1,0:T(8,128)(2,1)}, u32[]{:S(2)}) copy-start(bf16[1024,512]{1,0:T(8,128)(2,1)} %jac.3) | copy-start | bytes 3145732
  4.1 0.8 copy-start.9
  4.9 0.7 copy-start.13
  5.6 8.8 %copy-start.3 = (bf16[1024,512]{1,0:T(8,128)(2,1)S(1)}, bf16[1024,512]{1,0:T(8,128)(2,1)}, u32[]{:S(2)}) copy-start(bf16[1024,512]{1,0:T(8,128)(2,1)} %jac.3) | copy-start | bytes 3145732
  5.6 8.8 %copy-start.5 = (bf16[512,512]{1,0:T(8,128)(2,1)S(1)}, bf16[512,512]{1,0:T(8,128)(2,1)}, u32[]{:S(2)}) copy-start(bf16[512,512]{1,0:T(8,128)(2,1)} %constant.42.clone.order) | copy-start | bytes 1572868
  5.6 8.8 %copy-start.6 = (bf16[512,512]{1,0:T(8,128)(2,1)S(1)}, bf16[512,512]{1,0:T(8,128)(2,1)}, u32[]{:S(2)}) copy-start(bf16[512,512]{1,0:T(8,128)(2,1)} %constant.41.clone.table) | copy-start | bytes 1572868
  8.6 19.3 %collective-permute-start = (bf16[336,128]{1,0:T(8,128)(2,1)S(1)}, bf16[336,128]{1,0:T(8,128)(2,1)S(1)}, u32[]{:S(2)}, u32[]{:S(2)}) collective-permute-start(bf16[336,128]{1,0:T(8,128)(2,1)S(1)} %get-tuple-element.20), channel_id=1, source_target_pairs={{0,16},{16,32},{32,48},{48,64},{64,80},{80,96},{96,112},{112,0},{1... | collective-permute-start | bytes 258056 | tf_op jit(solution)/shard_map/ppermute | solution.py:623
  8.7 22.7 %collective-permute-start.1 = (bf16[336,128]{1,0:T(8,128)(2,1)S(1)}, bf16[336,128]{1,0:T(8,128)(2,1)S(1)}, u32[]{:S(2)}, u32[]{:S(2)}) collective-permute-start(bf16[336,128]{1,0:T(8,128)(2,1)S(1)} %get-tuple-element.21), channel_id=1, source_target_pairs={{0,112},{16,0},{32,16},{48,32},{64,48},{80,64},{96,80},{112,96},{1... | collective-permute-start | bytes 258056 | tf_op jit(solution)/shard_map/ppermute | solution.py:623
  12.2 19.3 %collective-permute-start.2 = (bf16[336,128]{1,0:T(8,128)(2,1)S(1)}, bf16[336,128]{1,0:T(8,128)(2,1)S(1)}, u32[]{:S(2)}, u32[]{:S(2)}) collective-permute-start(bf16[336,128]{1,0:T(8,128)(2,1)S(1)} %get-tuple-element.22), channel_id=1, source_target_pairs={{0,4},{4,8},{8,12},{12,0},{1,5},{5,9},{9,13},{13,1},{2,6},{6,10},{... | collective-permute-start | bytes 258056 | tf_op jit(solution)/shard_map/ppermute | solution.py:623
  12.6 18.8 %collective-permute-start.3 = (bf16[336,128]{1,0:T(8,128)(2,1)S(1)}, bf16[336,128]{1,0:T(8,128)(2,1)S(1)}, u32[]{:S(2)}, u32[]{:S(2)}) collective-permute-start(bf16[336,128]{1,0:T(8,128)(2,1)S(1)} %get-tuple-element.23), channel_id=1, source_target_pairs={{0,12},{4,0},{8,4},{12,8},{1,13},{5,1},{9,5},{13,9},{2,14},{6,2},{... | collective-permute-start | bytes 258056 | tf_op jit(solution)/shard_map/ppermute | solution.py:623
  14.2 17.3 %collective-permute-start.4 = (bf16[336,128]{1,0:T(8,128)(2,1)S(1)}, bf16[336,128]{1,0:T(8,128)(2,1)S(1)}, u32[]{:S(2)}, u32[]{:S(2)}) collective-permute-start(bf16[336,128]{1,0:T(8,128)(2,1)S(1)} %get-tuple-element.24), channel_id=1, source_target_pairs={{0,1},{1,2},{2,3},{3,0},{4,5},{5,6},{6,7},{7,4},{8,9},{9,10},{10,1... | collective-permute-start | bytes 258056 | tf_op jit(solution)/shard_map/ppermute | solution.py:623
  28.0 5.8 %copy-start.15 = (bf16[336,128]{1,0:T(8,128)(2,1)}, bf16[336,128]{1,0:T(8,128)(2,1)S(1)}, u32[]{:S(2)}) copy-start(bf16[336,128]{1,0:T(8,128)(2,1)S(1)} %collective-permute-done.a0) | copy-start | bytes 258052
  28.0 5.8 %collective-permute-start.5 = (bf16[336,128]{1,0:T(8,128)(2,1)S(1)}, bf16[336,128]{1,0:T(8,128)(2,1)S(1)}, u32[]{:S(2)}, u32[]{:S(2)}) collective-permute-start(bf16[336,128]{1,0:T(8,128)(2,1)S(1)} %get-tuple-element.25), channel_id=1, source_target_pairs={{0,3},{1,0},{2,1},{3,2},{4,7},{5,4},{6,5},{7,6},{8,11},{9,8},{10,9... | collective-permute-start | bytes 258056 | tf_op jit(solution)/shard_map/ppermute | solution.py:623
  31.4 27.7 %copy-start.10 = (bf16[16,128]{1,0:T(8,128)(2,1)S(1)}, bf16[16,128]{1,0:T(8,128)(2,1)}, u32[]{:S(2)}) copy-start(bf16[16,128]{1,0:T(8,128)(2,1)} %constant.45.clone.spread_c) | copy-start | bytes 12292
  31.4 27.7 %copy-start.11 = (bf16[16,128]{1,0:T(8,128)(2,1)S(1)}, bf16[16,128]{1,0:T(8,128)(2,1)}, u32[]{:S(2)}) copy-start(bf16[16,128]{1,0:T(8,128)(2,1)} %constant.44.clone.spread_a) | copy-start | bytes 12292
  31.4 2.3 %copy-start.16 = (bf16[336,128]{1,0:T(8,128)(2,1)}, bf16[336,128]{1,0:T(8,128)(2,1)S(1)}, u32[]{:S(2)}) copy-start(bf16[336,128]{1,0:T(8,128)(2,1)S(1)} %collective-permute-done.1.a1) | copy-start | bytes 258052
  31.4 2.3 %copy-start.17 = (bf16[336,128]{1,0:T(8,128)(2,1)}, bf16[336,128]{1,0:T(8,128)(2,1)S(1)}, u32[]{:S(2)}) copy-start(bf16[336,128]{1,0:T(8,128)(2,1)S(1)} %collective-permute-done.2.a2) | copy-start | bytes 258052
  31.4 2.3 %copy-start.18 = (bf16[336,128]{1,0:T(8,128)(2,1)}, bf16[336,128]{1,0:T(8,128)(2,1)S(1)}, u32[]{:S(2)}) copy-start(bf16[336,128]{1,0:T(8,128)(2,1)S(1)} %collective-permute-done.3.a3) | copy-start | bytes 258052
  31.5 2.3 %copy-start.19 = (bf16[336,128]{1,0:T(8,128)(2,1)}, bf16[336,128]{1,0:T(8,128)(2,1)S(1)}, u32[]{:S(2)}) copy-start(bf16[336,128]{1,0:T(8,128)(2,1)S(1)} %collective-permute-done.4.a4) | copy-start | bytes 258052
  33.8 0.6 copy-start.20
  52.7 4.8 %collective-permute-start.6 = (bf16[8,5760]{1,0:T(8,128)(2,1)}, bf16[8,5760]{1,0:T(8,128)(2,1)S(1)}, u32[]{:S(2)}, u32[]{:S(2)}) collective-permute-start(bf16[8,5760]{1,0:T(8,128)(2,1)} %get-tuple-element.28), channel_id=1, source_target_pairs={{0,1},{1,2},{2,3},{3,0},{4,5},{5,6},{6,7},{7,4},{8,9},{9,10},{10,1... | collective-permute-start | bytes 276488 | tf_op jit(solution)/shard_map/ppermute | solution.py:623
  53.1 6.0 %collective-permute-start.7 = (bf16[8,5760]{1,0:T(8,128)(2,1)}, bf16[8,5760]{1,0:T(8,128)(2,1)S(1)}, u32[]{:S(2)}, u32[]{:S(2)}) collective-permute-start(bf16[8,5760]{1,0:T(8,128)(2,1)} %get-tuple-element.29), channel_id=1, source_target_pairs={{0,3},{1,0},{2,1},{3,2},{4,7},{5,4},{6,5},{7,6},{8,11},{9,8},{10,9... | collective-permute-start | bytes 276488 | tf_op jit(solution)/shard_map/ppermute | solution.py:623
  59.1 1.0 %copy-start.7 = (f32[768,128]{1,0:T(8,128)S(1)}, f32[768,128]{1,0:T(8,128)}, u32[]{:S(2)}) copy-start(f32[768,128]{1,0:T(8,128)} %get-tuple-element.30.edge_a) | copy-start | bytes 1179652
  60.1 1.0 %copy-start.8 = (f32[640,128]{1,0:T(8,128)S(1)}, f32[640,128]{1,0:T(8,128)}, u32[]{:S(2)}) copy-start(f32[640,128]{1,0:T(8,128)} %get-tuple-element.31.edge_c) | copy-start | bytes 983044
  61.4 4.2 %collective-permute-start.8 = (bf16[224,128]{1,0:T(8,128)(2,1)S(1)}, bf16[224,128]{1,0:T(8,128)(2,1)S(1)}, u32[]{:S(2)}, u32[]{:S(2)}) collective-permute-start(bf16[224,128]{1,0:T(8,128)(2,1)S(1)} %get-tuple-element.32), channel_id=1, source_target_pairs={{0,4},{4,8},{8,12},{12,0},{1,5},{5,9},{9,13},{13,1},{2,6},{6,10},{... | collective-permute-start | bytes 172040 | tf_op jit(solution)/shard_map/ppermute | solution.py:623
  63.1 5.4 %collective-permute-start.9 = (bf16[224,128]{1,0:T(8,128)(2,1)S(1)}, bf16[224,128]{1,0:T(8,128)(2,1)S(1)}, u32[]{:S(2)}, u32[]{:S(2)}) collective-permute-start(bf16[224,128]{1,0:T(8,128)(2,1)S(1)} %get-tuple-element.33), channel_id=1, source_target_pairs={{0,12},{4,0},{8,4},{12,8},{1,13},{5,1},{9,5},{13,9},{2,14},{6,2},{... | collective-permute-start | bytes 172040 | tf_op jit(solution)/shard_map/ppermute | solution.py:623
  68.5 1.4 %copy-start.1 = (f32[3072,128]{1,0:T(8,128)S(1)}, f32[3072,128]{1,0:T(8,128)}, u32[]{:S(2)}) copy-start(f32[3072,128]{1,0:T(8,128)} %get-tuple-element.26.main_a) | copy-start | bytes 4718596
  69.9 1.1 %copy-start.4 = (f32[1280,128]{1,0:T(8,128)S(1)}, f32[1280,128]{1,0:T(8,128)}, u32[]{:S(2)}) copy-start(f32[1280,128]{1,0:T(8,128)} %get-tuple-element.27.main_c) | copy-start | bytes 1966084
  71.7 6.7 %collective-permute-start.10 = (bf16[896,128]{1,0:T(8,128)(2,1)S(1)}, bf16[896,128]{1,0:T(8,128)(2,1)S(1)}, u32[]{:S(2)}, u32[]{:S(2)}) collective-permute-start(bf16[896,128]{1,0:T(8,128)(2,1)S(1)} %get-tuple-element.36), channel_id=1, source_target_pairs={{0,16},{16,32},{32,48},{48,64},{64,80},{80,96},{96,112},{112,0},{1... | collective-permute-start | bytes 688136 | tf_op jit(solution)/shard_map/ppermute | solution.py:623
  71.7 6.6 %collective-permute-start.11 = (bf16[896,128]{1,0:T(8,128)(2,1)S(1)}, bf16[896,128]{1,0:T(8,128)(2,1)S(1)}, u32[]{:S(2)}, u32[]{:S(2)}) collective-permute-start(bf16[896,128]{1,0:T(8,128)(2,1)S(1)} %get-tuple-element.37), channel_id=1, source_target_pairs={{0,112},{16,0},{32,16},{48,32},{64,48},{80,64},{96,80},{112,96},{1... | collective-permute-start | bytes 688136 | tf_op jit(solution)/shard_map/ppermute | solution.py:623

commit v2 on v1

v2 whole, which is shorter than its diff:
```python
import jax
import jax.numpy as jnp
import numpy as np
from jax import lax
from jax.experimental import pallas as pl
from jax.experimental.pallas import tpu as pltpu
from jax.sharding import PartitionSpec as P

F32 = jnp.float32
BF16 = jnp.bfloat16
MIB = 1024 * 1024

GLL_NODES = np.array(
    [
        -1.0,
        -0.8717401485096066,
        -0.5917001814331423,
        -0.2092992179024789,
        0.2092992179024789,
        0.5917001814331423,
        0.8717401485096066,
        1.0,
    ]
)

SHIFTS = (("gx", 1), ("gx", -1), ("gy", 1), ("gy", -1), ("gz", 1), ("gz", -1))
STEPS = (16, -16, 4, -4, 1, -1)
PAYLOAD = 336


def gll_basis():
    targets = -1.0 + (2.0 * np.arange(8) + 1.0) / 8.0
    table = np.ones((8, 8))
    for node in range(8):
        for other in range(8):
            if other != node:
                table[:, node] *= (targets - GLL_NODES[other]) / (
                    GLL_NODES[node] - GLL_NODES[other]
                )
    return table


def plain_sinc(points):
    return np.sin(np.pi * points) / (np.pi * points)


def lanczos_taps():
    offsets = np.arange(8) - 3.5
    values = plain_sinc(offsets / 2.0) * plain_sinc(offsets / 4.0)
    return values / np.sum(values)


TAPS = [float(v) for v in lanczos_taps()]


def bf16_of(table):
    return np.asarray(table, np.float32).astype(jnp.bfloat16)


def interp_table():
    basis = gll_basis()
    table = np.einsum("ia,jb,kc->kijabc", basis, basis, basis).reshape(512, 512)
    return bf16_of(table)


def point_order():
    table = np.zeros((8, 8, 8, 8, 8, 8))
    for i in range(8):
        for j in range(8):
            for k in range(8):
                table[k, i, j, i, j, k] = 1.0
    return bf16_of(table.reshape(512, 512))


def depth_tables():
    taps = lanczos_taps()
    low = taps.astype(np.float32).astype(jnp.bfloat16).astype(np.float64)
    first = np.zeros((256, 132))
    for column in range(132):
        for tap in range(8):
            z = 2 * (column - 2) - 3 + tap
            if 0 <= z < 256:
                first[z, column] = low[tap]
    second = np.zeros((132, 70))
    for column in range(70):
        for tap in range(8):
            z = 2 * (column - 3) - 3 + tap + 2
            if 0 <= z < 132:
                second[z, column] = taps[tap]
    out = []
    for place in range(3):
        mid = first.copy()
        if place == 0:
            mid[:, :2] = 0.0
        if place == 2:
            mid[:, 130:] = 0.0
        both = mid @ second
        if place == 0:
            both[:, :3] = 0.0
        if place == 2:
            both[:, 67:] = 0.0
        columns = np.zeros((256, 256))
        columns[:, :128] = mid[:, 2:130]
        columns[:, 128:192] = both[:, 3:67]
        columns[:, 192:194] = mid[:, :2]
        columns[:, 194:196] = mid[:, 130:]
        columns[:, 196:199] = both[:, :3]
        columns[:, 199:202] = both[:, 67:]
        out.append(columns.reshape(32, 8, 256).transpose(1, 0, 2).reshape(256, 256))
    return bf16_of(np.stack(out))


def nt(a, b):
    return lax.dot_general(a, b, (((1,), (1,)), ((), ())), preferred_element_type=F32)


def nn(a, b):
    return lax.dot_general(a, b, (((1,), (0,)), ((), ())), preferred_element_type=F32)


def tn(a, b):
    return lax.dot_general(a, b, (((0,), (0,)), ((), ())), preferred_element_type=F32)


def pack_kernel(coords, home, jac_hbm, fields, *rest):
    outs = rest[:6]
    spots, picker, jac, index_v, index_s, sem_jac, sem_index, sem_rows = rest[6:]
    copy_jac = pltpu.make_async_copy(jac_hbm, jac, sem_jac)
    copy_jac.start()
    me = coords[3]
    slots = home[...]
    diff = (slots >> 10) - me
    tag = (slots & 1023) + 1
    masks = jnp.concatenate([jnp.where(diff == step, 1.0, 0.0) for step in STEPS], axis=0)
    upper = jnp.where(
        lax.broadcasted_iota(jnp.int32, (128, 128), 0)
        <= lax.broadcasted_iota(jnp.int32, (128, 128), 1),
        1.0,
        0.0,
    ).astype(BF16)
    counts = nn(masks.astype(BF16), upper)
    spots[...] = jnp.where(diff == 0, tag - 1, 1024)
    row = lax.broadcasted_iota(jnp.int32, (8, 128), 0)
    slot_id = lax.broadcasted_iota(jnp.int32, (16, 128), 0).astype(F32)
    for d in range(6):
        count = counts[d * 8 : d * 8 + 8]
        total = jnp.broadcast_to(count[:, 127:128], (8, 128))
        rank = count - 1.0
        for r in range(7):
            rank = rank + jnp.where(row > r, jnp.broadcast_to(total[r : r + 1], (8, 128)), 0.0)
        rank = jnp.where(masks[d * 8 : d * 8 + 8] > 0.5, rank, -1.0)
        for r in range(8):
            hit = jnp.broadcast_to(rank[r : r + 1], (16, 128)) == slot_id
            picker[d * 16 : d * 16 + 16, r * 128 : r * 128 + 128] = jnp.where(
                hit, 1.0, 0.0
            ).astype(BF16)
    picker[96:128, :] = jnp.zeros((32, 1024), BF16)
    lane = lax.broadcasted_iota(jnp.int32, (8, 128), 1)
    pieces = []
    for r in range(8):
        own_tag = jnp.broadcast_to(tag[r : r + 1], (8, 128))
        elem = lane + r * 128
        value = jnp.where(
            row == 0,
            elem >> 5,
            jnp.where(row == 1, elem & 31, jnp.where(row == 2, own_tag >> 5, own_tag & 31)),
        )
        pieces.append(value.astype(F32).astype(BF16))
    values = jnp.concatenate(pieces, axis=1)
    found = nt(values, picker[...])
    index = found[0:1] * 32.0 + found[1:2]
    index_v[...] = jnp.broadcast_to(index, (8, 128)).astype(jnp.int32)
    copy_index = pltpu.make_async_copy(index_v, index_s, sem_index)
    copy_index.start()
    copy_index.wait()
    copies = []
    for d in range(6):
        for s in range(16):
            start = pl.multiple_of(index_s[0, d * 16 + s] * 16, 16)
            copy = pltpu.make_async_copy(
                fields.at[pl.ds(start, 16)], outs[d].at[pl.ds(s * 16, 16)], sem_rows.at[d]
            )
            copy.start()
    copy_jac.wait()
    jac_rows = nn(picker[...], jac[...]).astype(BF16)
    tag_lane = lax.broadcasted_iota(jnp.int32, (16, 128), 1)
    tag_row = lax.broadcasted_iota(jnp.int32, (16, 128), 0)
    tag_hi = jnp.broadcast_to(found[2:3], (16, 128))
    tag_lo = jnp.broadcast_to(found[3:4], (16, 128))
    both = jnp.where(tag_row == 0, tag_hi, jnp.where(tag_row == 1, tag_lo, 0.0))
    for d in range(6):
        for c in range(4):
            outs[d][256 + c * 16 : 272 + c * 16, :] = jac_rows[
                d * 16 : d * 16 + 16, c * 128 : c * 128 + 128
            ]
        outs[d][320:336, :] = jnp.where((tag_lane >> 4) == d, both, 0.0).astype(BF16)
    for d in range(6):
        pltpu.make_async_copy(
            fields.at[pl.ds(0, 256)], outs[d].at[pl.ds(0, 256)], sem_rows.at[d]
        ).wait()


def pack(coords, home, jac, fields_rows):
    vmem = pl.BlockSpec(memory_space=pltpu.VMEM)
    hbm = pl.BlockSpec(memory_space=pltpu.HBM)
    return pl.pallas_call(
        pack_kernel,
        out_shape=[jax.ShapeDtypeStruct((PAYLOAD, 128), BF16)] * 6
        + [jax.ShapeDtypeStruct((8, 128), jnp.int32)],
        in_specs=[pl.BlockSpec(memory_space=pltpu.SMEM), vmem, hbm, hbm],
        out_specs=[vmem] * 7,
        scratch_shapes=[
            pltpu.VMEM((128, 1024), BF16),
            pltpu.VMEM((1024, 512), BF16),
            pltpu.VMEM((8, 128), jnp.int32),
            pltpu.SMEM((8, 128), jnp.int32),
            pltpu.SemaphoreType.DMA,
            pltpu.SemaphoreType.DMA,
            pltpu.SemaphoreType.DMA((6,)),
        ],
        compiler_params=pltpu.CompilerParams(vmem_limit_bytes=60 * MIB),
        name="pack",
    )(coords, home, jac, fields_rows)


def own_kernel(spot_s, spot_v, fields, jac, table, order, out, rows, jac_t):
    def clear(e, carry):
        rows[pl.ds(pl.multiple_of(e * 512, 512), 512), :] = jnp.zeros((512, 128), F32)
        return carry

    lax.fori_loop(0, 32, clear, 0)

    def place(e, carry):
        for u in range(16):
            spot = spot_s[e >> 3, (e & 7) * 16 + u]
            rows[pl.ds(pl.multiple_of(spot * 16, 16), 16), :] = fields[
                pl.ds(pl.multiple_of(e * 256 + u * 16, 16), 16), :
            ].astype(F32)
        return carry

    lax.fori_loop(0, 64, place, 0)
    ordered = nt(order[...], jac[...]).astype(BF16)
    for c in range(4):
        ids = lax.broadcasted_iota(jnp.int32, (256, 128), 0) + c * 256
        hit = jnp.concatenate(
            [
                jnp.where(
                    ids == jnp.broadcast_to(spot_v[r : r + 1, :], (256, 128)), 1.0, 0.0
                ).astype(BF16)
                for r in range(8)
            ],
            axis=1,
        )
        jac_t[:, c * 256 : c * 256 + 256] = nt(ordered, hit)

    for n in range(4):
        for f in range(4):
            pieces = [
                rows[pl.ds(n * 4096 + c * 4 + f, 256, stride=16), :].astype(BF16)
                for c in range(4)
            ]
            values = nt(table[...], jnp.concatenate(pieces, axis=1))
            out[f * 512 : f * 512 + 512, n * 256 : n * 256 + 256] = (
                values * jac_t[:, n * 256 : n * 256 + 256]
            ).astype(BF16)


def own_elements(spots, fields_rows, jac):
    vmem = pl.BlockSpec(memory_space=pltpu.VMEM)
    return pl.pallas_call(
        own_kernel,
        out_shape=jax.ShapeDtypeStruct((2048, 1024), BF16),
        in_specs=[pl.BlockSpec(memory_space=pltpu.SMEM)] + [vmem] * 5,
        out_specs=vmem,
        scratch_shapes=[
            pltpu.VMEM((1025 * 16, 128), F32),
            pltpu.VMEM((512, 1024), F32),
        ],
        compiler_params=pltpu.CompilerParams(vmem_limit_bytes=28 * MIB),
        cost_estimate=pl.CostEstimate(
            flops=6_000_000_000, bytes_accessed=10_000_000, transcendentals=0
        ),
        name="own_elements",
    )(
        spots,
        spots,
        fields_rows,
        jac,
        jnp.asarray(interp_table()),
        jnp.asarray(point_order()),
    )


def halve(values, outputs, shift):
    results = []
    for o in range(outputs):
        total = None
        for tap in range(8):
            at = 2 * o + tap - shift
            if 0 <= at < len(values):
                term = TAPS[tap] * values[at]
                total = term if total is None else total + term
        results.append(total)
    return results


def filter_kernel(
    coords, uniform, a0, a1, a2, a3, a4, a5, table, order, depths,
    main_a, edge_a, main_c, edge_c, to_low, to_high,
    raw, arrived, depth, wide, ya, yb, mb, yc, pbz, pcz, sem,
):
    arrays = (a0, a1, a2, a3, a4, a5)
    one = lambda flag: jnp.where(flag, 1.0, 0.0)
    x_low = one(coords[0] > 0)
    x_high = one(coords[0] < 7)
    y_low = one(coords[1] > 0)
    y_high = one(coords[1] < 3)

    spot_z = coords[2]
    place = jnp.where(spot_z == 0, 0, jnp.where(spot_z == 3, 2, 1))
    copy = pltpu.make_async_copy(depths.at[place], depth, sem)
    copy.start()
    raw[1536:2048, :] = jnp.zeros((512, 128), F32)
    for d in range(6):
        raw[d * 256 : d * 256 + 256, :] = arrays[d][0:256, :].astype(F32)
    jac = jnp.concatenate(
        [
            jnp.concatenate(
                [arrays[d][256 + c * 16 : 272 + c * 16, :] for c in range(4)], axis=1
            )
            for d in range(6)
        ]
        + [jnp.zeros((32, 512), BF16)],
        axis=0,
    )
    jac_t = nt(order[...], jac)
    for f in range(4):
        pieces = [
            raw[pl.ds(c * 4 + f, 128, stride=16), :].astype(BF16) for c in range(4)
        ]
        values = nt(table[...], jnp.concatenate(pieces, axis=1))
        arrived[f * 512 : f * 512 + 512, :] = (values * jac_t).astype(BF16)
    def pads(q, carry):
        zero = jnp.zeros((24, 128), F32)
        base = pl.multiple_of(q * 176, 8)
        for ref in (ya, yb):
            ref[pl.ds(base, 24), :] = zero
            ref[pl.ds(base + 152, 24), :] = zero
        return carry

    lax.fori_loop(0, 48, pads, 0)

    def more_pads(q, carry):
        zero = jnp.zeros((16, 128), F32)
        base = pl.multiple_of(q * 112, 8)
        yc[pl.ds(base, 16), :] = zero
        yc[pl.ds(base + 96, 16), :] = zero
        return carry

    lax.fori_loop(0, 40, more_pads, 0)
    copy.wait()

    tags = jnp.zeros((8, 128), F32)
    for d in range(6):
        tags = tags + arrays[d][320:336, :].astype(F32)[0:8]
    spot = (tags[0:1] * 32.0 + tags[1:2]).astype(jnp.int32) - 1
    def quarter(t, carry):
        row = lax.broadcasted_iota(jnp.int32, (256, 128), 0)
        ids = jnp.where(row < 128, row, row + 384) + t * 128
        hit = jnp.where(ids == jnp.broadcast_to(spot, (256, 128)), 1.0, 0.0).astype(BF16)
        lane = lax.broadcasted_iota(jnp.int32, (64, 128), 1)
        odd = (lane & 32) != 0
        upper = (lane & 64) != 0
        for f in range(4):
            both = nt(arrived[f * 512 : f * 512 + 512, :], hit)
            pieces = [[], [], [], []]
            for ex in range(2):
                part = both[:, ex * 128 : ex * 128 + 128]
                own = uniform[
                    f * 512 : f * 512 + 512,
                    pl.ds(pl.multiple_of(ex * 512 + t * 128, 128), 128),
                ]
                total = part + own.astype(F32)
                regrouped = []
                for h in range(2):
                    v = [total[(h * 4 + k) * 64 : (h * 4 + k) * 64 + 64] for k in range(4)]
                    for a, b in ((0, 1), (2, 3)):
                        v[a], v[b] = (
                            jnp.where(odd, pltpu.roll(v[b], 32, 1), v[a]),
                            jnp.where(odd, v[b], pltpu.roll(v[a], 96, 1)),
                        )
                    for a, b in ((0, 2), (1, 3)):
                        v[a], v[b] = (
                            jnp.where(upper, pltpu.roll(v[b], 64, 1), v[a]),
                            jnp.where(upper, v[b], pltpu.roll(v[a], 64, 1)),
                        )
                    regrouped.append(v)
                for e in range(4):
                    pieces[e].append(
                        jnp.concatenate([regrouped[0][e], regrouped[1][e]], axis=1).astype(BF16)
                    )
            operand = jnp.concatenate([p for e in range(4) for p in pieces[e]], axis=0)
            wide[f * 512 : f * 512 + 512, :] = nn(operand, depth[...])

        for f in range(4):
            for column in range(8):
                ref = (ya, yb)[column % 2]
                values = [
                    wide[
                        f * 512 + (column // 2) * 128 + ex * 64 + i * 8 : f * 512
                        + (column // 2) * 128 + ex * 64 + i * 8 + 8,
                        (column % 2) * 128 : (column % 2) * 128 + 128,
                    ]
                    for ex in range(2)
                    for i in range(8)
                ]
                results = halve(values, 12, 7)
                for o in range(12):
                    value = results[o]
                    if o < 2:
                        value = value * x_low
                    if o >= 10:
                        value = value * x_high
                    at = (f * 12 + o) * 176 + 24 + (column // 2) * 8 + t * 32
                    ref[pl.ds(pl.multiple_of(at, 8), 8), :] = value
        return carry

    lax.fori_loop(0, 4, quarter, 0)

    def along_y(ref, base, count):
        total = None
        for tap in range(8):
            term = TAPS[tap] * ref[pl.ds(base + 5 + tap, count, stride=2), :]
            total = term if total is None else total + term
        low = total[0:8] * y_low
        high = total[count - 8 : count] * y_high
        return low, total[8 : count - 8], high

    def first(q, carry):
        low, middle, high = along_y(ya, q * 176, 80)
        edge_a[pl.ds(pl.multiple_of(q * 16, 16), 8), :] = low
        edge_a[pl.ds(pl.multiple_of(q * 16 + 8, 8), 8), :] = high
        main_a[pl.ds(pl.multiple_of(q * 64, 64), 64), :] = middle
        low, middle, high = along_y(yb, q * 176, 80)
        base = pl.multiple_of(q * 80, 16)
        mb[pl.ds(base, 8), :] = low
        mb[pl.ds(base + 8, 64), :] = middle
        mb[pl.ds(base + 72, 8), :] = high
        pbz[pl.ds(pl.multiple_of(q * 16, 16), 16), :] = jnp.concatenate(
            [low, high], axis=0
        ).astype(BF16)
        pbz[pl.ds(pl.multiple_of(768 + q * 64, 64), 64), :] = middle.astype(BF16)
        return carry

    lax.fori_loop(0, 48, first, 0)

    def along_x(v, carry):
        for f in range(4):
            values = [
                mb[pl.ds(pl.multiple_of((f * 12 + o) * 80 + v * 8, 8), 8), :]
                for o in range(12)
            ]
            results = halve(values, 10, 7)
            for o in range(10):
                value = results[o]
                if o < 3:
                    value = value * x_low
                if o >= 7:
                    value = value * x_high
                at = (f * 10 + o) * 112 + 16 + v * 8
                yc[pl.ds(pl.multiple_of(at, 8), 8), :] = value
        return carry

    lax.fori_loop(0, 10, along_x, 0)

    def second(q, carry):
        low, middle, high = along_y(yc, q * 112, 48)
        edge_c[pl.ds(pl.multiple_of(q * 16, 16), 8), :] = low
        edge_c[pl.ds(pl.multiple_of(q * 16 + 8, 8), 8), :] = high
        main_c[pl.ds(pl.multiple_of(q * 32, 32), 32), :] = middle
        pcz[pl.ds(pl.multiple_of(q * 16, 16), 16), :] = jnp.concatenate(
            [low, high], axis=0
        ).astype(BF16)
        pcz[pl.ds(pl.multiple_of(640 + q * 32, 32), 32), :] = middle.astype(BF16)
        return carry

    lax.fori_loop(0, 40, second, 0)
    row = lax.broadcasted_iota(jnp.int32, (16, 128), 0)
    lane = lax.broadcasted_iota(jnp.int32, (16, 128), 1)
    pick = lambda count, first_lane: jnp.where(
        (row < count) & (lane == row + first_lane), 1.0, 0.0
    ).astype(BF16)
    for ref, at_mid, at_coarse in ((to_low, 64, 68), (to_high, 66, 71)):
        ref[:, 0:3840] = nt(pick(2, at_mid), pbz[...])[0:8].astype(BF16)
        ref[:, 3840:5760] = nt(pick(3, at_coarse), pcz[...])[0:8].astype(BF16)


def filters(coords, uniform_t, arrived):
    vmem = pl.BlockSpec(memory_space=pltpu.VMEM)
    return pl.pallas_call(
        filter_kernel,
        out_shape=[
            jax.ShapeDtypeStruct((48 * 64, 128), F32),
            jax.ShapeDtypeStruct((48 * 16, 128), F32),
            jax.ShapeDtypeStruct((40 * 32, 128), F32),
            jax.ShapeDtypeStruct((40 * 16, 128), F32),
            jax.ShapeDtypeStruct((8, 5760), BF16),
            jax.ShapeDtypeStruct((8, 5760), BF16),
        ],
        in_specs=[pl.BlockSpec(memory_space=pltpu.SMEM)]
        + [vmem] * 9
        + [pl.BlockSpec(memory_space=pltpu.HBM)],
        out_specs=[vmem] * 6,
        scratch_shapes=[
            pltpu.VMEM((2048, 128), F32),
            pltpu.VMEM((2048, 128), BF16),
            pltpu.VMEM((256, 256), BF16),
            pltpu.VMEM((2048, 256), F32),
            pltpu.VMEM((48 * 176, 128), F32),
            pltpu.VMEM((48 * 176, 128), F32),
            pltpu.VMEM((48 * 80, 128), F32),
            pltpu.VMEM((40 * 112, 128), F32),
            pltpu.VMEM((3840, 128), BF16),
            pltpu.VMEM((1920, 128), BF16),
            pltpu.SemaphoreType.DMA,
        ],
        compiler_params=pltpu.CompilerParams(vmem_limit_bytes=32 * MIB),
        name="filters",
    )(
        coords,
        uniform_t,
        *arrived,
        jnp.asarray(interp_table()),
        jnp.asarray(point_order()),
        jnp.asarray(depth_tables()),
    )


def depth_spread(first_lane_high, count):
    table = np.zeros((16, 128))
    for r in range(count):
        table[r, r] = 1.0
        table[8 + r, first_lane_high + r] = 1.0
    return bf16_of(table)


def y_edges_kernel(edge_a, edge_c, from_low, from_high, spread_a, spread_c,
                   to_low, to_high, sa, sc):
    lanes = jnp.concatenate([from_low[:, 0:768], from_high[:, 0:768]], axis=0)
    sa[...] = edge_a[...] + tn(lanes, spread_a[...])
    lanes = jnp.concatenate([from_low[:, 3840:4480], from_high[:, 3840:4480]], axis=0)
    sc[...] = edge_c[...] + tn(lanes, spread_c[...])
    for ref, ra, rc in ((to_low, 6, 5), (to_high, 8, 8)):
        for r in range(2):
            ref[r * 48 : r * 48 + 48, :] = sa[pl.ds(ra + r, 48, stride=16), :].astype(BF16)
        tail = [sc[pl.ds(rc + r, 40, stride=16), :] for r in range(3)] + [jnp.zeros((8, 128), F32)]
        ref[96:224, :] = jnp.concatenate(tail, axis=0).astype(BF16)


def vmem_call(kernel, out_shape, scratch, name, *operands, **options):
    vmem = pl.BlockSpec(memory_space=pltpu.VMEM)
    single = not isinstance(out_shape, list)
    return pl.pallas_call(
        kernel,
        out_shape=out_shape,
        in_specs=[vmem] * len(operands),
        out_specs=vmem if single else [vmem] * len(out_shape),
        scratch_shapes=scratch,
        compiler_params=pltpu.CompilerParams(vmem_limit_bytes=12 * MIB),
        name=name,
        **options,
    )(*operands)


def x_edges_kernel(main_a, main_c, zl, zh, yl, yh, spread_a, spread_c,
                   sa, sc, to_low, to_high, fl, fh):
    lanes = jnp.concatenate([zl[:, 768:3840], zh[:, 768:3840]], axis=0)
    sa[...] = main_a[...] + tn(lanes, spread_a[...])
    lanes = jnp.concatenate([zl[:, 4480:5760], zh[:, 4480:5760]], axis=0)
    sc[...] = main_c[...] + tn(lanes, spread_c[...])
    fl[...] = yl[...].astype(F32)
    fh[...] = yh[...].astype(F32)
    for r in range(2):
        sa[pl.ds(r, 48, stride=64), :] += fl[r * 48 : r * 48 + 48, :]
        sa[pl.ds(62 + r, 48, stride=64), :] += fh[r * 48 : r * 48 + 48, :]
    for r in range(3):
        sc[pl.ds(r, 40, stride=32), :] += fl[96 + r * 40 : 136 + r * 40, :]
        sc[pl.ds(29 + r, 40, stride=32), :] += fh[96 + r * 40 : 136 + r * 40, :]
    for ref, xa, xc in ((to_low, 0, 0), (to_high, 10, 7)):
        for f in range(4):
            ref[f * 128 : f * 128 + 128, :] = sa[
                (f * 12 + xa) * 64 : (f * 12 + xa) * 64 + 128, :
            ].astype(BF16)
            ref[512 + f * 96 : 608 + f * 96, :] = sc[
                (f * 10 + xc) * 32 : (f * 10 + xc) * 32 + 96, :
            ].astype(BF16)


def final_kernel(sa, sc, xl, xh, mid, coarse):
    for f in range(4):
        for x in range(8):
            base = (f * 12 + x + 2) * 64
            value = sa[base : base + 64, :]
            if x < 2:
                value = value + xl[f * 128 + x * 64 : f * 128 + x * 64 + 64, :].astype(F32)
            if x >= 6:
                at = f * 128 + (x - 6) * 64
                value = value + xh[at : at + 64, :].astype(F32)
            mid[f, x] = value
        for x in range(4):
            base = (f * 10 + x + 3) * 32
            value = sc[base : base + 32, :]
            if x < 3:
                at = 512 + f * 96 + x * 32
                value = value + xl[at : at + 32, :].astype(F32)
            if x >= 1:
                at = 512 + f * 96 + (x - 1) * 32
                value = value + xh[at : at + 32, :].astype(F32)
            coarse[f, x] = value[:, 0:64]


def shifted(x, axis, by):
    size = lax.axis_size(axis)
    return lax.ppermute(x, axis, [(i, (i + by) % size) for i in range(size)])


def local_views(fields, home_slot):
    fields_rows = fields.reshape(1024, 4, 4, 128).transpose(0, 2, 1, 3).reshape(16384, 128)
    return fields_rows, home_slot.reshape(8, 128)


def body(fields, jacobian, home_slot):
    ix, iy, iz = (lax.axis_index(axis) for axis in ("gx", "gy", "gz"))
    me = (ix * lax.axis_size("gy") + iy) * lax.axis_size("gz") + iz
    coords = jnp.stack([ix, iy, iz, me]).astype(jnp.int32)
    fields_rows, home_tile = local_views(fields, home_slot)
    *payloads, spots = pack(coords, home_tile, jacobian, fields_rows)
    arrived = [shifted(p, axis, by) for p, (axis, by) in zip(payloads, SHIFTS)]
    uniform_t = own_elements(spots, fields_rows, jacobian)
    main_a, edge_a, main_c, edge_c, z_low, z_high = filters(coords, uniform_t, arrived)
    from_z_low = shifted(z_high, "gz", 1)
    from_z_high = shifted(z_low, "gz", -1)
    spread_a = jnp.asarray(depth_spread(126, 2))
    spread_c = jnp.asarray(depth_spread(61, 3))
    y_low, y_high = vmem_call(
        y_edges_kernel,
        [jax.ShapeDtypeStruct((224, 128), BF16)] * 2,
        [pltpu.VMEM((768, 128), F32), pltpu.VMEM((640, 128), F32)],
        "y_edges",
        edge_a, edge_c, from_z_low, from_z_high, spread_a, spread_c,
    )
    from_y_low = shifted(y_high, "gy", 1)
    from_y_high = shifted(y_low, "gy", -1)
    sum_a, sum_c, x_low, x_high = vmem_call(
        x_edges_kernel,
        [
            jax.ShapeDtypeStruct((48 * 64, 128), F32),
            jax.ShapeDtypeStruct((40 * 32, 128), F32),
            jax.ShapeDtypeStruct((896, 128), BF16),
            jax.ShapeDtypeStruct((896, 128), BF16),
        ],
        [pltpu.VMEM((224, 128), F32), pltpu.VMEM((224, 128), F32)],
        "x_edges",
        main_a, main_c, from_z_low, from_z_high, from_y_low, from_y_high, spread_a, spread_c,
    )
    from_x_low = shifted(x_high, "gx", 1)
    from_x_high = shifted(x_low, "gx", -1)
    mid, coarse = vmem_call(
        final_kernel,
        [
            jax.ShapeDtypeStruct((4, 8, 64, 128), F32),
            jax.ShapeDtypeStruct((4, 4, 32, 64), F32),
        ],
        [],
        "final",
        sum_a, sum_c, from_x_low, from_x_high,
    )
    return mid, coarse


def solution(mesh):
    placed = (P(("gx", "gy", "gz"), None, None), P(("gx", "gy", "gz"), None), P(("gx", "gy", "gz")))
    return jax.shard_map(
        body,
        mesh=mesh,
        in_specs=placed,
        out_specs=(P(None, "gx", "gy", "gz"), P(None, "gx", "gy", "gz")),
        check_vma=False,
    )
```

time: 80.2 us -> 65.3 us (0.81)
  local copies, waits for them, and re-layouts: 11.6 us -> 2.9 us
  Pallas kernels: 37 us -> 32.4 us
  waiting for transfers between devices: 15.3 us -> 13.5 us
    pallas_call x2, Pallas kernels: 31.8 us -> 24.5 us  [the longest x1 14.1 us: filters(): pl.pallas_call(filter_kernel, out_shape=[jax.ShapeDtypeStruct((48 * 64, 1...]
    unnamed x42 -> x18, local copies, waits for them, and re-layouts: 9.99 us -> 2.9 us
    pallas_call x1, Pallas kernels: 3.03 us -> 5.66 us  [pack(): pl.pallas_call(pack_kernel, out_shape=[jax.ShapeDtypeStruct((PAYLOAD, 128...]
    ppermute x12, waiting for transfers between devices: 15.3 us -> 13.5 us  [shifted(): return lax.ppermute(x, axis, [(i, (i + by) % size) for i in range(size)])]
    squeeze x1 -> x0, local copies, waits for them, and re-layouts: 1.57 us -> none  [filters(): lax.dynamic_index_in_dim(jnp.asarray(depth_tables()), place, 0, keepdims=...]
  transfers between devices with their start and end apart: 12 -> 12, of which waited for: 6 -> 5; matrix products, arithmetic and copies ran while one was open for 2% -> 0% of each run, Pallas kernels for 17% -> 16%
where the time goes in v2:
time: 65.3 us; the launch traced here: 64.8 us
  Pallas kernels  32.4 us (50%)
  starting transfers between devices  14.6 us (22%)
  waiting for transfers between devices  13.5 us (21%)
  local copies, waits for them, and re-layouts  2.9 us (4%)
  between operations  0.8 us (1%)
    ppermute x12, starting transfers between devices, shifted(): return lax.ppermute(x, axis, [(i, (i + by) % size) for i in range(size)])  14.6 us
    pallas_call x1, Pallas kernels, filters(): pl.pallas_call(filter_kernel, out_shape=[jax.ShapeDtypeStruct((48 * 64, 1...  14.1 us
    ppermute x12, waiting for transfers between devices, shifted(): return lax.ppermute(x, axis, [(i, (i + by) % size) for i in range(size)])  13.5 us
    pallas_call x1, Pallas kernels, own_elements(): pl.pallas_call(own_kernel, out_shape=jax.ShapeDtypeStruct((2048, 1024), B...  10.4 us
    pallas_call x1, Pallas kernels, pack(): pl.pallas_call(pack_kernel, out_shape=[jax.ShapeDtypeStruct((PAYLOAD, 128...  5.66 us
    unnamed x18, local copies, waits for them, and re-layouts  2.9 us
    pallas_call x3, Pallas kernels, vmem_call(): pl.pallas_call(kernel, out_shape=out_shape, in_specs=[vmem] * len(operand...  2.22 us
  transfers between devices with their start and end apart: 12, of which 5 were waited for; matrix products, arithmetic and copies ran while one was open for 0% of the time, Pallas kernels for 16%

profile of v2, /device:TPU:30, one launch (start us, length us, event | category | flops | bytes accessed | tf_op | source)
XLA Modules:
  0.0 64.8 jit_solution(2627019073274474494)
XLA Ops:
  0.6 0.0 copy-start.2
  0.6 0.0 copy-start.3
  0.7 0.0 copy-start.1
  0.7 0.6 pad_add_fusion.coords
  1.3 5.7 %pack.1 = (bf16[336,128]{1,0:T(8,128)(2,1)}, bf16[336,128]{1,0:T(8,128)(2,1)}, bf16[336,128]{1,0:T(8,128)(2,1)}, bf16[336,128]{1,0:T(8,128)(2,1)}, bf16[336,128]...) custom-call(s32[4]{0:T(128)} %pad_add_fusion.coords, s32[8,128]{1,0:T(8,128)} %bitcast.12, ...), custom_call_target="tpu_custom_call" | custom-call | tf_op jit(solution)/shard_map/pack/pallas_call | solution.py:206
  7.0 0.0 collective-permute-start
  7.0 3.4 %collective-permute-start.1 = (bf16[336,128]{1,0:T(8,128)(2,1)}, bf16[336,128]{1,0:T(8,128)(2,1)S(1)}, u32[]{:S(2)}, u32[]{:S(2)}) collective-permute-start(bf16[336,128]{1,0:T(8,128)(2,1)} %get-tuple-element.23), channel_id=1, source_target_pairs={{0,112},{16,0},{32,16},{48,32},{64,48},{80,64},{96,80},{112,96},{1... | collective-permute-start | bytes 258056 | tf_op jit(solution)/shard_map/ppermute | solution.py:624
  10.4 0.3 collective-permute-start.2
  10.7 1.7 %collective-permute-start.3 = (bf16[336,128]{1,0:T(8,128)(2,1)}, bf16[336,128]{1,0:T(8,128)(2,1)S(1)}, u32[]{:S(2)}, u32[]{:S(2)}) collective-permute-start(bf16[336,128]{1,0:T(8,128)(2,1)} %get-tuple-element.25), channel_id=1, source_target_pairs={{0,12},{4,0},{8,4},{12,8},{1,13},{5,1},{9,5},{13,9},{2,14},{6,2},{... | collective-permute-start | bytes 258056 | tf_op jit(solution)/shard_map/ppermute | solution.py:624
  12.4 0.3 collective-permute-start.4
  12.7 0.0 collective-permute-done.a0
  12.7 1.7 %collective-permute-start.5 = (bf16[336,128]{1,0:T(8,128)(2,1)}, bf16[336,128]{1,0:T(8,128)(2,1)S(1)}, u32[]{:S(2)}, u32[]{:S(2)}) collective-permute-start(bf16[336,128]{1,0:T(8,128)(2,1)} %get-tuple-element.27), channel_id=1, source_target_pairs={{0,3},{1,0},{2,1},{3,2},{4,7},{5,4},{6,5},{7,6},{8,11},{9,8},{10,9... | collective-permute-start | bytes 258056 | tf_op jit(solution)/shard_map/ppermute | solution.py:624
  14.4 0.0 copy-done.2
  14.4 0.0 copy-done.3
  14.4 0.0 copy-done.1
  14.4 0.0 copy-start
  14.5 2.2 %copy-done = bf16[1024,4,512]{2,1,0:T(4,128)(2,1)S(1)} copy-done((bf16[1024,4,512]{2,1,0:T(4,128)(2,1)S(1)}, bf16[1024,4,512]{2,1,0:T(4,128)(2,1)}, u32[]{:S(2)}) %copy-start) | copy-done | bytes 4194328
  16.6 0.0 copy-start.8
  16.6 0.7 %copy-done.8 = s32[8,128]{1,0:T(8,128)S(1)} copy-done((s32[8,128]{1,0:T(8,128)S(1)}, s32[8,128]{1,0:T(8,128)}, u32[]{:S(2)}) %copy-start.8) | copy-done | bytes 4120
  17.3 0.0 copy-start.4
  17.3 0.0 copy-start.7
  17.3 10.4 %own_elements.1.uniform = bf16[2048,1024]{1,0:T(8,128)(2,1)S(1)} custom-call(s32[8,128]{1,0:T(8,128)S(1)} %copy-done.8, s32[8,128]{1,0:T(8,128)S(1)} %copy-done.8, bf16[16384,128]{1,0:T(8,128)(2,1)S(1)} %bitcast.11, bf16[1024,512]{1,0:T(8,128)(2,1)S(1)} %copy-done.1, bf16[512,512]{1,0:T(8,128)(2,1)S(1)} %copy-done.3, bf16[512,512]{1,0:T(8,128)(2,1)S(1)} %copy-done.2), custom_call_target="tpu_custom_call" | custom-call | flops 6000000000 | bytes 10000000 | tf_op jit(solution)/shard_map/own_elements/pallas_call | solution.py:270
  27.7 0.0 copy-start.5
  27.7 0.0 copy-start.6
  27.7 0.0 collective-permute-done.1.a1
  27.7 0.0 collective-permute-done.2.a2
  27.7 0.0 collective-permute-done.3.a3
  27.7 0.0 collective-permute-done.4.a4
  27.8 0.0 collective-permute-done.5.a5
  27.8 0.0 copy-done.4
  27.8 0.0 copy-done.7
  27.8 14.1 %filters.1 = (f32[3072,128]{1,0:T(8,128)S(1)}, f32[768,128]{1,0:T(8,128)S(1)}, f32[1280,128]{1,0:T(8,128)S(1)}, f32[640,128]{1,0:T(8,128)S(1)}, bf16[8,5760]{1,0...) custom-call(s32[4]{0:T(128)S(1)} %copy-done.7, bf16[2048,1024]{1,0:T(8,128)(2,1)S(1)} %own_elements.1.uniform, ...), custom_call_target="tpu_custom_call" | custom-call | tf_op jit(solution)/shard_map/filters/pallas_call | solution.py:500
  41.9 1.6 %collective-permute-start.6 = (bf16[8,5760]{1,0:T(8,128)(2,1)S(1)}, bf16[8,5760]{1,0:T(8,128)(2,1)S(1)}, u32[]{:S(2)}, u32[]{:S(2)}) collective-permute-start(bf16[8,5760]{1,0:T(8,128)(2,1)S(1)} %get-tuple-element.30), channel_id=1, source_target_pairs={{0,1},{1,2},{2,3},{3,0},{4,5},{5,6},{6,7},{7,4},{8,9},{9,10},{10,1... | collective-permute-start | bytes 276488 | tf_op jit(solution)/shard_map/ppermute | solution.py:624
  43.5 0.5 collective-permute-start.7
  44.0 2.5 %collective-permute-done.6.from_low.zl = bf16[8,5760]{1,0:T(8,128)(2,1)S(1)} collective-permute-done((bf16[8,5760]{1,0:T(8,128)(2,1)S(1)}, bf16[8,5760]{1,0:T(8,128)(2,1)S(1)}, u32[]{:S(2)}, u32[]{:S(2)}) %collective-permute-start.6) | collective-permute-done | bytes 92192 | tf_op jit(solution)/shard_map/ppermute | solution.py:624
  46.5 2.7 %collective-permute-done.7.from_high.zh = bf16[8,5760]{1,0:T(8,128)(2,1)S(1)} collective-permute-done((bf16[8,5760]{1,0:T(8,128)(2,1)S(1)}, bf16[8,5760]{1,0:T(8,128)(2,1)S(1)}, u32[]{:S(2)}, u32[]{:S(2)}) %collective-permute-start.7) | collective-permute-done | bytes 92192 | tf_op jit(solution)/shard_map/ppermute | solution.py:624
  49.3 0.0 copy-done.5
  49.3 0.0 copy-done.6
  49.3 0.3 y_edges.1
  49.6 1.3 %collective-permute-start.8 = (bf16[224,128]{1,0:T(8,128)(2,1)S(1)}, bf16[224,128]{1,0:T(8,128)(2,1)S(1)}, u32[]{:S(2)}, u32[]{:S(2)}) collective-permute-start(bf16[224,128]{1,0:T(8,128)(2,1)S(1)} %get-tuple-element.34), channel_id=1, source_target_pairs={{0,4},{4,8},{8,12},{12,0},{1,5},{5,9},{9,13},{13,1},{2,6},{6,10},{... | collective-permute-start | bytes 172040 | tf_op jit(solution)/shard_map/ppermute | solution.py:624
  50.9 0.8 %collective-permute-start.9 = (bf16[224,128]{1,0:T(8,128)(2,1)S(1)}, bf16[224,128]{1,0:T(8,128)(2,1)S(1)}, u32[]{:S(2)}, u32[]{:S(2)}) collective-permute-start(bf16[224,128]{1,0:T(8,128)(2,1)S(1)} %get-tuple-element.35), channel_id=1, source_target_pairs={{0,12},{4,0},{8,4},{12,8},{1,13},{5,1},{9,5},{13,9},{2,14},{6,2},{... | collective-permute-start | bytes 172040 | tf_op jit(solution)/shard_map/ppermute | solution.py:624
  51.7 2.2 %collective-permute-done.8.yl = bf16[224,128]{1,0:T(8,128)(2,1)S(1)} collective-permute-done((bf16[224,128]{1,0:T(8,128)(2,1)S(1)}, bf16[224,128]{1,0:T(8,128)(2,1)S(1)}, u32[]{:S(2)}, u32[]{:S(2)}) %collective-permute-start.8) | collective-permute-done | bytes 57376 | tf_op jit(solution)/shard_map/ppermute | solution.py:624
  53.9 2.4 %collective-permute-done.9.yh = bf16[224,128]{1,0:T(8,128)(2,1)S(1)} collective-permute-done((bf16[224,128]{1,0:T(8,128)(2,1)S(1)}, bf16[224,128]{1,0:T(8,128)(2,1)S(1)}, u32[]{:S(2)}, u32[]{:S(2)}) %collective-permute-start.9) | collective-permute-done | bytes 57376 | tf_op jit(solution)/shard_map/ppermute | solution.py:624
  56.3 0.7 %x_edges.1 = (f32[3072,128]{1,0:T(8,128)S(1)}, f32[1280,128]{1,0:T(8,128)S(1)}, bf16[896,128]{1,0:T(8,128)(2,1)S(1)}, bf16[896,128]{1,0:T(8,128)(2,1)S(1)}) custom-call(f32[3072,128]{1,0:T(8,128)S(1)} %get-tuple-element.28.main_a, f32[1280,128]{1,0:T(8,128)S(1)} %get-tuple-element.29.main_c, bf16[8,5760]{1,0:T(8,128)(2,1)S(1)} %collective-permute-done.6.from_low.zl, ...), custom_call_target="tpu_custom_call" | custom-call | tf_op jit(solution)/shard_map/x_edges/pallas_call | solution.py:563
  57.0 0.0 collective-permute-start.10
  57.1 2.9 %collective-permute-start.11 = (bf16[896,128]{1,0:T(8,128)(2,1)S(1)}, bf16[896,128]{1,0:T(8,128)(2,1)S(1)}, u32[]{:S(2)}, u32[]{:S(2)}) collective-permute-start(bf16[896,128]{1,0:T(8,128)(2,1)S(1)} %get-tuple-element.39), channel_id=1, source_target_pairs={{0,112},{16,0},{32,16},{48,32},{64,48},{80,64},{96,80},{112,96},{1... | collective-permute-start | bytes 688136 | tf_op jit(solution)/shard_map/ppermute | solution.py:624
  60.0 3.7 %collective-permute-done.10.xl = bf16[896,128]{1,0:T(8,128)(2,1)S(1)} collective-permute-done((bf16[896,128]{1,0:T(8,128)(2,1)S(1)}, bf16[896,128]{1,0:T(8,128)(2,1)S(1)}, u32[]{:S(2)}, u32[]{:S(2)}) %collective-permute-start.10) | collective-permute-done | bytes 229408 | tf_op jit(solution)/shard_map/ppermute | solution.py:624
  63.7 0.0 collective-permute-done.11.xh
  63.7 1.1 %final.1 = (f32[4,8,64,128]{3,2,1,0:T(8,128)}, f32[4,4,32,64]{3,2,1,0:T(8,128)}) custom-call(f32[3072,128]{1,0:T(8,128)S(1)} %get-tuple-element.36.sa, f32[1280,128]{1,0:T(8,128)S(1)} %get-tuple-element.37.sc, bf16[896,128]{1,0:T(8,128)(2,1)S(1)} %collective-permute-done.10.xl, bf16[896,128]{1,0:T(8,128)(2,1)S(1)} %collective-permute-done.11.xh), custom_call_target="tpu_custom_call" | custom-call | tf_op jit(solution)/shard_map/final/pallas_call | solution.py:563
Async XLA Ops:
  0.6 13.8 %copy-start.2 = (bf16[512,512]{1,0:T(8,128)(2,1)S(1)}, bf16[512,512]{1,0:T(8,128)(2,1)}, u32[]{:S(2)}) copy-start(bf16[512,512]{1,0:T(8,128)(2,1)} %constant.26.clone.order) | copy-start | bytes 1572868
  0.6 13.8 %copy-start.3 = (bf16[512,512]{1,0:T(8,128)(2,1)S(1)}, bf16[512,512]{1,0:T(8,128)(2,1)}, u32[]{:S(2)}) copy-start(bf16[512,512]{1,0:T(8,128)(2,1)} %constant.25.clone.table) | copy-start | bytes 1572868
  0.7 13.8 %copy-start.1 = (bf16[1024,512]{1,0:T(8,128)(2,1)S(1)}, bf16[1024,512]{1,0:T(8,128)(2,1)}, u32[]{:S(2)}) copy-start(bf16[1024,512]{1,0:T(8,128)(2,1)} %jac.1) | copy-start | bytes 3145732
  7.0 5.8 %collective-permute-start = (bf16[336,128]{1,0:T(8,128)(2,1)}, bf16[336,128]{1,0:T(8,128)(2,1)S(1)}, u32[]{:S(2)}, u32[]{:S(2)}) collective-permute-start(bf16[336,128]{1,0:T(8,128)(2,1)} %get-tuple-element.22), channel_id=1, source_target_pairs={{0,16},{16,32},{32,48},{48,64},{64,80},{80,96},{96,112},{112,0},{1... | collective-permute-start | bytes 258056 | tf_op jit(solution)/shard_map/ppermute | solution.py:624
  7.0 20.7 %collective-permute-start.1 = (bf16[336,128]{1,0:T(8,128)(2,1)}, bf16[336,128]{1,0:T(8,128)(2,1)S(1)}, u32[]{:S(2)}, u32[]{:S(2)}) collective-permute-start(bf16[336,128]{1,0:T(8,128)(2,1)} %get-tuple-element.23), channel_id=1, source_target_pairs={{0,112},{16,0},{32,16},{48,32},{64,48},{80,64},{96,80},{112,96},{1... | collective-permute-start | bytes 258056 | tf_op jit(solution)/shard_map/ppermute | solution.py:624
  10.4 17.3 %collective-permute-start.2 = (bf16[336,128]{1,0:T(8,128)(2,1)}, bf16[336,128]{1,0:T(8,128)(2,1)S(1)}, u32[]{:S(2)}, u32[]{:S(2)}) collective-permute-start(bf16[336,128]{1,0:T(8,128)(2,1)} %get-tuple-element.24), channel_id=1, source_target_pairs={{0,4},{4,8},{8,12},{12,0},{1,5},{5,9},{9,13},{13,1},{2,6},{6,10},{... | collective-permute-start | bytes 258056 | tf_op jit(solution)/shard_map/ppermute | solution.py:624
  10.7 17.0 %collective-permute-start.3 = (bf16[336,128]{1,0:T(8,128)(2,1)}, bf16[336,128]{1,0:T(8,128)(2,1)S(1)}, u32[]{:S(2)}, u32[]{:S(2)}) collective-permute-start(bf16[336,128]{1,0:T(8,128)(2,1)} %get-tuple-element.25), channel_id=1, source_target_pairs={{0,12},{4,0},{8,4},{12,8},{1,13},{5,1},{9,5},{13,9},{2,14},{6,2},{... | collective-permute-start | bytes 258056 | tf_op jit(solution)/shard_map/ppermute | solution.py:624
  12.4 15.3 %collective-permute-start.4 = (bf16[336,128]{1,0:T(8,128)(2,1)}, bf16[336,128]{1,0:T(8,128)(2,1)S(1)}, u32[]{:S(2)}, u32[]{:S(2)}) collective-permute-start(bf16[336,128]{1,0:T(8,128)(2,1)} %get-tuple-element.26), channel_id=1, source_target_pairs={{0,1},{1,2},{2,3},{3,0},{4,5},{5,6},{6,7},{7,4},{8,9},{9,10},{10,1... | collective-permute-start | bytes 258056 | tf_op jit(solution)/shard_map/ppermute | solution.py:624
  12.7 15.0 %collective-permute-start.5 = (bf16[336,128]{1,0:T(8,128)(2,1)}, bf16[336,128]{1,0:T(8,128)(2,1)S(1)}, u32[]{:S(2)}, u32[]{:S(2)}) collective-permute-start(bf16[336,128]{1,0:T(8,128)(2,1)} %get-tuple-element.27), channel_id=1, source_target_pairs={{0,3},{1,0},{2,1},{3,2},{4,7},{5,4},{6,5},{7,6},{8,11},{9,8},{10,9... | collective-permute-start | bytes 258056 | tf_op jit(solution)/shard_map/ppermute | solution.py:624
  14.4 2.2 %copy-start = (bf16[1024,4,512]{2,1,0:T(4,128)(2,1)S(1)}, bf16[1024,4,512]{2,1,0:T(4,128)(2,1)}, u32[]{:S(2)}) copy-start(bf16[1024,4,512]{2,1,0:T(4,128)(2,1)} %param.10) | copy-start | bytes 12582916
  16.6 0.7 %copy-start.8 = (s32[8,128]{1,0:T(8,128)S(1)}, s32[8,128]{1,0:T(8,128)}, u32[]{:S(2)}) copy-start(s32[8,128]{1,0:T(8,128)} %get-tuple-element.21.spot_s.spot_v) | copy-start | bytes 12292
  17.3 10.5 %copy-start.4 = (bf16[3,256,256]{2,1,0:T(8,128)(2,1)S(1)}, bf16[3,256,256]{2,1,0:T(8,128)(2,1)}, u32[]{:S(2)}) copy-start(bf16[3,256,256]{2,1,0:T(8,128)(2,1)} %constant.27.clone.depths) | copy-start | bytes 1179652
  17.3 10.5 %copy-start.7 = (s32[4]{0:T(128)S(1)}, s32[4]{0:T(128)}, u32[]{:S(2)}) copy-start(s32[4]{0:T(128)} %pad_add_fusion.coords) | copy-start | bytes 52
  27.7 21.6 %copy-start.5 = (bf16[16,128]{1,0:T(8,128)(2,1)S(1)}, bf16[16,128]{1,0:T(8,128)(2,1)}, u32[]{:S(2)}) copy-start(bf16[16,128]{1,0:T(8,128)(2,1)} %constant.29.clone.spread_c) | copy-start | bytes 12292
  27.7 21.6 %copy-start.6 = (bf16[16,128]{1,0:T(8,128)(2,1)S(1)}, bf16[16,128]{1,0:T(8,128)(2,1)}, u32[]{:S(2)}) copy-start(bf16[16,128]{1,0:T(8,128)(2,1)} %constant.28.clone.spread_a) | copy-start | bytes 12292
  41.9 4.6 %collective-permute-start.6 = (bf16[8,5760]{1,0:T(8,128)(2,1)S(1)}, bf16[8,5760]{1,0:T(8,128)(2,1)S(1)}, u32[]{:S(2)}, u32[]{:S(2)}) collective-permute-start(bf16[8,5760]{1,0:T(8,128)(2,1)S(1)} %get-tuple-element.30), channel_id=1, source_target_pairs={{0,1},{1,2},{2,3},{3,0},{4,5},{5,6},{6,7},{7,4},{8,9},{9,10},{10,1... | collective-permute-start | bytes 276488 | tf_op jit(solution)/shard_map/ppermute | solution.py:624
  43.5 5.8 %collective-permute-start.7 = (bf16[8,5760]{1,0:T(8,128)(2,1)S(1)}, bf16[8,5760]{1,0:T(8,128)(2,1)S(1)}, u32[]{:S(2)}, u32[]{:S(2)}) collective-permute-start(bf16[8,5760]{1,0:T(8,128)(2,1)S(1)} %get-tuple-element.31), channel_id=1, source_target_pairs={{0,3},{1,0},{2,1},{3,2},{4,7},{5,4},{6,5},{7,6},{8,11},{9,8},{10,9... | collective-permute-start | bytes 276488 | tf_op jit(solution)/shard_map/ppermute | solution.py:624
  49.6 4.2 %collective-permute-start.8 = (bf16[224,128]{1,0:T(8,128)(2,1)S(1)}, bf16[224,128]{1,0:T(8,128)(2,1)S(1)}, u32[]{:S(2)}, u32[]{:S(2)}) collective-permute-start(bf16[224,128]{1,0:T(8,128)(2,1)S(1)} %get-tuple-element.34), channel_id=1, source_target_pairs={{0,4},{4,8},{8,12},{12,0},{1,5},{5,9},{9,13},{13,1},{2,6},{6,10},{... | collective-permute-start | bytes 172040 | tf_op jit(solution)/shard_map/ppermute | solution.py:624
  50.9 5.4 %collective-permute-start.9 = (bf16[224,128]{1,0:T(8,128)(2,1)S(1)}, bf16[224,128]{1,0:T(8,128)(2,1)S(1)}, u32[]{:S(2)}, u32[]{:S(2)}) collective-permute-start(bf16[224,128]{1,0:T(8,128)(2,1)S(1)} %get-tuple-element.35), channel_id=1, source_target_pairs={{0,12},{4,0},{8,4},{12,8},{1,13},{5,1},{9,5},{13,9},{2,14},{6,2},{... | collective-permute-start | bytes 172040 | tf_op jit(solution)/shard_map/ppermute | solution.py:624
  57.0 6.7 %collective-permute-start.10 = (bf16[896,128]{1,0:T(8,128)(2,1)S(1)}, bf16[896,128]{1,0:T(8,128)(2,1)S(1)}, u32[]{:S(2)}, u32[]{:S(2)}) collective-permute-start(bf16[896,128]{1,0:T(8,128)(2,1)S(1)} %get-tuple-element.38), channel_id=1, source_target_pairs={{0,16},{16,32},{32,48},{48,64},{64,80},{80,96},{96,112},{112,0},{1... | collective-permute-start | bytes 688136 | tf_op jit(solution)/shard_map/ppermute | solution.py:624
  57.1 6.6 %collective-permute-start.11 = (bf16[896,128]{1,0:T(8,128)(2,1)S(1)}, bf16[896,128]{1,0:T(8,128)(2,1)S(1)}, u32[]{:S(2)}, u32[]{:S(2)}) collective-permute-start(bf16[896,128]{1,0:T(8,128)(2,1)S(1)} %get-tuple-element.39), channel_id=1, source_target_pairs={{0,112},{16,0},{32,16},{48,32},{64,48},{80,64},{96,80},{112,96},{1... | collective-permute-start | bytes 688136 | tf_op jit(solution)/shard_map/ppermute | solution.py:624

commit v3 on v2

--- a/solution.py
+++ b/solution.py
@@ -223,29 +223,32 @@
     )(coords, home, jac, fields_rows)
 
 
-def own_kernel(spot_s, spot_v, fields, jac, table, order, out, rows, jac_t):
-    def clear(e, carry):
-        rows[pl.ds(pl.multiple_of(e * 512, 512), 512), :] = jnp.zeros((512, 128), F32)
-        return carry
-
-    lax.fori_loop(0, 32, clear, 0)
-
-    def place(e, carry):
-        for u in range(16):
-            spot = spot_s[e >> 3, (e & 7) * 16 + u]
-            rows[pl.ds(pl.multiple_of(spot * 16, 16), 16), :] = fields[
-                pl.ds(pl.multiple_of(e * 256 + u * 16, 16), 16), :
-            ].astype(F32)
-        return carry
-
-    lax.fori_loop(0, 64, place, 0)
+def local_call(kernel, outs, specs, operands, name, out_specs=None, scratch=(),
+               aliases=None, flops=0, limit=16):
+    vmem = pl.BlockSpec(memory_space=pltpu.VMEM)
+    return pl.pallas_call(
+        kernel,
+        out_shape=list(outs),
+        in_specs=specs,
+        out_specs=out_specs or [vmem] * len(outs),
+        scratch_shapes=list(scratch),
+        input_output_aliases=aliases or {},
+        compiler_params=pltpu.CompilerParams(vmem_limit_bytes=limit * MIB),
+        cost_estimate=pl.CostEstimate(
+            flops=flops, bytes_accessed=1_000_000, transcendentals=0
+        ),
+        name=name,
+    )(*operands)
+
+
+def jacobian_kernel(spots, jac, order, jac_t):
     ordered = nt(order[...], jac[...]).astype(BF16)
     for c in range(4):
         ids = lax.broadcasted_iota(jnp.int32, (256, 128), 0) + c * 256
         hit = jnp.concatenate(
             [
                 jnp.where(
-                    ids == jnp.broadcast_to(spot_v[r : r + 1, :], (256, 128)), 1.0, 0.0
+                    ids == jnp.broadcast_to(spots[r : r + 1, :], (256, 128)), 1.0, 0.0
                 ).astype(BF16)
                 for r in range(8)
             ],
@@ -253,76 +256,29 @@
         )
         jac_t[:, c * 256 : c * 256 + 256] = nt(ordered, hit)
 
-    for n in range(4):
-        for f in range(4):
-            pieces = [
-                rows[pl.ds(n * 4096 + c * 4 + f, 256, stride=16), :].astype(BF16)
-                for c in range(4)
-            ]
-            values = nt(table[...], jnp.concatenate(pieces, axis=1))
-            out[f * 512 : f * 512 + 512, n * 256 : n * 256 + 256] = (
-                values * jac_t[:, n * 256 : n * 256 + 256]
-            ).astype(BF16)
-
-
-def own_elements(spots, fields_rows, jac):
-    vmem = pl.BlockSpec(memory_space=pltpu.VMEM)
-    return pl.pallas_call(
-        own_kernel,
-        out_shape=jax.ShapeDtypeStruct((2048, 1024), BF16),
-        in_specs=[pl.BlockSpec(memory_space=pltpu.SMEM)] + [vmem] * 5,
-        out_specs=vmem,
-        scratch_shapes=[
-            pltpu.VMEM((1025 * 16, 128), F32),
-            pltpu.VMEM((512, 1024), F32),
-        ],
-        compiler_params=pltpu.CompilerParams(vmem_limit_bytes=28 * MIB),
-        cost_estimate=pl.CostEstimate(
-            flops=6_000_000_000, bytes_accessed=10_000_000, transcendentals=0
-        ),
-        name="own_elements",
-    )(
-        spots,
-        spots,
-        fields_rows,
-        jac,
-        jnp.asarray(interp_table()),
-        jnp.asarray(point_order()),
-    )
-
-
-def halve(values, outputs, shift):
-    results = []
-    for o in range(outputs):
-        total = None
-        for tap in range(8):
-            at = 2 * o + tap - shift
-            if 0 <= at < len(values):
-                term = TAPS[tap] * values[at]
-                total = term if total is None else total + term
-        results.append(total)
-    return results
-
-
-def filter_kernel(
-    coords, uniform, a0, a1, a2, a3, a4, a5, table, order, depths,
-    main_a, edge_a, main_c, edge_c, to_low, to_high,
-    raw, arrived, depth, wide, ya, yb, mb, yc, pbz, pcz, sem,
-):
+
+def place_kernel(spots, fields, rows):
+    def place(e, carry):
+        targets = [spots[e * 32 + u] for u in range(32)]
+        values = [fields[e * 32 + u] for u in range(32)]
+        for u in range(32):
+            rows[targets[u]] = values[u].astype(F32)
+        return carry
+
+    lax.fori_loop(0, 32, place, 0)
+
+
+def arrive_kernel(a0, a1, a2, a3, a4, a5, order, jac_in, rows_in, jac_t, rows,
+                  staged, spot_v, spot_s, sem, sem_rows):
     arrays = (a0, a1, a2, a3, a4, a5)
-    one = lambda flag: jnp.where(flag, 1.0, 0.0)
-    x_low = one(coords[0] > 0)
-    x_high = one(coords[0] < 7)
-    y_low = one(coords[1] > 0)
-    y_high = one(coords[1] < 3)
-
-    spot_z = coords[2]
-    place = jnp.where(spot_z == 0, 0, jnp.where(spot_z == 3, 2, 1))
-    copy = pltpu.make_async_copy(depths.at[place], depth, sem)
+    tags = jnp.zeros((8, 128), F32)
+    for d in range(6):
+        tags = tags + arrays[d][320:336, :].astype(F32)[0:8]
+    spot = (tags[0:1] * 32.0 + tags[1:2]).astype(jnp.int32) - 1
+    spare = lax.broadcasted_iota(jnp.int32, (1, 128), 1) + 1024
+    spot_v[...] = jnp.broadcast_to(jnp.where(spot < 0, spare, spot), (8, 128))
+    copy = pltpu.make_async_copy(spot_v, spot_s, sem)
     copy.start()
-    raw[1536:2048, :] = jnp.zeros((512, 128), F32)
-    for d in range(6):
-        raw[d * 256 : d * 256 + 256, :] = arrays[d][0:256, :].astype(F32)
     jac = jnp.concatenate(
         [
             jnp.concatenate(
@@ -333,13 +289,147 @@
         + [jnp.zeros((32, 512), BF16)],
         axis=0,
     )
-    jac_t = nt(order[...], jac)
-    for f in range(4):
-        pieces = [
-            raw[pl.ds(c * 4 + f, 128, stride=16), :].astype(BF16) for c in range(4)
-        ]
-        values = nt(table[...], jnp.concatenate(pieces, axis=1))
-        arrived[f * 512 : f * 512 + 512, :] = (values * jac_t).astype(BF16)
+    ordered = nt(order[...], jac).astype(BF16)
+    for c in range(4):
+        ids = lax.broadcasted_iota(jnp.int32, (256, 128), 0) + c * 256
+        hit = jnp.where(ids == jnp.broadcast_to(spot, (256, 128)), 1.0, 0.0).astype(BF16)
+        jac_t[:, c * 256 : c * 256 + 256] = jac_in[:, c * 256 : c * 256 + 256] + nt(ordered, hit)
+    for d in range(6):
+        for e in range(16):
+            staged[d * 16 + e] = arrays[d][e * 16 : e * 16 + 16, :].astype(F32)
+    copy.wait()
+    for e in range(96):
+        pltpu.make_async_copy(staged.at[e], rows.at[spot_s[0, e]], sem_rows).start()
+    pltpu.make_async_copy(staged, rows.at[pl.ds(0, 96)], sem_rows).wait()
+
+
+def fields_kernel(rows, jac_t, table, u0, u1, u2, u3):
+    for f, out in enumerate((u0, u1, u2, u3)):
+        for n in range(4):
+            pieces = [
+                rows[pl.ds(n * 4096 + c * 4 + f, 256, stride=16), :].astype(BF16)
+                for c in range(4)
+            ]
+            values = nt(table[...], jnp.concatenate(pieces, axis=1))
+            out[:, n * 256 : n * 256 + 256] = (
+                values * jac_t[:, n * 256 : n * 256 + 256]
+            ).astype(BF16)
+
+
+def own_elements(spots, fields_elems, jac):
+    vmem = pl.BlockSpec(memory_space=pltpu.VMEM)
+    smem = pl.BlockSpec(memory_space=pltpu.SMEM)
+    order = jnp.asarray(point_order())
+    [jac_t] = local_call(
+        jacobian_kernel,
+        [jax.ShapeDtypeStruct((512, 1024), F32)],
+        [vmem] * 3,
+        [spots, jac, order],
+        "jacobians",
+        flops=2_000_000_000,
+    )
+    [rows] = local_call(
+        place_kernel,
+        [jax.ShapeDtypeStruct((1152, 16, 128), F32)],
+        [smem, vmem],
+        [spots.reshape(1024), fields_elems],
+        "place",
+        flops=2_000_000_000,
+    )
+    return rows, jac_t
+
+
+def all_elements(rows, jac_t, arrived):
+    vmem = pl.BlockSpec(memory_space=pltpu.VMEM)
+    anywhere = pl.BlockSpec(memory_space=pl.ANY)
+    jac_t, rows = local_call(
+        arrive_kernel,
+        [
+            jax.ShapeDtypeStruct((512, 1024), F32),
+            jax.ShapeDtypeStruct((1152, 16, 128), F32),
+        ],
+        [vmem] * 8 + [anywhere],
+        [*arrived, jnp.asarray(point_order()), jac_t, rows],
+        "arrive",
+        out_specs=[vmem, anywhere],
+        scratch=[
+            pltpu.VMEM((96, 16, 128), F32),
+            pltpu.VMEM((8, 128), jnp.int32),
+            pltpu.SMEM((8, 128), jnp.int32),
+            pltpu.SemaphoreType.DMA,
+            pltpu.SemaphoreType.DMA,
+        ],
+        aliases={8: 1},
+    )
+    return local_call(
+        fields_kernel,
+        [jax.ShapeDtypeStruct((512, 1024), BF16)] * 4,
+        [vmem] * 3,
+        [rows.reshape(1152 * 16, 128), jac_t, jnp.asarray(interp_table())],
+        "fields",
+        limit=24,
+    )
+
+
+def halve(values, outputs, shift):
+    results = []
+    for o in range(outputs):
+        total = None
+        for tap in range(4):
+            pair = [
+                values[at]
+                for at in (2 * o + tap - shift, 2 * o + 7 - tap - shift)
+                if 0 <= at < len(values)
+            ]
+            if pair:
+                term = TAPS[tap] * (pair[0] + pair[1] if len(pair) == 2 else pair[0])
+                total = term if total is None else total + term
+        results.append(total)
+    return results
+
+
+def along_y(ref, base, count, y_low, y_high):
+    total = None
+    for tap in range(4):
+        pair = (
+            ref[pl.ds(base + 5 + tap, count, stride=2), :]
+            + ref[pl.ds(base + 12 - tap, count, stride=2), :]
+        )
+        total = TAPS[tap] * pair if total is None else total + TAPS[tap] * pair
+    low = total[0:8] * y_low
+    high = total[count - 8 : count] * y_high
+    return low, total[8 : count - 8], high
+
+
+def first_y_kernel(coords, ya, main_a, edge_a):
+    y_low = jnp.where(coords[1] > 0, 1.0, 0.0)
+    y_high = jnp.where(coords[1] < 3, 1.0, 0.0)
+
+    def first(q, carry):
+        low, middle, high = along_y(ya, q * 176, 80, y_low, y_high)
+        edge_a[pl.ds(pl.multiple_of(q * 16, 16), 8), :] = low
+        edge_a[pl.ds(pl.multiple_of(q * 16 + 8, 8), 8), :] = high
+        main_a[pl.ds(pl.multiple_of(q * 64, 64), 64), :] = middle
+        return carry
+
+    lax.fori_loop(0, 48, first, 0)
+
+
+def filter_kernel(
+    coords, u0, u1, u2, u3, depths,
+    ya, main_c, edge_c, to_low, to_high,
+    depth, wide, yb, mb, yc, pbz, pcz, sem,
+):
+    one = lambda flag: jnp.where(flag, 1.0, 0.0)
+    x_low = one(coords[0] > 0)
+    x_high = one(coords[0] < 7)
+    y_low = one(coords[1] > 0)
+    y_high = one(coords[1] < 3)
+
+    spot_z = coords[2]
+    place = jnp.where(spot_z == 0, 0, jnp.where(spot_z == 3, 2, 1))
+    copy = pltpu.make_async_copy(depths.at[place], depth, sem)
+    copy.start()
     def pads(q, carry):
         zero = jnp.zeros((24, 128), F32)
         base = pl.multiple_of(q * 176, 8)
@@ -360,27 +450,16 @@
     lax.fori_loop(0, 40, more_pads, 0)
     copy.wait()
 
-    tags = jnp.zeros((8, 128), F32)
-    for d in range(6):
-        tags = tags + arrays[d][320:336, :].astype(F32)[0:8]
-    spot = (tags[0:1] * 32.0 + tags[1:2]).astype(jnp.int32) - 1
     def quarter(t, carry):
-        row = lax.broadcasted_iota(jnp.int32, (256, 128), 0)
-        ids = jnp.where(row < 128, row, row + 384) + t * 128
-        hit = jnp.where(ids == jnp.broadcast_to(spot, (256, 128)), 1.0, 0.0).astype(BF16)
         lane = lax.broadcasted_iota(jnp.int32, (64, 128), 1)
         odd = (lane & 32) != 0
         upper = (lane & 64) != 0
         for f in range(4):
-            both = nt(arrived[f * 512 : f * 512 + 512, :], hit)
             pieces = [[], [], [], []]
             for ex in range(2):
-                part = both[:, ex * 128 : ex * 128 + 128]
-                own = uniform[
-                    f * 512 : f * 512 + 512,
-                    pl.ds(pl.multiple_of(ex * 512 + t * 128, 128), 128),
+                total = (u0, u1, u2, u3)[f][
+                    :, pl.ds(pl.multiple_of(ex * 512 + t * 128, 128), 128)
                 ]
-                total = part + own.astype(F32)
                 regrouped = []
                 for h in range(2):
                     v = [total[(h * 4 + k) * 64 : (h * 4 + k) * 64 + 64] for k in range(4)]
@@ -397,7 +476,7 @@
                     regrouped.append(v)
                 for e in range(4):
                     pieces[e].append(
-                        jnp.concatenate([regrouped[0][e], regrouped[1][e]], axis=1).astype(BF16)
+                        jnp.concatenate([regrouped[0][e], regrouped[1][e]], axis=1)
                     )
             operand = jnp.concatenate([p for e in range(4) for p in pieces[e]], axis=0)
             wide[f * 512 : f * 512 + 512, :] = nn(operand, depth[...])
@@ -427,21 +506,8 @@
 
     lax.fori_loop(0, 4, quarter, 0)
 
-    def along_y(ref, base, count):
-        total = None
-        for tap in range(8):
-            term = TAPS[tap] * ref[pl.ds(base + 5 + tap, count, stride=2), :]
-            total = term if total is None else total + term
-        low = total[0:8] * y_low
-        high = total[count - 8 : count] * y_high
-        return low, total[8 : count - 8], high
-
     def first(q, carry):
-        low, middle, high = along_y(ya, q * 176, 80)
-        edge_a[pl.ds(pl.multiple_of(q * 16, 16), 8), :] = low
-        edge_a[pl.ds(pl.multiple_of(q * 16 + 8, 8), 8), :] = high
-        main_a[pl.ds(pl.multiple_of(q * 64, 64), 64), :] = middle
-        low, middle, high = along_y(yb, q * 176, 80)
+        low, middle, high = along_y(yb, q * 176, 80, y_low, y_high)
         base = pl.multiple_of(q * 80, 16)
         mb[pl.ds(base, 8), :] = low
         mb[pl.ds(base + 8, 64), :] = middle
@@ -474,7 +540,7 @@
     lax.fori_loop(0, 10, along_x, 0)
 
     def second(q, carry):
-        low, middle, high = along_y(yc, q * 112, 48)
+        low, middle, high = along_y(yc, q * 112, 48, y_low, y_high)
         edge_c[pl.ds(pl.multiple_of(q * 16, 16), 8), :] = low
         edge_c[pl.ds(pl.multiple_of(q * 16 + 8, 8), 8), :] = high
         main_c[pl.ds(pl.multiple_of(q * 32, 32), 32), :] = middle
@@ -487,36 +553,37 @@
     lax.fori_loop(0, 40, second, 0)
     row = lax.broadcasted_iota(jnp.int32, (16, 128), 0)
     lane = lax.broadcasted_iota(jnp.int32, (16, 128), 1)
-    pick = lambda count, first_lane: jnp.where(
-        (row < count) & (lane == row + first_lane), 1.0, 0.0
-    ).astype(BF16)
-    for ref, at_mid, at_coarse in ((to_low, 64, 68), (to_high, 66, 71)):
-        ref[:, 0:3840] = nt(pick(2, at_mid), pbz[...])[0:8].astype(BF16)
-        ref[:, 3840:5760] = nt(pick(3, at_coarse), pcz[...])[0:8].astype(BF16)
-
-
-def filters(coords, uniform_t, arrived):
+
+    def pick(count, low_lane, high_lane):
+        low = (row < count) & (lane == row + low_lane)
+        high = (row >= 8) & (row < 8 + count) & (lane == row - 8 + high_lane)
+        return jnp.where(low | high, 1.0, 0.0).astype(BF16)
+
+    mid = nt(pick(2, 64, 66), pbz[...])
+    coarse = nt(pick(3, 68, 71), pcz[...])
+    for ref, at in ((to_low, 0), (to_high, 8)):
+        ref[:, 0:3840] = mid[at : at + 8].astype(BF16)
+        ref[:, 3840:5760] = coarse[at : at + 8].astype(BF16)
+
+
+def filters(coords, uniform_t):
     vmem = pl.BlockSpec(memory_space=pltpu.VMEM)
-    return pl.pallas_call(
+    smem = pl.BlockSpec(memory_space=pltpu.SMEM)
+    return local_call(
         filter_kernel,
-        out_shape=[
-            jax.ShapeDtypeStruct((48 * 64, 128), F32),
-            jax.ShapeDtypeStruct((48 * 16, 128), F32),
+        [
+            jax.ShapeDtypeStruct((48 * 176, 128), F32),
             jax.ShapeDtypeStruct((40 * 32, 128), F32),
             jax.ShapeDtypeStruct((40 * 16, 128), F32),
             jax.ShapeDtypeStruct((8, 5760), BF16),
             jax.ShapeDtypeStruct((8, 5760), BF16),
         ],
-        in_specs=[pl.BlockSpec(memory_space=pltpu.SMEM)]
-        + [vmem] * 9
-        + [pl.BlockSpec(memory_space=pltpu.HBM)],
-        out_specs=[vmem] * 6,
-        scratch_shapes=[
-            pltpu.VMEM((2048, 128), F32),
-            pltpu.VMEM((2048, 128), BF16),
+        [smem] + [vmem] * 4 + [pl.BlockSpec(memory_space=pltpu.HBM)],
+        [coords, *uniform_t, jnp.asarray(depth_tables())],
+        "filters",
+        scratch=[
             pltpu.VMEM((256, 256), BF16),
             pltpu.VMEM((2048, 256), F32),
-            pltpu.VMEM((48 * 176, 128), F32),
             pltpu.VMEM((48 * 176, 128), F32),
             pltpu.VMEM((48 * 80, 128), F32),
             pltpu.VMEM((40 * 112, 128), F32),
@@ -524,15 +591,19 @@
             pltpu.VMEM((1920, 128), BF16),
             pltpu.SemaphoreType.DMA,
         ],
-        compiler_params=pltpu.CompilerParams(vmem_limit_bytes=32 * MIB),
-        name="filters",
-    )(
-        coords,
-        uniform_t,
-        *arrived,
-        jnp.asarray(interp_table()),
-        jnp.asarray(point_order()),
-        jnp.asarray(depth_tables()),
+        limit=32,
+    )
+
+
+def first_y(coords, ya):
+    vmem = pl.BlockSpec(memory_space=pltpu.VMEM)
+    return local_call(
+        first_y_kernel,
+        [jax.ShapeDtypeStruct((48 * 64, 128), F32), jax.ShapeDtypeStruct((48 * 16, 128), F32)],
+        [pl.BlockSpec(memory_space=pltpu.SMEM), vmem],
+        [coords, ya],
+        "first_y",
+        flops=2_000_000_000,
     )
 
 
@@ -572,12 +643,16 @@
     )(*operands)
 
 
-def x_edges_kernel(main_a, main_c, zl, zh, yl, yh, spread_a, spread_c,
-                   sa, sc, to_low, to_high, fl, fh):
+def z_main_kernel(main_a, main_c, zl, zh, spread_a, spread_c, sa, sc):
     lanes = jnp.concatenate([zl[:, 768:3840], zh[:, 768:3840]], axis=0)
     sa[...] = main_a[...] + tn(lanes, spread_a[...])
     lanes = jnp.concatenate([zl[:, 4480:5760], zh[:, 4480:5760]], axis=0)
     sc[...] = main_c[...] + tn(lanes, spread_c[...])
+
+
+def x_edges_kernel(sa_in, sc_in, yl, yh, sa, sc, to_low, to_high, fl, fh):
+    sa[...] = sa_in[...]
+    sc[...] = sc_in[...]
     fl[...] = yl[...].astype(F32)
     fh[...] = yh[...].astype(F32)
     for r in range(2):
@@ -626,20 +701,22 @@
 
 def local_views(fields, home_slot):
     fields_rows = fields.reshape(1024, 4, 4, 128).transpose(0, 2, 1, 3).reshape(16384, 128)
-    return fields_rows, home_slot.reshape(8, 128)
+    return fields_rows, fields_rows.reshape(1024, 16, 128), home_slot.reshape(8, 128)
 
 
 def body(fields, jacobian, home_slot):
     ix, iy, iz = (lax.axis_index(axis) for axis in ("gx", "gy", "gz"))
     me = (ix * lax.axis_size("gy") + iy) * lax.axis_size("gz") + iz
     coords = jnp.stack([ix, iy, iz, me]).astype(jnp.int32)
-    fields_rows, home_tile = local_views(fields, home_slot)
+    fields_rows, fields_elems, home_tile = local_views(fields, home_slot)
     *payloads, spots = pack(coords, home_tile, jacobian, fields_rows)
-    arrived = [shifted(p, axis, by) for p, (axis, by) in zip(payloads, SHIFTS)]
-    uniform_t = own_elements(spots, fields_rows, jacobian)
-    main_a, edge_a, main_c, edge_c, z_low, z_high = filters(coords, uniform_t, arrived)
+    arrived = [shifted(p, *move) for p, move in zip(payloads, SHIFTS)]
+    rows, jac_t = own_elements(spots, fields_elems, jacobian)
+    uniform_t = all_elements(rows, jac_t, arrived)
+    ya, main_c, edge_c, z_low, z_high = filters(coords, uniform_t)
     from_z_low = shifted(z_high, "gz", 1)
     from_z_high = shifted(z_low, "gz", -1)
+    main_a, edge_a = first_y(coords, ya)
     spread_a = jnp.asarray(depth_spread(126, 2))
     spread_c = jnp.asarray(depth_spread(61, 3))
     y_low, y_high = vmem_call(
@@ -651,17 +728,26 @@
     )
     from_y_low = shifted(y_high, "gy", 1)
     from_y_high = shifted(y_low, "gy", -1)
-    sum_a, sum_c, x_low, x_high = vmem_call(
+    vmem = pl.BlockSpec(memory_space=pltpu.VMEM)
+    shapes = [
+        jax.ShapeDtypeStruct((48 * 64, 128), F32),
+        jax.ShapeDtypeStruct((40 * 32, 128), F32),
+    ]
+    sum_a, sum_c = local_call(
+        z_main_kernel,
+        shapes,
+        [vmem] * 6,
+        [main_a, main_c, from_z_low, from_z_high, spread_a, spread_c],
+        "z_main",
+        flops=2_000_000_000,
+    )
+    sum_a, sum_c, x_low, x_high = local_call(
         x_edges_kernel,
-        [
-            jax.ShapeDtypeStruct((48 * 64, 128), F32),
-            jax.ShapeDtypeStruct((40 * 32, 128), F32),
-            jax.ShapeDtypeStruct((896, 128), BF16),
-            jax.ShapeDtypeStruct((896, 128), BF16),
-        ],
-        [pltpu.VMEM((224, 128), F32), pltpu.VMEM((224, 128), F32)],
+        shapes + [jax.ShapeDtypeStruct((896, 128), BF16)] * 2,
+        [vmem] * 4,
+        [sum_a, sum_c, from_y_low, from_y_high],
         "x_edges",
-        main_a, main_c, from_z_low, from_z_high, from_y_low, from_y_high, spread_a, spread_c,
+        scratch=[pltpu.VMEM((224, 128), F32), pltpu.VMEM((224, 128), F32)],
     )
     from_x_low = shifted(x_high, "gx", 1)
     from_x_high = shifted(x_low, "gx", -1)

time: 65.3 us -> 58.1 us (0.89)
  Pallas kernels: 32.4 us -> 28.7 us
  local copies, waits for them, and re-layouts: 2.9 us -> 0.72 us
  waiting for transfers between devices: 13.5 us -> 12.2 us
    pallas_call x2 -> x8, Pallas kernels: 24.5 us -> 21.4 us  [local_call(): pl.pallas_call(kernel, out_shape=list(outs), in_specs=specs, out_specs=ou...]
    unnamed x18 -> x22, local copies, waits for them, and re-layouts: 2.9 us -> 0.72 us
    ppermute x12, waiting for transfers between devices: 13.5 us -> 12.2 us  [shifted(): return lax.ppermute(x, axis, [(i, (i + by) % size) for i in range(size)])]
    pallas_call x3 -> x2, Pallas kernels: 2.22 us -> 1.49 us  [vmem_call(): pl.pallas_call(kernel, out_shape=out_shape, in_specs=[vmem] * len(operand...]
  transfers between devices with their start and end apart: 12 -> 12, of which waited for: 5 -> 6; matrix products, arithmetic and copies ran while one was open for 0% -> 0% of each run, Pallas kernels for 16% -> 10%
where the time goes in v3:
time: 58.1 us; the launch traced here: 57.6 us
  Pallas kernels  28.7 us (49%)
  starting transfers between devices  14.6 us (25%)
  waiting for transfers between devices  12.2 us (21%)
  between operations  0.85 us (1%)
  local copies, waits for them, and re-layouts  0.72 us (1%)
  other arithmetic  0.62 us (1%)
    pallas_call x8, Pallas kernels, local_call(): pl.pallas_call(kernel, out_shape=list(outs), in_specs=specs, out_specs=ou...  21.4 us
    ppermute x12, starting transfers between devices, shifted(): return lax.ppermute(x, axis, [(i, (i + by) % size) for i in range(size)])  14.6 us
    ppermute x12, waiting for transfers between devices, shifted(): return lax.ppermute(x, axis, [(i, (i + by) % size) for i in range(size)])  12.2 us
    pallas_call x1, Pallas kernels, pack(): pl.pallas_call(pack_kernel, out_shape=[jax.ShapeDtypeStruct((PAYLOAD, 128...  5.77 us
    pallas_call x2, Pallas kernels, vmem_call(): pl.pallas_call(kernel, out_shape=out_shape, in_specs=[vmem] * len(operand...  1.49 us
  transfers between devices with their start and end apart: 12, of which 6 were waited for; matrix products, arithmetic and copies ran while one was open for 0% of the time, Pallas kernels for 10%

profile of v3, /device:TPU:30, one launch (start us, length us, event | category | flops | bytes accessed | tf_op | source)
XLA Modules:
  0.0 57.6 jit_solution(12569893231424057987)
XLA Ops:
  0.6 0.6 %pad_add_fusion.coords = s32[4]{0:T(128)} fusion(s32[1]{0:T(128)} %bitcast.3, s32[1]{0:T(128)} %bitcast.2, s32[1]{0:T(128)} %bitcast.1, s32[1]{0:T(128)} %bitcast), kind=kLoop, calls=%fused_computation | loop fusion | flops 12 | bytes 32 | tf_op jit(solution)/shard_map/stack | solution.py:710
  1.3 0.0 copy-start.1
  1.3 0.0 copy-start.3
  1.3 5.8 %pack.1 = (bf16[336,128]{1,0:T(8,128)(2,1)}, bf16[336,128]{1,0:T(8,128)(2,1)}, bf16[336,128]{1,0:T(8,128)(2,1)}, bf16[336,128]{1,0:T(8,128)(2,1)}, bf16[336,128]...) custom-call(s32[4]{0:T(128)} %pad_add_fusion.coords, s32[8,128]{1,0:T(8,128)} %bitcast.18, ...), custom_call_target="tpu_custom_call" | custom-call | tf_op jit(solution)/shard_map/pack/pallas_call | solution.py:206
  7.0 0.0 collective-permute-start
  7.1 3.3 %collective-permute-start.1 = (bf16[336,128]{1,0:T(8,128)(2,1)}, bf16[336,128]{1,0:T(8,128)(2,1)S(1)}, u32[]{:S(2)}, u32[]{:S(2)}) collective-permute-start(bf16[336,128]{1,0:T(8,128)(2,1)} %get-tuple-element.31), channel_id=1, source_target_pairs={{0,112},{16,0},{32,16},{48,32},{64,48},{80,64},{96,80},{112,96},{1... | collective-permute-start | bytes 258056 | tf_op jit(solution)/shard_map/ppermute | solution.py:699
  10.3 0.6 %collective-permute-start.2 = (bf16[336,128]{1,0:T(8,128)(2,1)}, bf16[336,128]{1,0:T(8,128)(2,1)S(1)}, u32[]{:S(2)}, u32[]{:S(2)}) collective-permute-start(bf16[336,128]{1,0:T(8,128)(2,1)} %get-tuple-element.32), channel_id=1, source_target_pairs={{0,4},{4,8},{8,12},{12,0},{1,5},{5,9},{9,13},{13,1},{2,6},{6,10},{... | collective-permute-start | bytes 258056 | tf_op jit(solution)/shard_map/ppermute | solution.py:699
  11.0 1.4 %collective-permute-start.3 = (bf16[336,128]{1,0:T(8,128)(2,1)}, bf16[336,128]{1,0:T(8,128)(2,1)S(1)}, u32[]{:S(2)}, u32[]{:S(2)}) collective-permute-start(bf16[336,128]{1,0:T(8,128)(2,1)} %get-tuple-element.33), channel_id=1, source_target_pairs={{0,12},{4,0},{8,4},{12,8},{1,13},{5,1},{9,5},{13,9},{2,14},{6,2},{... | collective-permute-start | bytes 258056 | tf_op jit(solution)/shard_map/ppermute | solution.py:699
  12.4 0.3 collective-permute-start.4
  12.7 0.0 copy-done.1
  12.7 0.0 copy-done.3
  12.7 0.0 copy-start.6
  12.7 0.7 %copy-done.6 = s32[8,128]{1,0:T(8,128)S(1)} copy-done((s32[8,128]{1,0:T(8,128)S(1)}, s32[8,128]{1,0:T(8,128)}, u32[]{:S(2)}) %copy-start.6) | copy-done | bytes 4120
  13.4 0.0 copy-start.10
  13.4 0.0 copy-start
  13.4 0.0 copy-start.7
  13.4 1.8 %jacobians.1.jac_in = f32[512,1024]{1,0:T(8,128)S(1)} custom-call(s32[8,128]{1,0:T(8,128)S(1)} %copy-done.6, bf16[1024,512]{1,0:T(8,128)(2,1)S(1)} %copy-done.1, bf16[512,512]{1,0:T(8,128)(2,1)S(1)} %copy-done.3), custom_call_target="tpu_custom_call" | custom-call | flops 2000000000 | bytes 1000000 | tf_op jit(solution)/shard_map/jacobians/pallas_call | solution.py:229
  15.2 0.0 collective-permute-done.a0
  15.2 0.0 copy-done.10
  15.2 1.8 %collective-permute-start.5 = (bf16[336,128]{1,0:T(8,128)(2,1)S(1)}, bf16[336,128]{1,0:T(8,128)(2,1)S(1)}, u32[]{:S(2)}, u32[]{:S(2)}) collective-permute-start(bf16[336,128]{1,0:T(8,128)(2,1)S(1)} %copy-done.10), channel_id=1, source_target_pairs={{0,3},{1,0},{2,1},{3,2},{4,7},{5,4},{6,5},{7,6},{8,11},{9,8},{10,9... | collective-permute-start | bytes 258056 | tf_op jit(solution)/shard_map/ppermute | solution.py:699
  17.0 0.0 copy-done
  17.0 0.0 copy-done.7
  17.0 1.8 %place.1.rows_in = f32[1152,16,128]{2,1,0:T(8,128)S(1)} custom-call(s32[1024]{0:T(1024)S(1)} %bitcast.17, bf16[1024,16,128]{2,1,0:T(8,128)(2,1)S(1)} %bitcast.16), custom_call_target="tpu_custom_call" | custom-call | flops 2000000000 | bytes 1000000 | tf_op jit(solution)/shard_map/place/pallas_call | solution.py:229
  18.8 0.0 copy-start.2
  18.8 0.0 collective-permute-done.1.a1
  18.8 0.0 collective-permute-done.2.a2
  18.8 0.0 collective-permute-done.3.a3
  18.8 0.0 collective-permute-done.4.a4
  18.8 2.1 %collective-permute-done.5.a5 = bf16[336,128]{1,0:T(8,128)(2,1)S(1)} collective-permute-done((bf16[336,128]{1,0:T(8,128)(2,1)S(1)}, bf16[336,128]{1,0:T(8,128)(2,1)S(1)}, u32[]{:S(2)}, u32[]{:S(2)}) %collective-permute-start.5) | collective-permute-done | bytes 86048 | tf_op jit(solution)/shard_map/ppermute | solution.py:699
  21.0 2.7 %arrive.1 = (f32[512,1024]{1,0:T(8,128)S(1)}, f32[1152,16,128]{2,1,0:T(8,128)S(1)}) custom-call(bf16[336,128]{1,0:T(8,128)(2,1)S(1)} %collective-permute-done.a0, bf16[336,128]{1,0:T(8,128)(2,1)S(1)} %collective-permute-done.1.a1, bf16[336,128]{1,0:T(8,128)(2,1)S(1)} %collective-permute-done.2.a2, ...), custom_call_target="tpu_custom_call", output_to_operand_aliasing={{1}: (8, {})} | custom-call | bytes 1000000 | tf_op jit(solution)/shard_map/arrive/pallas_call | solution.py:229
  23.7 0.0 copy-done.2
  23.7 0.0 copy-start.4
  23.7 0.0 copy-start.5
  23.7 3.1 %fields.1 = (bf16[512,1024]{1,0:T(8,128)(2,1)S(1)}, bf16[512,1024]{1,0:T(8,128)(2,1)S(1)}, bf16[512,1024]{1,0:T(8,128)(2,1)S(1)}, bf16[512,1024]{1,0:T(8,128)(2,1)S(1)}) custom-call(f32[18432,128]{1,0:T(8,128)S(1)} %bitcast.14, f32[512,1024]{1,0:T(8,128)S(1)} %get-tuple-element.38.jac_t, bf16[512,512]{1,0:T(8,128)(2,1)S(1)} %copy-done.2), custom_call_target="tpu_custom_call" | custom-call | bytes 1000000 | tf_op jit(solution)/shard_map/fields/pallas_call | solution.py:229
  26.9 0.0 copy-done.4
  26.9 0.0 copy-done.5
  26.9 9.1 %filters.1 = (f32[8448,128]{1,0:T(8,128)S(1)}, f32[1280,128]{1,0:T(8,128)S(1)}, f32[640,128]{1,0:T(8,128)S(1)}, bf16[8,5760]{1,0:T(8,128)(2,1)S(1)}, bf16[8,5760]{1,0:T(8,128)(2,1)S(1)}) custom-call(s32[4]{0:T(128)S(1)} %copy-done.5, bf16[512,1024]{1,0:T(8,128)(2,1)S(1)} %get-tuple-element.39.u0, bf16[512,1024]{1,0:T(8,128)(2,1)S(1)} %get-tuple-element.40.u1, ...), custom_call_target="tpu_custom_call" | custom-call | bytes 1000000 | tf_op jit(solution)/shard_map/filters/pallas_call | solution.py:229
  36.0 0.1 collective-permute-start.6
  36.1 2.0 %collective-permute-start.7 = (bf16[8,5760]{1,0:T(8,128)(2,1)S(1)}, bf16[8,5760]{1,0:T(8,128)(2,1)S(1)}, u32[]{:S(2)}, u32[]{:S(2)}) collective-permute-start(bf16[8,5760]{1,0:T(8,128)(2,1)S(1)} %get-tuple-element.47), channel_id=1, source_target_pairs={{0,3},{1,0},{2,1},{3,2},{4,7},{5,4},{6,5},{7,6},{8,11},{9,8},{10,9... | collective-permute-start | bytes 276488 | tf_op jit(solution)/shard_map/ppermute | solution.py:699
  38.1 0.0 copy-start.8
  38.1 0.0 copy-start.9
  38.1 1.9 %first_y.1 = (f32[3072,128]{1,0:T(8,128)S(1)}, f32[768,128]{1,0:T(8,128)S(1)}) custom-call(s32[4]{0:T(128)S(1)} %copy-done.5, f32[8448,128]{1,0:T(8,128)S(1)} %get-tuple-element.43.ya), custom_call_target="tpu_custom_call" | custom-call | flops 2000000000 | bytes 1000000 | tf_op jit(solution)/shard_map/first_y/pallas_call | solution.py:229
  40.0 0.6 %collective-permute-done.6.zl.from_low = bf16[8,5760]{1,0:T(8,128)(2,1)S(1)} collective-permute-done((bf16[8,5760]{1,0:T(8,128)(2,1)S(1)}, bf16[8,5760]{1,0:T(8,128)(2,1)S(1)}, u32[]{:S(2)}, u32[]{:S(2)}) %collective-permute-start.6) | collective-permute-done | bytes 92192 | tf_op jit(solution)/shard_map/ppermute | solution.py:699
  40.6 1.3 %collective-permute-done.7.zh.from_high = bf16[8,5760]{1,0:T(8,128)(2,1)S(1)} collective-permute-done((bf16[8,5760]{1,0:T(8,128)(2,1)S(1)}, bf16[8,5760]{1,0:T(8,128)(2,1)S(1)}, u32[]{:S(2)}, u32[]{:S(2)}) %collective-permute-start.7) | collective-permute-done | bytes 92192 | tf_op jit(solution)/shard_map/ppermute | solution.py:699
  41.9 0.0 copy-done.8
  41.9 0.0 copy-done.9
  41.9 0.3 y_edges.1
  42.3 1.7 %collective-permute-start.8 = (bf16[224,128]{1,0:T(8,128)(2,1)S(1)}, bf16[224,128]{1,0:T(8,128)(2,1)S(1)}, u32[]{:S(2)}, u32[]{:S(2)}) collective-permute-start(bf16[224,128]{1,0:T(8,128)(2,1)S(1)} %get-tuple-element.52), channel_id=1, source_target_pairs={{0,4},{4,8},{8,12},{12,0},{1,5},{5,9},{9,13},{13,1},{2,6},{6,10},{... | collective-permute-start | bytes 172040 | tf_op jit(solution)/shard_map/ppermute | solution.py:699
  43.9 0.4 collective-permute-start.9
  44.3 0.5 z_main.1
  44.9 1.6 %collective-permute-done.8.yl = bf16[224,128]{1,0:T(8,128)(2,1)S(1)} collective-permute-done((bf16[224,128]{1,0:T(8,128)(2,1)S(1)}, bf16[224,128]{1,0:T(8,128)(2,1)S(1)}, u32[]{:S(2)}, u32[]{:S(2)}) %collective-permute-start.8) | collective-permute-done | bytes 57376 | tf_op jit(solution)/shard_map/ppermute | solution.py:699
  46.5 2.8 %collective-permute-done.9.yh = bf16[224,128]{1,0:T(8,128)(2,1)S(1)} collective-permute-done((bf16[224,128]{1,0:T(8,128)(2,1)S(1)}, bf16[224,128]{1,0:T(8,128)(2,1)S(1)}, u32[]{:S(2)}, u32[]{:S(2)}) %collective-permute-start.9) | collective-permute-done | bytes 57376 | tf_op jit(solution)/shard_map/ppermute | solution.py:699
  49.3 0.5 x_edges.1
  49.8 0.0 collective-permute-start.10
  49.8 2.9 %collective-permute-start.11 = (bf16[896,128]{1,0:T(8,128)(2,1)S(1)}, bf16[896,128]{1,0:T(8,128)(2,1)S(1)}, u32[]{:S(2)}, u32[]{:S(2)}) collective-permute-start(bf16[896,128]{1,0:T(8,128)(2,1)S(1)} %get-tuple-element.57), channel_id=1, source_target_pairs={{0,112},{16,0},{32,16},{48,32},{64,48},{80,64},{96,80},{112,96},{1... | collective-permute-start | bytes 688136 | tf_op jit(solution)/shard_map/ppermute | solution.py:699
  52.8 3.7 %collective-permute-done.10.xl = bf16[896,128]{1,0:T(8,128)(2,1)S(1)} collective-permute-done((bf16[896,128]{1,0:T(8,128)(2,1)S(1)}, bf16[896,128]{1,0:T(8,128)(2,1)S(1)}, u32[]{:S(2)}, u32[]{:S(2)}) %collective-permute-start.10) | collective-permute-done | bytes 229408 | tf_op jit(solution)/shard_map/ppermute | solution.py:699
  56.5 0.0 collective-permute-done.11.xh
  56.5 1.1 %final.1 = (f32[4,8,64,128]{3,2,1,0:T(8,128)}, f32[4,4,32,64]{3,2,1,0:T(8,128)}) custom-call(f32[3072,128]{1,0:T(8,128)S(1)} %get-tuple-element.54.sa, f32[1280,128]{1,0:T(8,128)S(1)} %get-tuple-element.55.sc, bf16[896,128]{1,0:T(8,128)(2,1)S(1)} %collective-permute-done.10.xl, bf16[896,128]{1,0:T(8,128)(2,1)S(1)} %collective-permute-done.11.xh), custom_call_target="tpu_custom_call" | custom-call | tf_op jit(solution)/shard_map/final/pallas_call | solution.py:634
Async XLA Ops:
  1.3 11.4 %copy-start.1 = (bf16[1024,512]{1,0:T(8,128)(2,1)S(1)}, bf16[1024,512]{1,0:T(8,128)(2,1)}, u32[]{:S(2)}) copy-start(bf16[1024,512]{1,0:T(8,128)(2,1)} %jac.1) | copy-start | bytes 3145732
  1.3 11.4 %copy-start.3 = (bf16[512,512]{1,0:T(8,128)(2,1)S(1)}, bf16[512,512]{1,0:T(8,128)(2,1)}, u32[]{:S(2)}) copy-start(bf16[512,512]{1,0:T(8,128)(2,1)} %constant.25.clone.order) | copy-start | bytes 1572868
  7.0 8.2 %collective-permute-start = (bf16[336,128]{1,0:T(8,128)(2,1)}, bf16[336,128]{1,0:T(8,128)(2,1)S(1)}, u32[]{:S(2)}, u32[]{:S(2)}) collective-permute-start(bf16[336,128]{1,0:T(8,128)(2,1)} %get-tuple-element.30), channel_id=1, source_target_pairs={{0,16},{16,32},{32,48},{48,64},{64,80},{80,96},{96,112},{112,0},{1... | collective-permute-start | bytes 258056 | tf_op jit(solution)/shard_map/ppermute | solution.py:699
  7.1 11.7 %collective-permute-start.1 = (bf16[336,128]{1,0:T(8,128)(2,1)}, bf16[336,128]{1,0:T(8,128)(2,1)S(1)}, u32[]{:S(2)}, u32[]{:S(2)}) collective-permute-start(bf16[336,128]{1,0:T(8,128)(2,1)} %get-tuple-element.31), channel_id=1, source_target_pairs={{0,112},{16,0},{32,16},{48,32},{64,48},{80,64},{96,80},{112,96},{1... | collective-permute-start | bytes 258056 | tf_op jit(solution)/shard_map/ppermute | solution.py:699
  10.3 8.5 %collective-permute-start.2 = (bf16[336,128]{1,0:T(8,128)(2,1)}, bf16[336,128]{1,0:T(8,128)(2,1)S(1)}, u32[]{:S(2)}, u32[]{:S(2)}) collective-permute-start(bf16[336,128]{1,0:T(8,128)(2,1)} %get-tuple-element.32), channel_id=1, source_target_pairs={{0,4},{4,8},{8,12},{12,0},{1,5},{5,9},{9,13},{13,1},{2,6},{6,10},{... | collective-permute-start | bytes 258056 | tf_op jit(solution)/shard_map/ppermute | solution.py:699
  11.0 7.8 %collective-permute-start.3 = (bf16[336,128]{1,0:T(8,128)(2,1)}, bf16[336,128]{1,0:T(8,128)(2,1)S(1)}, u32[]{:S(2)}, u32[]{:S(2)}) collective-permute-start(bf16[336,128]{1,0:T(8,128)(2,1)} %get-tuple-element.33), channel_id=1, source_target_pairs={{0,12},{4,0},{8,4},{12,8},{1,13},{5,1},{9,5},{13,9},{2,14},{6,2},{... | collective-permute-start | bytes 258056 | tf_op jit(solution)/shard_map/ppermute | solution.py:699
  12.4 6.5 %collective-permute-start.4 = (bf16[336,128]{1,0:T(8,128)(2,1)}, bf16[336,128]{1,0:T(8,128)(2,1)S(1)}, u32[]{:S(2)}, u32[]{:S(2)}) collective-permute-start(bf16[336,128]{1,0:T(8,128)(2,1)} %get-tuple-element.34), channel_id=1, source_target_pairs={{0,1},{1,2},{2,3},{3,0},{4,5},{5,6},{6,7},{7,4},{8,9},{9,10},{10,1... | collective-permute-start | bytes 258056 | tf_op jit(solution)/shard_map/ppermute | solution.py:699
  12.7 0.7 %copy-start.6 = (s32[8,128]{1,0:T(8,128)S(1)}, s32[8,128]{1,0:T(8,128)}, u32[]{:S(2)}) copy-start(s32[8,128]{1,0:T(8,128)} %get-tuple-element.36.spots) | copy-start | bytes 12292
  13.4 1.8 %copy-start.10 = (bf16[336,128]{1,0:T(8,128)(2,1)S(1)}, bf16[336,128]{1,0:T(8,128)(2,1)}, u32[]{:S(2)}) copy-start(bf16[336,128]{1,0:T(8,128)(2,1)} %get-tuple-element.35) | copy-start | bytes 258052
  13.4 3.6 %copy-start = (bf16[1024,4,512]{2,1,0:T(4,128)(2,1)S(1)}, bf16[1024,4,512]{2,1,0:T(4,128)(2,1)}, u32[]{:S(2)}) copy-start(bf16[1024,4,512]{2,1,0:T(4,128)(2,1)} %param.9) | copy-start | bytes 12582916
  13.4 3.6 %copy-start.7 = (s32[8,128]{1,0:T(8,128)S(1)}, s32[8,128]{1,0:T(8,128)}, u32[]{:S(2)}) copy-start(s32[8,128]{1,0:T(8,128)} %get-tuple-element.36.spots) | copy-start | bytes 12292
  15.2 5.8 %collective-permute-start.5 = (bf16[336,128]{1,0:T(8,128)(2,1)S(1)}, bf16[336,128]{1,0:T(8,128)(2,1)S(1)}, u32[]{:S(2)}, u32[]{:S(2)}) collective-permute-start(bf16[336,128]{1,0:T(8,128)(2,1)S(1)} %copy-done.10), channel_id=1, source_target_pairs={{0,3},{1,0},{2,1},{3,2},{4,7},{5,4},{6,5},{7,6},{8,11},{9,8},{10,9... | collective-permute-start | bytes 258056 | tf_op jit(solution)/shard_map/ppermute | solution.py:699
  18.8 4.9 %copy-start.2 = (bf16[512,512]{1,0:T(8,128)(2,1)S(1)}, bf16[512,512]{1,0:T(8,128)(2,1)}, u32[]{:S(2)}) copy-start(bf16[512,512]{1,0:T(8,128)(2,1)} %constant.26.clone.table) | copy-start | bytes 1572868
  23.7 3.2 %copy-start.4 = (bf16[3,256,256]{2,1,0:T(8,128)(2,1)S(1)}, bf16[3,256,256]{2,1,0:T(8,128)(2,1)}, u32[]{:S(2)}) copy-start(bf16[3,256,256]{2,1,0:T(8,128)(2,1)} %constant.27.clone.depths) | copy-start | bytes 1179652
  23.7 3.2 %copy-start.5 = (s32[4]{0:T(128)S(1)}, s32[4]{0:T(128)}, u32[]{:S(2)}) copy-start(s32[4]{0:T(128)} %pad_add_fusion.coords) | copy-start | bytes 52
  36.0 4.6 %collective-permute-start.6 = (bf16[8,5760]{1,0:T(8,128)(2,1)S(1)}, bf16[8,5760]{1,0:T(8,128)(2,1)S(1)}, u32[]{:S(2)}, u32[]{:S(2)}) collective-permute-start(bf16[8,5760]{1,0:T(8,128)(2,1)S(1)} %get-tuple-element.46), channel_id=1, source_target_pairs={{0,1},{1,2},{2,3},{3,0},{4,5},{5,6},{6,7},{7,4},{8,9},{9,10},{10,1... | collective-permute-start | bytes 276488 | tf_op jit(solution)/shard_map/ppermute | solution.py:699
  36.1 5.8 %collective-permute-start.7 = (bf16[8,5760]{1,0:T(8,128)(2,1)S(1)}, bf16[8,5760]{1,0:T(8,128)(2,1)S(1)}, u32[]{:S(2)}, u32[]{:S(2)}) collective-permute-start(bf16[8,5760]{1,0:T(8,128)(2,1)S(1)} %get-tuple-element.47), channel_id=1, source_target_pairs={{0,3},{1,0},{2,1},{3,2},{4,7},{5,4},{6,5},{7,6},{8,11},{9,8},{10,9... | collective-permute-start | bytes 276488 | tf_op jit(solution)/shard_map/ppermute | solution.py:699
  38.1 3.8 %copy-start.8 = (bf16[16,128]{1,0:T(8,128)(2,1)S(1)}, bf16[16,128]{1,0:T(8,128)(2,1)}, u32[]{:S(2)}) copy-start(bf16[16,128]{1,0:T(8,128)(2,1)} %constant.29.clone.spread_c) | copy-start | bytes 12292
  38.1 3.8 %copy-start.9 = (bf16[16,128]{1,0:T(8,128)(2,1)S(1)}, bf16[16,128]{1,0:T(8,128)(2,1)}, u32[]{:S(2)}) copy-start(bf16[16,128]{1,0:T(8,128)(2,1)} %constant.28.clone.spread_a) | copy-start | bytes 12292
  42.3 4.2 %collective-permute-start.8 = (bf16[224,128]{1,0:T(8,128)(2,1)S(1)}, bf16[224,128]{1,0:T(8,128)(2,1)S(1)}, u32[]{:S(2)}, u32[]{:S(2)}) collective-permute-start(bf16[224,128]{1,0:T(8,128)(2,1)S(1)} %get-tuple-element.52), channel_id=1, source_target_pairs={{0,4},{4,8},{8,12},{12,0},{1,5},{5,9},{9,13},{13,1},{2,6},{6,10},{... | collective-permute-start | bytes 172040 | tf_op jit(solution)/shard_map/ppermute | solution.py:699
  43.9 5.4 %collective-permute-start.9 = (bf16[224,128]{1,0:T(8,128)(2,1)S(1)}, bf16[224,128]{1,0:T(8,128)(2,1)S(1)}, u32[]{:S(2)}, u32[]{:S(2)}) collective-permute-start(bf16[224,128]{1,0:T(8,128)(2,1)S(1)} %get-tuple-element.53), channel_id=1, source_target_pairs={{0,12},{4,0},{8,4},{12,8},{1,13},{5,1},{9,5},{13,9},{2,14},{6,2},{... | collective-permute-start | bytes 172040 | tf_op jit(solution)/shard_map/ppermute | solution.py:699
  49.8 6.7 %collective-permute-start.10 = (bf16[896,128]{1,0:T(8,128)(2,1)S(1)}, bf16[896,128]{1,0:T(8,128)(2,1)S(1)}, u32[]{:S(2)}, u32[]{:S(2)}) collective-permute-start(bf16[896,128]{1,0:T(8,128)(2,1)S(1)} %get-tuple-element.56), channel_id=1, source_target_pairs={{0,16},{16,32},{32,48},{48,64},{64,80},{80,96},{96,112},{112,0},{1... | collective-permute-start | bytes 688136 | tf_op jit(solution)/shard_map/ppermute | solution.py:699
  49.8 6.6 %collective-permute-start.11 = (bf16[896,128]{1,0:T(8,128)(2,1)S(1)}, bf16[896,128]{1,0:T(8,128)(2,1)S(1)}, u32[]{:S(2)}, u32[]{:S(2)}) collective-permute-start(bf16[896,128]{1,0:T(8,128)(2,1)S(1)} %get-tuple-element.57), channel_id=1, source_target_pairs={{0,112},{16,0},{32,16},{48,32},{64,48},{80,64},{96,80},{112,96},{1... | collective-permute-start | bytes 688136 | tf_op jit(solution)/shard_map/ppermute | solution.py:699

commit v4 on v3

--- a/solution.py
+++ b/solution.py
@@ -122,12 +122,17 @@
     return lax.dot_general(a, b, (((0,), (0,)), ((), ())), preferred_element_type=F32)
 
 
-def pack_kernel(coords, home, jac_hbm, fields, *rest):
+def brick_place():
+    return tuple(lax.axis_index(axis) for axis in ("gx", "gy", "gz"))
+
+
+def pack_kernel(home, jac_hbm, fields, *rest):
     outs = rest[:6]
     spots, picker, jac, index_v, index_s, sem_jac, sem_index, sem_rows = rest[6:]
     copy_jac = pltpu.make_async_copy(jac_hbm, jac, sem_jac)
     copy_jac.start()
-    me = coords[3]
+    ix, iy, iz = brick_place()
+    me = (ix * 4 + iy) * 4 + iz
     slots = home[...]
     diff = (slots >> 10) - me
     tag = (slots & 1023) + 1
@@ -200,14 +205,14 @@
         ).wait()
 
 
-def pack(coords, home, jac, fields_rows):
+def pack(home, jac, fields_rows):
     vmem = pl.BlockSpec(memory_space=pltpu.VMEM)
     hbm = pl.BlockSpec(memory_space=pltpu.HBM)
     return pl.pallas_call(
         pack_kernel,
         out_shape=[jax.ShapeDtypeStruct((PAYLOAD, 128), BF16)] * 6
         + [jax.ShapeDtypeStruct((8, 128), jnp.int32)],
-        in_specs=[pl.BlockSpec(memory_space=pltpu.SMEM), vmem, hbm, hbm],
+        in_specs=[vmem, hbm, hbm],
         out_specs=[vmem] * 7,
         scratch_shapes=[
             pltpu.VMEM((128, 1024), BF16),
@@ -220,7 +225,7 @@
         ],
         compiler_params=pltpu.CompilerParams(vmem_limit_bytes=60 * MIB),
         name="pack",
-    )(coords, home, jac, fields_rows)
+    )(home, jac, fields_rows)
 
 
 def local_call(kernel, outs, specs, operands, name, out_specs=None, scratch=(),
@@ -241,7 +246,7 @@
     )(*operands)
 
 
-def jacobian_kernel(spots, jac, order, jac_t):
+def jacobian_kernel(spots, jac, order, first_arrived, jac_t):
     ordered = nt(order[...], jac[...]).astype(BF16)
     for c in range(4):
         ids = lax.broadcasted_iota(jnp.int32, (256, 128), 0) + c * 256
@@ -257,7 +262,7 @@
         jac_t[:, c * 256 : c * 256 + 256] = nt(ordered, hit)
 
 
-def place_kernel(spots, fields, rows):
+def place_kernel(spots, fields, _, rows):
     def place(e, carry):
         targets = [spots[e * 32 + u] for u in range(32)]
         values = [fields[e * 32 + u] for u in range(32)]
@@ -268,15 +273,14 @@
     lax.fori_loop(0, 32, place, 0)
 
 
-def arrive_kernel(a0, a1, a2, a3, a4, a5, order, jac_in, rows_in, jac_t, rows,
-                  staged, spot_v, spot_s, sem, sem_rows):
+def brick_kernel(a0, a1, a2, a3, a4, a5, order, table, jac_in, rows, u0, u1, u2, u3, _,
+                 jac_t, spot_v, spot_s, sem):
     arrays = (a0, a1, a2, a3, a4, a5)
     tags = jnp.zeros((8, 128), F32)
     for d in range(6):
         tags = tags + arrays[d][320:336, :].astype(F32)[0:8]
     spot = (tags[0:1] * 32.0 + tags[1:2]).astype(jnp.int32) - 1
-    spare = lax.broadcasted_iota(jnp.int32, (1, 128), 1) + 1024
-    spot_v[...] = jnp.broadcast_to(jnp.where(spot < 0, spare, spot), (8, 128))
+    spot_v[...] = jnp.broadcast_to(jnp.where(spot < 0, 1024, spot), (8, 128))
     copy = pltpu.make_async_copy(spot_v, spot_s, sem)
     copy.start()
     jac = jnp.concatenate(
@@ -294,20 +298,15 @@
         ids = lax.broadcasted_iota(jnp.int32, (256, 128), 0) + c * 256
         hit = jnp.where(ids == jnp.broadcast_to(spot, (256, 128)), 1.0, 0.0).astype(BF16)
         jac_t[:, c * 256 : c * 256 + 256] = jac_in[:, c * 256 : c * 256 + 256] + nt(ordered, hit)
+    copy.wait()
     for d in range(6):
         for e in range(16):
-            staged[d * 16 + e] = arrays[d][e * 16 : e * 16 + 16, :].astype(F32)
-    copy.wait()
-    for e in range(96):
-        pltpu.make_async_copy(staged.at[e], rows.at[spot_s[0, e]], sem_rows).start()
-    pltpu.make_async_copy(staged, rows.at[pl.ds(0, 96)], sem_rows).wait()
-
-
-def fields_kernel(rows, jac_t, table, u0, u1, u2, u3):
+            rows[spot_s[0, d * 16 + e]] = arrays[d][e * 16 : e * 16 + 16, :].astype(F32)
+    flat = rows.reshape(1040 * 16, 128)
     for f, out in enumerate((u0, u1, u2, u3)):
         for n in range(4):
             pieces = [
-                rows[pl.ds(n * 4096 + c * 4 + f, 256, stride=16), :].astype(BF16)
+                flat[pl.ds(n * 4096 + c * 4 + f, 256, stride=16), :].astype(BF16)
                 for c in range(4)
             ]
             values = nt(table[...], jnp.concatenate(pieces, axis=1))
@@ -316,23 +315,23 @@
             ).astype(BF16)
 
 
-def own_elements(spots, fields_elems, jac):
+def own_elements(spots, fields_elems, jac, first_arrived):
     vmem = pl.BlockSpec(memory_space=pltpu.VMEM)
     smem = pl.BlockSpec(memory_space=pltpu.SMEM)
     order = jnp.asarray(point_order())
     [jac_t] = local_call(
         jacobian_kernel,
         [jax.ShapeDtypeStruct((512, 1024), F32)],
-        [vmem] * 3,
-        [spots, jac, order],
+        [vmem] * 3 + [pl.BlockSpec(memory_space=pl.ANY)],
+        [spots, jac, order, first_arrived],
         "jacobians",
         flops=2_000_000_000,
     )
     [rows] = local_call(
         place_kernel,
-        [jax.ShapeDtypeStruct((1152, 16, 128), F32)],
-        [smem, vmem],
-        [spots.reshape(1024), fields_elems],
+        [jax.ShapeDtypeStruct((1040, 16, 128), F32)],
+        [smem, vmem, pl.BlockSpec(memory_space=pl.ANY)],
+        [spots.reshape(1024), fields_elems, jac_t],
         "place",
         flops=2_000_000_000,
     )
@@ -341,34 +340,22 @@
 
 def all_elements(rows, jac_t, arrived):
     vmem = pl.BlockSpec(memory_space=pltpu.VMEM)
-    anywhere = pl.BlockSpec(memory_space=pl.ANY)
-    jac_t, rows = local_call(
-        arrive_kernel,
-        [
-            jax.ShapeDtypeStruct((512, 1024), F32),
-            jax.ShapeDtypeStruct((1152, 16, 128), F32),
-        ],
-        [vmem] * 8 + [anywhere],
-        [*arrived, jnp.asarray(point_order()), jac_t, rows],
-        "arrive",
-        out_specs=[vmem, anywhere],
+    return local_call(
+        brick_kernel,
+        [jax.ShapeDtypeStruct((512, 1024), BF16)] * 4
+        + [jax.ShapeDtypeStruct((1040, 16, 128), F32)],
+        [vmem] * 10,
+        [*arrived, jnp.asarray(point_order()), jnp.asarray(interp_table()), jac_t, rows],
+        "brick",
         scratch=[
-            pltpu.VMEM((96, 16, 128), F32),
+            pltpu.VMEM((512, 1024), F32),
             pltpu.VMEM((8, 128), jnp.int32),
             pltpu.SMEM((8, 128), jnp.int32),
             pltpu.SemaphoreType.DMA,
-            pltpu.SemaphoreType.DMA,
         ],
-        aliases={8: 1},
-    )
-    return local_call(
-        fields_kernel,
-        [jax.ShapeDtypeStruct((512, 1024), BF16)] * 4,
-        [vmem] * 3,
-        [rows.reshape(1152 * 16, 128), jac_t, jnp.asarray(interp_table())],
-        "fields",
-        limit=24,
-    )
+        aliases={9: 4},
+        limit=36,
+    )[:4]
 
 
 def halve(values, outputs, shift):
@@ -401,9 +388,50 @@
     return low, total[8 : count - 8], high
 
 
-def first_y_kernel(coords, ya, main_a, edge_a):
-    y_low = jnp.where(coords[1] > 0, 1.0, 0.0)
-    y_high = jnp.where(coords[1] < 3, 1.0, 0.0)
+def inner_sides():
+    ix, iy, _ = brick_place()
+    return tuple(jnp.where(flag, 1.0, 0.0) for flag in (ix > 0, ix < 7, iy > 0, iy < 3))
+
+
+def clear_pads(ref, count, size, width):
+    def pads(q, carry):
+        zero = jnp.zeros((width, 128), F32)
+        base = pl.multiple_of(q * size, 8)
+        ref[pl.ds(base, width), :] = zero
+        ref[pl.ds(base + size - width, width), :] = zero
+        return carry
+
+    lax.fori_loop(0, count, pads, 0)
+
+
+def along_x(values, outputs, edge, x_low, x_high):
+    results = halve(values, outputs, 7)
+    return [
+        r * x_low if o < edge else r * x_high if o >= outputs - edge else r
+        for o, r in enumerate(results)
+    ]
+
+
+def first_x(wide, base, f, e, t, ref, x_low, x_high):
+    values = [
+        wide[pl.ds(pl.multiple_of(base + e * 128 + x * 8, 8), 8), :] for x in range(16)
+    ]
+    for o, value in enumerate(along_x(values, 12, 2, x_low, x_high)):
+        at = (f * 12 + o) * 176 + 24 + e * 8 + t * 32
+        ref[pl.ds(pl.multiple_of(at, 8), 8), :] = value
+
+
+def first_a_kernel(wide, main_a, edge_a, ya):
+    x_low, x_high, y_low, y_high = inner_sides()
+    clear_pads(ya, 48, 176, 24)
+
+    def quarter(t, carry):
+        for f in range(4):
+            for e in range(4):
+                first_x(wide, t * 2048 + f * 512, f, e, t, ya, x_low, x_high)
+        return carry
+
+    lax.fori_loop(0, 4, quarter, 0)
 
     def first(q, carry):
         low, middle, high = along_y(ya, q * 176, 80, y_low, y_high)
@@ -415,39 +443,15 @@
     lax.fori_loop(0, 48, first, 0)
 
 
-def filter_kernel(
-    coords, u0, u1, u2, u3, depths,
-    ya, main_c, edge_c, to_low, to_high,
-    depth, wide, yb, mb, yc, pbz, pcz, sem,
-):
-    one = lambda flag: jnp.where(flag, 1.0, 0.0)
-    x_low = one(coords[0] > 0)
-    x_high = one(coords[0] < 7)
-    y_low = one(coords[1] > 0)
-    y_high = one(coords[1] < 3)
-
-    spot_z = coords[2]
-    place = jnp.where(spot_z == 0, 0, jnp.where(spot_z == 3, 2, 1))
+def filter_kernel(u0, u1, u2, u3, depths, wide_a, main_c, edge_c, to_low, to_high,
+                  depth, wide_b, yb, mb, yc, pbz, pcz, sem):
+    x_low, x_high, y_low, y_high = inner_sides()
+    _, _, iz = brick_place()
+    place = jnp.where(iz == 0, 0, jnp.where(iz == 3, 2, 1))
     copy = pltpu.make_async_copy(depths.at[place], depth, sem)
     copy.start()
-    def pads(q, carry):
-        zero = jnp.zeros((24, 128), F32)
-        base = pl.multiple_of(q * 176, 8)
-        for ref in (ya, yb):
-            ref[pl.ds(base, 24), :] = zero
-            ref[pl.ds(base + 152, 24), :] = zero
-        return carry
-
-    lax.fori_loop(0, 48, pads, 0)
-
-    def more_pads(q, carry):
-        zero = jnp.zeros((16, 128), F32)
-        base = pl.multiple_of(q * 112, 8)
-        yc[pl.ds(base, 16), :] = zero
-        yc[pl.ds(base + 96, 16), :] = zero
-        return carry
-
-    lax.fori_loop(0, 40, more_pads, 0)
+    clear_pads(yb, 48, 176, 24)
+    clear_pads(yc, 40, 112, 16)
     copy.wait()
 
     def quarter(t, carry):
@@ -479,29 +483,12 @@
                         jnp.concatenate([regrouped[0][e], regrouped[1][e]], axis=1)
                     )
             operand = jnp.concatenate([p for e in range(4) for p in pieces[e]], axis=0)
-            wide[f * 512 : f * 512 + 512, :] = nn(operand, depth[...])
-
+            both = nn(operand, depth[...])
+            wide_a[pl.ds(pl.multiple_of(t * 2048 + f * 512, 512), 512), :] = both[:, 0:128]
+            wide_b[f * 512 : f * 512 + 512, :] = both[:, 128:256]
         for f in range(4):
-            for column in range(8):
-                ref = (ya, yb)[column % 2]
-                values = [
-                    wide[
-                        f * 512 + (column // 2) * 128 + ex * 64 + i * 8 : f * 512
-                        + (column // 2) * 128 + ex * 64 + i * 8 + 8,
-                        (column % 2) * 128 : (column % 2) * 128 + 128,
-                    ]
-                    for ex in range(2)
-                    for i in range(8)
-                ]
-                results = halve(values, 12, 7)
-                for o in range(12):
-                    value = results[o]
-                    if o < 2:
-                        value = value * x_low
-                    if o >= 10:
-                        value = value * x_high
-                    at = (f * 12 + o) * 176 + 24 + (column // 2) * 8 + t * 32
-                    ref[pl.ds(pl.multiple_of(at, 8), 8), :] = value
+            for e in range(4):
+                first_x(wide_b, f * 512, f, e, t, yb, x_low, x_high)
         return carry
 
     lax.fori_loop(0, 4, quarter, 0)
@@ -520,24 +507,17 @@
 
     lax.fori_loop(0, 48, first, 0)
 
-    def along_x(v, carry):
+    def second_x(v, carry):
         for f in range(4):
             values = [
-                mb[pl.ds(pl.multiple_of((f * 12 + o) * 80 + v * 8, 8), 8), :]
-                for o in range(12)
+                mb[pl.ds(pl.multiple_of((f * 12 + o) * 80 + v * 8, 8), 8), :] for o in range(12)
             ]
-            results = halve(values, 10, 7)
-            for o in range(10):
-                value = results[o]
-                if o < 3:
-                    value = value * x_low
-                if o >= 7:
-                    value = value * x_high
+            for o, value in enumerate(along_x(values, 10, 3, x_low, x_high)):
                 at = (f * 10 + o) * 112 + 16 + v * 8
                 yc[pl.ds(pl.multiple_of(at, 8), 8), :] = value
         return carry
 
-    lax.fori_loop(0, 10, along_x, 0)
+    lax.fori_loop(0, 10, second_x, 0)
 
     def second(q, carry):
         low, middle, high = along_y(yc, q * 112, 48, y_low, y_high)
@@ -562,28 +542,27 @@
     mid = nt(pick(2, 64, 66), pbz[...])
     coarse = nt(pick(3, 68, 71), pcz[...])
     for ref, at in ((to_low, 0), (to_high, 8)):
-        ref[:, 0:3840] = mid[at : at + 8].astype(BF16)
-        ref[:, 3840:5760] = coarse[at : at + 8].astype(BF16)
-
-
-def filters(coords, uniform_t):
+        ref[:, 0:3840] = mid[at : at + 4].astype(BF16)
+        ref[:, 3840:5760] = coarse[at : at + 4].astype(BF16)
+
+
+def filters(uniform_t):
     vmem = pl.BlockSpec(memory_space=pltpu.VMEM)
-    smem = pl.BlockSpec(memory_space=pltpu.SMEM)
     return local_call(
         filter_kernel,
         [
-            jax.ShapeDtypeStruct((48 * 176, 128), F32),
+            jax.ShapeDtypeStruct((8192, 128), F32),
             jax.ShapeDtypeStruct((40 * 32, 128), F32),
             jax.ShapeDtypeStruct((40 * 16, 128), F32),
-            jax.ShapeDtypeStruct((8, 5760), BF16),
-            jax.ShapeDtypeStruct((8, 5760), BF16),
+            jax.ShapeDtypeStruct((4, 5760), BF16),
+            jax.ShapeDtypeStruct((4, 5760), BF16),
         ],
-        [smem] + [vmem] * 4 + [pl.BlockSpec(memory_space=pltpu.HBM)],
-        [coords, *uniform_t, jnp.asarray(depth_tables())],
+        [vmem] * 4 + [pl.BlockSpec(memory_space=pltpu.HBM)],
+        [*uniform_t, jnp.asarray(depth_tables())],
         "filters",
         scratch=[
             pltpu.VMEM((256, 256), BF16),
-            pltpu.VMEM((2048, 256), F32),
+            pltpu.VMEM((2048, 128), F32),
             pltpu.VMEM((48 * 176, 128), F32),
             pltpu.VMEM((48 * 80, 128), F32),
             pltpu.VMEM((40 * 112, 128), F32),
@@ -595,23 +574,23 @@
     )
 
 
-def first_y(coords, ya):
-    vmem = pl.BlockSpec(memory_space=pltpu.VMEM)
+def first_a(wide):
     return local_call(
-        first_y_kernel,
+        first_a_kernel,
         [jax.ShapeDtypeStruct((48 * 64, 128), F32), jax.ShapeDtypeStruct((48 * 16, 128), F32)],
-        [pl.BlockSpec(memory_space=pltpu.SMEM), vmem],
-        [coords, ya],
-        "first_y",
-        flops=2_000_000_000,
+        [pl.BlockSpec(memory_space=pltpu.VMEM)],
+        [wide],
+        "first_a",
+        scratch=[pltpu.VMEM((48 * 176, 128), F32)],
+        flops=3_000_000_000,
     )
 
 
 def depth_spread(first_lane_high, count):
-    table = np.zeros((16, 128))
+    table = np.zeros((8, 128))
     for r in range(count):
         table[r, r] = 1.0
-        table[8 + r, first_lane_high + r] = 1.0
+        table[4 + r, first_lane_high + r] = 1.0
     return bf16_of(table)
 
 
@@ -666,32 +645,58 @@
             ref[f * 128 : f * 128 + 128, :] = sa[
                 (f * 12 + xa) * 64 : (f * 12 + xa) * 64 + 128, :
             ].astype(BF16)
-            ref[512 + f * 96 : 608 + f * 96, :] = sc[
-                (f * 10 + xc) * 32 : (f * 10 + xc) * 32 + 96, :
-            ].astype(BF16)
-
-
-def final_kernel(sa, sc, xl, xh, mid, coarse):
+        for pair in range(2):
+            left, right = (
+                sc[(f * 10 + xc) * 32 : (f * 10 + xc) * 32 + 96, :]
+                for f in (2 * pair, 2 * pair + 1)
+            )
+            lane = lax.broadcasted_iota(jnp.int32, (96, 128), 1)
+            ref[512 + pair * 96 : 608 + pair * 96, :] = jnp.where(
+                lane < 64, left, pltpu.roll(right, 64, 1)
+            ).astype(BF16)
+
+
+def inside_kernel(sa, mid, sems):
+    copies = [
+        pltpu.make_async_copy(
+            sa.at[pl.ds(f * 12 + 4, 4)], mid.at[f].at[pl.ds(2, 4)], sems.at[f]
+        )
+        for f in range(4)
+    ]
+    for copy in copies:
+        copy.start()
+    for copy in copies:
+        copy.wait()
+
+
+def final_kernel(sa, sc, xl, xh, _, coarse, mid, planes, sems):
+    copies = []
+    for side, ref in enumerate((xl, xh)):
+        for f in range(4):
+            for x in range(2):
+                plane = f * 12 + 2 + side * 6 + x
+                at = f * 128 + x * 64
+                planes[side * 4 + f, x] = sa[plane] + ref[at : at + 64, :].astype(F32)
+            copy = pltpu.make_async_copy(
+                planes.at[side * 4 + f],
+                mid.at[f].at[pl.ds(side * 6, 2)],
+                sems.at[side * 4 + f],
+            )
+            copy.start()
+            copies.append(copy)
     for f in range(4):
-        for x in range(8):
-            base = (f * 12 + x + 2) * 64
-            value = sa[base : base + 64, :]
-            if x < 2:
-                value = value + xl[f * 128 + x * 64 : f * 128 + x * 64 + 64, :].astype(F32)
-            if x >= 6:
-                at = f * 128 + (x - 6) * 64
-                value = value + xh[at : at + 64, :].astype(F32)
-            mid[f, x] = value
+        half = f % 2 * 64
         for x in range(4):
             base = (f * 10 + x + 3) * 32
-            value = sc[base : base + 32, :]
+            value = sc[base : base + 32, :][:, 0:64]
+            start = 512 + f // 2 * 96 + x * 32
             if x < 3:
-                at = 512 + f * 96 + x * 32
-                value = value + xl[at : at + 32, :].astype(F32)
+                value = value + xl[start : start + 32, :].astype(F32)[:, half : half + 64]
             if x >= 1:
-                at = 512 + f * 96 + (x - 1) * 32
-                value = value + xh[at : at + 32, :].astype(F32)
-            coarse[f, x] = value[:, 0:64]
+                value = value + xh[start - 32 : start, :].astype(F32)[:, half : half + 64]
+            coarse[f, x] = value
+    for copy in copies:
+        copy.wait()
 
 
 def shifted(x, axis, by):
@@ -705,18 +710,15 @@
 
 
 def body(fields, jacobian, home_slot):
-    ix, iy, iz = (lax.axis_index(axis) for axis in ("gx", "gy", "gz"))
-    me = (ix * lax.axis_size("gy") + iy) * lax.axis_size("gz") + iz
-    coords = jnp.stack([ix, iy, iz, me]).astype(jnp.int32)
     fields_rows, fields_elems, home_tile = local_views(fields, home_slot)
-    *payloads, spots = pack(coords, home_tile, jacobian, fields_rows)
+    *payloads, spots = pack(home_tile, jacobian, fields_rows)
     arrived = [shifted(p, *move) for p, move in zip(payloads, SHIFTS)]
-    rows, jac_t = own_elements(spots, fields_elems, jacobian)
+    rows, jac_t = own_elements(spots, fields_elems, jacobian, arrived[0])
     uniform_t = all_elements(rows, jac_t, arrived)
-    ya, main_c, edge_c, z_low, z_high = filters(coords, uniform_t)
+    wide_a, main_c, edge_c, z_low, z_high = filters(uniform_t)
     from_z_low = shifted(z_high, "gz", 1)
     from_z_high = shifted(z_low, "gz", -1)
-    main_a, edge_a = first_y(coords, ya)
+    main_a, edge_a = first_a(wide_a)
     spread_a = jnp.asarray(depth_spread(126, 2))
     spread_c = jnp.asarray(depth_spread(61, 3))
     y_low, y_high = vmem_call(
@@ -743,7 +745,7 @@
     )
     sum_a, sum_c, x_low, x_high = local_call(
         x_edges_kernel,
-        shapes + [jax.ShapeDtypeStruct((896, 128), BF16)] * 2,
+        shapes + [jax.ShapeDtypeStruct((704, 128), BF16)] * 2,
         [vmem] * 4,
         [sum_a, sum_c, from_y_low, from_y_high],
         "x_edges",
@@ -751,15 +753,28 @@
     )
     from_x_low = shifted(x_high, "gx", 1)
     from_x_high = shifted(x_low, "gx", -1)
-    mid, coarse = vmem_call(
+    hbm = pl.BlockSpec(memory_space=pltpu.HBM)
+    planes = sum_a.reshape(48, 64, 128)
+    mid_shape = jax.ShapeDtypeStruct((4, 8, 64, 128), F32)
+    [mid] = local_call(
+        inside_kernel,
+        [mid_shape],
+        [vmem],
+        [planes],
+        "inside",
+        out_specs=[hbm],
+        scratch=[pltpu.SemaphoreType.DMA((4,))],
+        flops=2_000_000_000,
+    )
+    coarse, mid = local_call(
         final_kernel,
-        [
-            jax.ShapeDtypeStruct((4, 8, 64, 128), F32),
-            jax.ShapeDtypeStruct((4, 4, 32, 64), F32),
-        ],
-        [],
+        [jax.ShapeDtypeStruct((4, 4, 32, 64), F32), mid_shape],
+        [vmem] * 4 + [hbm],
+        [planes, sum_c, from_x_low, from_x_high, mid],
         "final",
-        sum_a, sum_c, from_x_low, from_x_high,
+        out_specs=[vmem, hbm],
+        scratch=[pltpu.VMEM((8, 2, 64, 128), F32), pltpu.SemaphoreType.DMA((8,))],
+        aliases={4: 1},
     )
     return mid, coarse
 

time: 58.1 us -> 54.5 us (0.938)
  waiting for transfers between devices: 12.2 us -> 9.39 us
  other arithmetic: 0.62 us -> 0 us
    ppermute x12, waiting for transfers between devices: 12.2 us -> 9.39 us  [shifted(): return lax.ppermute(x, axis, [(i, (i + by) % size) for i in range(size)])]
    pallas_call x8 -> x9, Pallas kernels: 21.4 us -> 22.7 us  [local_call(): pl.pallas_call(kernel, out_shape=list(outs), in_specs=specs, out_specs=ou...]
    pallas_call x2 -> x1, Pallas kernels: 1.49 us -> 0.34 us  [vmem_call(): pl.pallas_call(kernel, out_shape=out_shape, in_specs=[vmem] * len(operand...]
    another operation x1 -> x0, other arithmetic: 0.62 us -> none  [body(): coords = jnp.stack([ix, iy, iz, me]).astype(jnp.int32)]
  transfers between devices with their start and end apart: 12 -> 12, of which waited for: 6 -> 4; matrix products, arithmetic and copies ran while one was open for 0% -> 0% of each run, Pallas kernels for 10% -> 14%
where the time goes in v4:
time: 54.5 us; the launch traced here: 54.2 us
  Pallas kernels  29 us (53%)
  starting transfers between devices  14.2 us (26%)
  waiting for transfers between devices  9.39 us (17%)
  between operations  0.84 us (2%)
  local copies, waits for them, and re-layouts  0.71 us (1%)
    pallas_call x9, Pallas kernels, local_call(): pl.pallas_call(kernel, out_shape=list(outs), in_specs=specs, out_specs=ou...  22.7 us
    ppermute x12, starting transfers between devices, shifted(): return lax.ppermute(x, axis, [(i, (i + by) % size) for i in range(size)])  14.2 us
    ppermute x12, waiting for transfers between devices, shifted(): return lax.ppermute(x, axis, [(i, (i + by) % size) for i in range(size)])  9.39 us
    pallas_call x1, Pallas kernels, pack(): pl.pallas_call(pack_kernel, out_shape=[jax.ShapeDtypeStruct((PAYLOAD, 128...  5.93 us
  transfers between devices with their start and end apart: 12, of which 4 were waited for; matrix products, arithmetic and copies ran while one was open for 0% of the time, Pallas kernels for 14%

profile of v4, /device:TPU:30, one launch (start us, length us, event | category | flops | bytes accessed | tf_op | source)
XLA Modules:
  0.0 54.2 jit_solution(3306548061307615904)
XLA Ops:
  0.6 0.0 copy-start.2
  0.6 0.0 copy-start.1
  0.7 5.9 %pack.1 = (bf16[336,128]{1,0:T(8,128)(2,1)}, bf16[336,128]{1,0:T(8,128)(2,1)}, bf16[336,128]{1,0:T(8,128)(2,1)}, bf16[336,128]{1,0:T(8,128)(2,1)}, bf16[336,128]...) custom-call(s32[8,128]{1,0:T(8,128)} %bitcast.15, bf16[1024,512]{1,0:T(8,128)(2,1)} %jac.1, ...), custom_call_target="tpu_custom_call" | custom-call | tf_op jit(solution)/shard_map/pack/pallas_call | solution.py:211
  6.6 0.0 copy-start
  6.6 0.0 collective-permute-start
  6.6 3.0 %collective-permute-start.1 = (bf16[336,128]{1,0:T(8,128)(2,1)}, bf16[336,128]{1,0:T(8,128)(2,1)S(1)}, u32[]{:S(2)}, u32[]{:S(2)}) collective-permute-start(bf16[336,128]{1,0:T(8,128)(2,1)} %get-tuple-element.31), channel_id=1, source_target_pairs={{0,112},{16,0},{32,16},{48,32},{64,48},{80,64},{96,80},{112,96},{1... | collective-permute-start | bytes 258056 | tf_op jit(solution)/shard_map/ppermute | solution.py:704
  9.6 0.9 %collective-permute-start.2 = (bf16[336,128]{1,0:T(8,128)(2,1)}, bf16[336,128]{1,0:T(8,128)(2,1)S(1)}, u32[]{:S(2)}, u32[]{:S(2)}) collective-permute-start(bf16[336,128]{1,0:T(8,128)(2,1)} %get-tuple-element.32), channel_id=1, source_target_pairs={{0,4},{4,8},{8,12},{12,0},{1,5},{5,9},{9,13},{13,1},{2,6},{6,10},{... | collective-permute-start | bytes 258056 | tf_op jit(solution)/shard_map/ppermute | solution.py:704
  10.6 1.1 %collective-permute-start.3 = (bf16[336,128]{1,0:T(8,128)(2,1)}, bf16[336,128]{1,0:T(8,128)(2,1)S(1)}, u32[]{:S(2)}, u32[]{:S(2)}) collective-permute-start(bf16[336,128]{1,0:T(8,128)(2,1)} %get-tuple-element.33), channel_id=1, source_target_pairs={{0,12},{4,0},{8,4},{12,8},{1,13},{5,1},{9,5},{13,9},{2,14},{6,2},{... | collective-permute-start | bytes 258056 | tf_op jit(solution)/shard_map/ppermute | solution.py:704
  11.7 0.3 collective-permute-start.4
  12.0 0.0 collective-permute-done.first_arrived.a0
  12.0 1.7 %collective-permute-start.5 = (bf16[336,128]{1,0:T(8,128)(2,1)}, bf16[336,128]{1,0:T(8,128)(2,1)S(1)}, u32[]{:S(2)}, u32[]{:S(2)}) collective-permute-start(bf16[336,128]{1,0:T(8,128)(2,1)} %get-tuple-element.35), channel_id=1, source_target_pairs={{0,3},{1,0},{2,1},{3,2},{4,7},{5,4},{6,5},{7,6},{8,11},{9,8},{10,9... | collective-permute-start | bytes 258056 | tf_op jit(solution)/shard_map/ppermute | solution.py:704
  13.7 0.0 copy-done.2
  13.7 0.0 copy-done.1
  13.7 0.0 copy-start.5
  13.7 0.7 %copy-done.5 = s32[8,128]{1,0:T(8,128)S(1)} copy-done((s32[8,128]{1,0:T(8,128)S(1)}, s32[8,128]{1,0:T(8,128)}, u32[]{:S(2)}) %copy-start.5) | copy-done | bytes 4120
  14.4 1.8 %jacobians.1._.jac_in = f32[512,1024]{1,0:T(8,128)S(1)} custom-call(s32[8,128]{1,0:T(8,128)S(1)} %copy-done.5, bf16[1024,512]{1,0:T(8,128)(2,1)S(1)} %copy-done.1, bf16[512,512]{1,0:T(8,128)(2,1)S(1)} %copy-done.2, bf16[336,128]{1,0:T(8,128)(2,1)S(1)} %collective-permute-done.first_arrived.a0), custom_call_target="tpu_custom_call" | custom-call | flops 2000000000 | bytes 1000000 | tf_op jit(solution)/shard_map/jacobians/pallas_call | solution.py:234
  16.2 0.0 copy-done
  16.2 0.0 copy-start.3
  16.2 1.8 %place.1.rows = f32[1040,16,128]{2,1,0:T(8,128)S(1)} custom-call(s32[1024]{0:T(1024)S(1)} %bitcast.14, bf16[1024,16,128]{2,1,0:T(8,128)(2,1)S(1)} %bitcast.11, f32[512,1024]{1,0:T(8,128)S(1)} %jacobians.1._.jac_in), custom_call_target="tpu_custom_call" | custom-call | flops 2000000000 | bytes 1000000 | tf_op jit(solution)/shard_map/place/pallas_call | solution.py:234
  18.0 0.0 copy-start.4
  18.0 0.0 collective-permute-done.1.a1
  18.0 0.0 collective-permute-done.2.a2
  18.1 0.0 collective-permute-done.3.a3
  18.1 0.0 collective-permute-done.4.a4
  18.1 0.0 collective-permute-done.5.a5
  18.1 0.0 copy-done.3
  18.1 5.3 %brick.1 = (bf16[512,1024]{1,0:T(8,128)(2,1)S(1)}, bf16[512,1024]{1,0:T(8,128)(2,1)S(1)}, bf16[512,1024]{1,0:T(8,128)(2,1)S(1)}, bf16[512,1024]{1,0:T(8,128)(2,1)S(1)}, f32[1040,16,128]{2,1,0:T(8,128)S(1)}) custom-call(bf16[336,128]{1,0:T(8,128)(2,1)S(1)} %collective-permute-done.first_arrived.a0, ...), custom_call_target="tpu_custom_call", output_to_operand_aliasing={{4}: (9, {})} | custom-call | bytes 1000000 | tf_op jit(solution)/shard_map/brick/pallas_call | solution.py:234
  23.4 0.0 copy-done.4
  23.4 7.9 %filters.1 = (f32[8192,128]{1,0:T(8,128)S(1)}, f32[1280,128]{1,0:T(8,128)S(1)}, f32[640,128]{1,0:T(8,128)S(1)}, bf16[4,5760]{1,0:T(4,128)(2,1)S(1)}, bf16[4,5760]{1,0:T(4,128)(2,1)S(1)}) custom-call(bf16[512,1024]{1,0:T(8,128)(2,1)S(1)} %get-tuple-element.37.u0, bf16[512,1024]{1,0:T(8,128)(2,1)S(1)} %get-tuple-element.38.u1, ...), custom_call_target="tpu_custom_call" | custom-call | bytes 1000000 | tf_op jit(solution)/shard_map/filters/pallas_call | solution.py:234
  31.3 1.6 %collective-permute-start.6 = (bf16[4,5760]{1,0:T(4,128)(2,1)S(1)}, bf16[4,5760]{1,0:T(4,128)(2,1)S(1)}, u32[]{:S(2)}, u32[]{:S(2)}) collective-permute-start(bf16[4,5760]{1,0:T(4,128)(2,1)S(1)} %get-tuple-element.44), channel_id=1, source_target_pairs={{0,1},{1,2},{2,3},{3,0},{4,5},{5,6},{6,7},{7,4},{8,9},{9,10},{10,1... | collective-permute-start | bytes 138248 | tf_op jit(solution)/shard_map/ppermute | solution.py:704
  32.9 0.5 collective-permute-start.7
  33.4 0.0 copy-start.6
  33.4 0.0 copy-start.7
  33.4 2.5 %first_a.1 = (f32[3072,128]{1,0:T(8,128)S(1)}, f32[768,128]{1,0:T(8,128)S(1)}) custom-call(f32[8192,128]{1,0:T(8,128)S(1)} %get-tuple-element.41.wide), custom_call_target="tpu_custom_call" | custom-call | flops 3000000000 | bytes 1000000 | tf_op jit(solution)/shard_map/first_a/pallas_call | solution.py:234
  35.9 0.0 collective-permute-done.6.zl.from_low
  35.9 2.3 %collective-permute-done.7.zh.from_high = bf16[4,5760]{1,0:T(4,128)(2,1)S(1)} collective-permute-done((bf16[4,5760]{1,0:T(4,128)(2,1)S(1)}, bf16[4,5760]{1,0:T(4,128)(2,1)S(1)}, u32[]{:S(2)}, u32[]{:S(2)}) %collective-permute-start.7) | collective-permute-done | bytes 46112 | tf_op jit(solution)/shard_map/ppermute | solution.py:704
  38.2 0.0 copy-done.6
  38.2 0.0 copy-done.7
  38.2 0.3 y_edges.1
  38.6 2.0 %collective-permute-start.8 = (bf16[224,128]{1,0:T(8,128)(2,1)S(1)}, bf16[224,128]{1,0:T(8,128)(2,1)S(1)}, u32[]{:S(2)}, u32[]{:S(2)}) collective-permute-start(bf16[224,128]{1,0:T(8,128)(2,1)S(1)} %get-tuple-element.50), channel_id=1, source_target_pairs={{0,4},{4,8},{8,12},{12,0},{1,5},{5,9},{9,13},{13,1},{2,6},{6,10},{... | collective-permute-start | bytes 172040 | tf_op jit(solution)/shard_map/ppermute | solution.py:704
  40.5 0.1 collective-permute-start.9
  40.6 0.5 z_main.1
  41.2 1.6 %collective-permute-done.8.yl = bf16[224,128]{1,0:T(8,128)(2,1)S(1)} collective-permute-done((bf16[224,128]{1,0:T(8,128)(2,1)S(1)}, bf16[224,128]{1,0:T(8,128)(2,1)S(1)}, u32[]{:S(2)}, u32[]{:S(2)}) %collective-permute-start.8) | collective-permute-done | bytes 57376 | tf_op jit(solution)/shard_map/ppermute | solution.py:704
  42.8 3.1 %collective-permute-done.9.yh = bf16[224,128]{1,0:T(8,128)(2,1)S(1)} collective-permute-done((bf16[224,128]{1,0:T(8,128)(2,1)S(1)}, bf16[224,128]{1,0:T(8,128)(2,1)S(1)}, u32[]{:S(2)}, u32[]{:S(2)}) %collective-permute-start.9) | collective-permute-done | bytes 57376 | tf_op jit(solution)/shard_map/ppermute | solution.py:704
  45.9 0.5 %x_edges.1 = (f32[3072,128]{1,0:T(8,128)S(1)}, f32[1280,128]{1,0:T(8,128)S(1)}, bf16[704,128]{1,0:T(8,128)(2,1)S(1)}, bf16[704,128]{1,0:T(8,128)(2,1)S(1)}) custom-call(f32[3072,128]{1,0:T(8,128)S(1)} %get-tuple-element.46.sa_in, f32[1280,128]{1,0:T(8,128)S(1)} %get-tuple-element.47.sc_in, bf16[224,128]{1,0:T(8,128)(2,1)S(1)} %collective-permute-done.8.yl, ...), custom_call_target="tpu_custom_call" | custom-call | bytes 1000000 | tf_op jit(solution)/shard_map/x_edges/pallas_call | solution.py:234
  46.5 0.0 collective-permute-start.10
  46.5 2.9 %collective-permute-start.11 = (bf16[704,128]{1,0:T(8,128)(2,1)S(1)}, bf16[704,128]{1,0:T(8,128)(2,1)S(1)}, u32[]{:S(2)}, u32[]{:S(2)}) collective-permute-start(bf16[704,128]{1,0:T(8,128)(2,1)S(1)} %get-tuple-element.55), channel_id=1, source_target_pairs={{0,112},{16,0},{32,16},{48,32},{64,48},{80,64},{96,80},{112,96},{1... | collective-permute-start | bytes 540680 | tf_op jit(solution)/shard_map/ppermute | solution.py:704
  49.4 0.8 %inside.1._ = f32[4,8,64,128]{3,2,1,0:T(8,128)} custom-call(f32[48,64,128]{2,1,0:T(8,128)S(1)} %bitcast.12), custom_call_target="tpu_custom_call" | custom-call | flops 2000000000 | bytes 1000000 | tf_op jit(solution)/shard_map/inside/pallas_call | solution.py:234
  50.2 2.3 %collective-permute-done.10.xl = bf16[704,128]{1,0:T(8,128)(2,1)S(1)} collective-permute-done((bf16[704,128]{1,0:T(8,128)(2,1)S(1)}, bf16[704,128]{1,0:T(8,128)(2,1)S(1)}, u32[]{:S(2)}, u32[]{:S(2)}) %collective-permute-start.10) | collective-permute-done | bytes 180256 | tf_op jit(solution)/shard_map/ppermute | solution.py:704
  52.6 0.0 collective-permute-done.11.xh
  52.6 1.6 %final.1 = (f32[4,4,32,64]{3,2,1,0:T(8,128)}, f32[4,8,64,128]{3,2,1,0:T(8,128)}) custom-call(f32[48,64,128]{2,1,0:T(8,128)S(1)} %bitcast.13, f32[1280,128]{1,0:T(8,128)S(1)} %get-tuple-element.53.sc, bf16[704,128]{1,0:T(8,128)(2,1)S(1)} %collective-permute-done.10.xl, ...), custom_call_target="tpu_custom_call", output_to_operand_aliasing={{1}: (4, {})} | custom-call | bytes 1000000 | tf_op jit(solution)/shard_map/final/pallas_call | solution.py:234
Async XLA Ops:
  0.6 13.1 %copy-start.2 = (bf16[512,512]{1,0:T(8,128)(2,1)S(1)}, bf16[512,512]{1,0:T(8,128)(2,1)}, u32[]{:S(2)}) copy-start(bf16[512,512]{1,0:T(8,128)(2,1)} %constant.10.clone.order) | copy-start | bytes 1572868
  0.6 13.1 %copy-start.1 = (bf16[1024,512]{1,0:T(8,128)(2,1)S(1)}, bf16[1024,512]{1,0:T(8,128)(2,1)}, u32[]{:S(2)}) copy-start(bf16[1024,512]{1,0:T(8,128)(2,1)} %jac.1) | copy-start | bytes 3145732
  6.6 9.6 %copy-start = (bf16[1024,4,512]{2,1,0:T(4,128)(2,1)S(1)}, bf16[1024,4,512]{2,1,0:T(4,128)(2,1)}, u32[]{:S(2)}) copy-start(bf16[1024,4,512]{2,1,0:T(4,128)(2,1)} %param.9) | copy-start | bytes 12582916
  6.6 5.4 %collective-permute-start = (bf16[336,128]{1,0:T(8,128)(2,1)}, bf16[336,128]{1,0:T(8,128)(2,1)S(1)}, u32[]{:S(2)}, u32[]{:S(2)}) collective-permute-start(bf16[336,128]{1,0:T(8,128)(2,1)} %get-tuple-element.30), channel_id=1, source_target_pairs={{0,16},{16,32},{32,48},{48,64},{64,80},{80,96},{96,112},{112,0},{1... | collective-permute-start | bytes 258056 | tf_op jit(solution)/shard_map/ppermute | solution.py:704
  6.6 11.4 %collective-permute-start.1 = (bf16[336,128]{1,0:T(8,128)(2,1)}, bf16[336,128]{1,0:T(8,128)(2,1)S(1)}, u32[]{:S(2)}, u32[]{:S(2)}) collective-permute-start(bf16[336,128]{1,0:T(8,128)(2,1)} %get-tuple-element.31), channel_id=1, source_target_pairs={{0,112},{16,0},{32,16},{48,32},{64,48},{80,64},{96,80},{112,96},{1... | collective-permute-start | bytes 258056 | tf_op jit(solution)/shard_map/ppermute | solution.py:704
  9.6 8.4 %collective-permute-start.2 = (bf16[336,128]{1,0:T(8,128)(2,1)}, bf16[336,128]{1,0:T(8,128)(2,1)S(1)}, u32[]{:S(2)}, u32[]{:S(2)}) collective-permute-start(bf16[336,128]{1,0:T(8,128)(2,1)} %get-tuple-element.32), channel_id=1, source_target_pairs={{0,4},{4,8},{8,12},{12,0},{1,5},{5,9},{9,13},{13,1},{2,6},{6,10},{... | collective-permute-start | bytes 258056 | tf_op jit(solution)/shard_map/ppermute | solution.py:704
  10.6 7.5 %collective-permute-start.3 = (bf16[336,128]{1,0:T(8,128)(2,1)}, bf16[336,128]{1,0:T(8,128)(2,1)S(1)}, u32[]{:S(2)}, u32[]{:S(2)}) collective-permute-start(bf16[336,128]{1,0:T(8,128)(2,1)} %get-tuple-element.33), channel_id=1, source_target_pairs={{0,12},{4,0},{8,4},{12,8},{1,13},{5,1},{9,5},{13,9},{2,14},{6,2},{... | collective-permute-start | bytes 258056 | tf_op jit(solution)/shard_map/ppermute | solution.py:704
  11.7 6.4 %collective-permute-start.4 = (bf16[336,128]{1,0:T(8,128)(2,1)}, bf16[336,128]{1,0:T(8,128)(2,1)S(1)}, u32[]{:S(2)}, u32[]{:S(2)}) collective-permute-start(bf16[336,128]{1,0:T(8,128)(2,1)} %get-tuple-element.34), channel_id=1, source_target_pairs={{0,1},{1,2},{2,3},{3,0},{4,5},{5,6},{6,7},{7,4},{8,9},{9,10},{10,1... | collective-permute-start | bytes 258056 | tf_op jit(solution)/shard_map/ppermute | solution.py:704
  12.0 6.1 %collective-permute-start.5 = (bf16[336,128]{1,0:T(8,128)(2,1)}, bf16[336,128]{1,0:T(8,128)(2,1)S(1)}, u32[]{:S(2)}, u32[]{:S(2)}) collective-permute-start(bf16[336,128]{1,0:T(8,128)(2,1)} %get-tuple-element.35), channel_id=1, source_target_pairs={{0,3},{1,0},{2,1},{3,2},{4,7},{5,4},{6,5},{7,6},{8,11},{9,8},{10,9... | collective-permute-start | bytes 258056 | tf_op jit(solution)/shard_map/ppermute | solution.py:704
  13.7 0.7 %copy-start.5 = (s32[8,128]{1,0:T(8,128)S(1)}, s32[8,128]{1,0:T(8,128)}, u32[]{:S(2)}) copy-start(s32[8,128]{1,0:T(8,128)} %get-tuple-element.36.spots) | copy-start | bytes 12292
  16.2 1.9 %copy-start.3 = (bf16[512,512]{1,0:T(8,128)(2,1)S(1)}, bf16[512,512]{1,0:T(8,128)(2,1)}, u32[]{:S(2)}) copy-start(bf16[512,512]{1,0:T(8,128)(2,1)} %constant.11.clone.table) | copy-start | bytes 1572868
  18.0 5.4 %copy-start.4 = (bf16[3,256,256]{2,1,0:T(8,128)(2,1)S(1)}, bf16[3,256,256]{2,1,0:T(8,128)(2,1)}, u32[]{:S(2)}) copy-start(bf16[3,256,256]{2,1,0:T(8,128)(2,1)} %constant.12.clone.depths) | copy-start | bytes 1179652
  31.3 4.6 %collective-permute-start.6 = (bf16[4,5760]{1,0:T(4,128)(2,1)S(1)}, bf16[4,5760]{1,0:T(4,128)(2,1)S(1)}, u32[]{:S(2)}, u32[]{:S(2)}) collective-permute-start(bf16[4,5760]{1,0:T(4,128)(2,1)S(1)} %get-tuple-element.44), channel_id=1, source_target_pairs={{0,1},{1,2},{2,3},{3,0},{4,5},{5,6},{6,7},{7,4},{8,9},{9,10},{10,1... | collective-permute-start | bytes 138248 | tf_op jit(solution)/shard_map/ppermute | solution.py:704
  32.9 5.3 %collective-permute-start.7 = (bf16[4,5760]{1,0:T(4,128)(2,1)S(1)}, bf16[4,5760]{1,0:T(4,128)(2,1)S(1)}, u32[]{:S(2)}, u32[]{:S(2)}) collective-permute-start(bf16[4,5760]{1,0:T(4,128)(2,1)S(1)} %get-tuple-element.45), channel_id=1, source_target_pairs={{0,3},{1,0},{2,1},{3,2},{4,7},{5,4},{6,5},{7,6},{8,11},{9,8},{10,9... | collective-permute-start | bytes 138248 | tf_op jit(solution)/shard_map/ppermute | solution.py:704
  33.4 4.8 %copy-start.6 = (bf16[8,128]{1,0:T(8,128)(2,1)S(1)}, bf16[8,128]{1,0:T(8,128)(2,1)}, u32[]{:S(2)}) copy-start(bf16[8,128]{1,0:T(8,128)(2,1)} %constant.14.clone.spread_c) | copy-start | bytes 6148
  33.4 4.8 %copy-start.7 = (bf16[8,128]{1,0:T(8,128)(2,1)S(1)}, bf16[8,128]{1,0:T(8,128)(2,1)}, u32[]{:S(2)}) copy-start(bf16[8,128]{1,0:T(8,128)(2,1)} %constant.13.clone.spread_a) | copy-start | bytes 6148
  38.6 4.2 %collective-permute-start.8 = (bf16[224,128]{1,0:T(8,128)(2,1)S(1)}, bf16[224,128]{1,0:T(8,128)(2,1)S(1)}, u32[]{:S(2)}, u32[]{:S(2)}) collective-permute-start(bf16[224,128]{1,0:T(8,128)(2,1)S(1)} %get-tuple-element.50), channel_id=1, source_target_pairs={{0,4},{4,8},{8,12},{12,0},{1,5},{5,9},{9,13},{13,1},{2,6},{6,10},{... | collective-permute-start | bytes 172040 | tf_op jit(solution)/shard_map/ppermute | solution.py:704
  40.5 5.4 %collective-permute-start.9 = (bf16[224,128]{1,0:T(8,128)(2,1)S(1)}, bf16[224,128]{1,0:T(8,128)(2,1)S(1)}, u32[]{:S(2)}, u32[]{:S(2)}) collective-permute-start(bf16[224,128]{1,0:T(8,128)(2,1)S(1)} %get-tuple-element.51), channel_id=1, source_target_pairs={{0,12},{4,0},{8,4},{12,8},{1,13},{5,1},{9,5},{13,9},{2,14},{6,2},{... | collective-permute-start | bytes 172040 | tf_op jit(solution)/shard_map/ppermute | solution.py:704
  46.5 6.1 %collective-permute-start.10 = (bf16[704,128]{1,0:T(8,128)(2,1)S(1)}, bf16[704,128]{1,0:T(8,128)(2,1)S(1)}, u32[]{:S(2)}, u32[]{:S(2)}) collective-permute-start(bf16[704,128]{1,0:T(8,128)(2,1)S(1)} %get-tuple-element.54), channel_id=1, source_target_pairs={{0,16},{16,32},{32,48},{48,64},{64,80},{80,96},{96,112},{112,0},{1... | collective-permute-start | bytes 540680 | tf_op jit(solution)/shard_map/ppermute | solution.py:704
  46.5 6.1 %collective-permute-start.11 = (bf16[704,128]{1,0:T(8,128)(2,1)S(1)}, bf16[704,128]{1,0:T(8,128)(2,1)S(1)}, u32[]{:S(2)}, u32[]{:S(2)}) collective-permute-start(bf16[704,128]{1,0:T(8,128)(2,1)S(1)} %get-tuple-element.55), channel_id=1, source_target_pairs={{0,112},{16,0},{32,16},{48,32},{64,48},{80,64},{96,80},{112,96},{1... | collective-permute-start | bytes 540680 | tf_op jit(solution)/shard_map/ppermute | solution.py:704

commit v5 on v4

--- a/solution.py
+++ b/solution.py
@@ -223,7 +223,7 @@
             pltpu.SemaphoreType.DMA,
             pltpu.SemaphoreType.DMA((6,)),
         ],
-        compiler_params=pltpu.CompilerParams(vmem_limit_bytes=60 * MIB),
+        compiler_params=pltpu.CompilerParams(vmem_limit_bytes=53 * MIB),
         name="pack",
     )(home, jac, fields_rows)
 
@@ -401,7 +401,7 @@
         ref[pl.ds(base + size - width, width), :] = zero
         return carry
 
-    lax.fori_loop(0, count, pads, 0)
+    lax.fori_loop(0, count, pads, 0, unroll=4)
 
 
 def along_x(values, outputs, edge, x_low, x_high):
@@ -440,7 +440,7 @@
         main_a[pl.ds(pl.multiple_of(q * 64, 64), 64), :] = middle
         return carry
 
-    lax.fori_loop(0, 48, first, 0)
+    lax.fori_loop(0, 48, first, 0, unroll=4)
 
 
 def filter_kernel(u0, u1, u2, u3, depths, wide_a, main_c, edge_c, to_low, to_high,
@@ -505,7 +505,7 @@
         pbz[pl.ds(pl.multiple_of(768 + q * 64, 64), 64), :] = middle.astype(BF16)
         return carry
 
-    lax.fori_loop(0, 48, first, 0)
+    lax.fori_loop(0, 48, first, 0, unroll=4)
 
     def second_x(v, carry):
         for f in range(4):
@@ -517,7 +517,7 @@
                 yc[pl.ds(pl.multiple_of(at, 8), 8), :] = value
         return carry
 
-    lax.fori_loop(0, 10, second_x, 0)
+    lax.fori_loop(0, 10, second_x, 0, unroll=2)
 
     def second(q, carry):
         low, middle, high = along_y(yc, q * 112, 48, y_low, y_high)
@@ -530,7 +530,7 @@
         pcz[pl.ds(pl.multiple_of(640 + q * 32, 32), 32), :] = middle.astype(BF16)
         return carry
 
-    lax.fori_loop(0, 40, second, 0)
+    lax.fori_loop(0, 40, second, 0, unroll=4)
     row = lax.broadcasted_iota(jnp.int32, (16, 128), 0)
     lane = lax.broadcasted_iota(jnp.int32, (16, 128), 1)
 
@@ -669,7 +669,7 @@
         copy.wait()
 
 
-def final_kernel(sa, sc, xl, xh, _, coarse, mid, planes, sems):
+def final_kernel(sa, sc, xl, xh, _, coarse, mid, planes, small, sems):
     copies = []
     for side, ref in enumerate((xl, xh)):
         for f in range(4):
@@ -694,8 +694,10 @@
                 value = value + xl[start : start + 32, :].astype(F32)[:, half : half + 64]
             if x >= 1:
                 value = value + xh[start - 32 : start, :].astype(F32)[:, half : half + 64]
-            coarse[f, x] = value
-    for copy in copies:
+            small[f, x] = value
+    copy = pltpu.make_async_copy(small, coarse, sems.at[8])
+    copy.start()
+    for copy in copies + [copy]:
         copy.wait()
 
 
@@ -772,8 +774,12 @@
         [vmem] * 4 + [hbm],
         [planes, sum_c, from_x_low, from_x_high, mid],
         "final",
-        out_specs=[vmem, hbm],
-        scratch=[pltpu.VMEM((8, 2, 64, 128), F32), pltpu.SemaphoreType.DMA((8,))],
+        out_specs=[hbm, hbm],
+        scratch=[
+            pltpu.VMEM((8, 2, 64, 128), F32),
+            pltpu.VMEM((4, 4, 32, 64), F32),
+            pltpu.SemaphoreType.DMA((9,)),
+        ],
         aliases={4: 1},
     )
     return mid, coarse

time: 54.5 us -> 51.4 us (0.943)
  Pallas kernels: 29 us -> 25.6 us
    pallas_call x9, Pallas kernels: 22.7 us -> 20.9 us  [local_call(): pl.pallas_call(kernel, out_shape=list(outs), in_specs=specs, out_specs=ou...]
    pallas_call x1, Pallas kernels: 5.93 us -> 4.33 us  [pack(): pl.pallas_call(pack_kernel, out_shape=[jax.ShapeDtypeStruct((PAYLOAD, 128...]
  transfers between devices with their start and end apart: 12 -> 12, of which waited for: 4 -> 6; matrix products, arithmetic and copies ran while one was open for 0% -> 0% of each run, Pallas kernels for 14% -> 14%
where the time goes in v5:
time: 51.4 us; the launch traced here: 51.2 us
  Pallas kernels  25.6 us (50%)
  starting transfers between devices  14.4 us (28%)
  waiting for transfers between devices  9.5 us (18%)
  local copies, waits for them, and re-layouts  0.83 us (2%)
  between operations  0.83 us (2%)
    pallas_call x9, Pallas kernels, local_call(): pl.pallas_call(kernel, out_shape=list(outs), in_specs=specs, out_specs=ou...  20.9 us
    ppermute x12, starting transfers between devices, shifted(): return lax.ppermute(x, axis, [(i, (i + by) % size) for i in range(size)])  14.4 us
    ppermute x12, waiting for transfers between devices, shifted(): return lax.ppermute(x, axis, [(i, (i + by) % size) for i in range(size)])  9.5 us
    pallas_call x1, Pallas kernels, pack(): pl.pallas_call(pack_kernel, out_shape=[jax.ShapeDtypeStruct((PAYLOAD, 128...  4.33 us
  transfers between devices with their start and end apart: 12, of which 6 were waited for; matrix products, arithmetic and copies ran while one was open for 0% of the time, Pallas kernels for 14%

profile of v5, /device:TPU:30, one launch (start us, length us, event | category | flops | bytes accessed | tf_op | source)
XLA Modules:
  0.0 51.2 jit_solution(11090409591253271550)
XLA Ops:
  0.6 0.0 copy-start.2
  0.6 0.0 copy-start.1
  0.7 0.0 copy-start.5
  0.7 0.8 %copy-done.5 = s32[1024]{0:T(1024)S(1)} copy-done((s32[1024]{0:T(1024)S(1)}, s32[1024]{0:T(1024)}, u32[]{:S(2)}) %copy-start.5) | copy-done | bytes 4120
  1.5 4.3 %pack.1 = (bf16[336,128]{1,0:T(8,128)(2,1)S(1)}, bf16[336,128]{1,0:T(8,128)(2,1)S(1)}, bf16[336,128]{1,0:T(8,128)(2,1)S(1)}, bf16[336,128]{1,0:T(8,128)(2,1)S(1)...) custom-call(s32[8,128]{1,0:T(8,128)S(1)} %bitcast.14, bf16[1024,512]{1,0:T(8,128)(2,1)} %jac.1, ...), custom_call_target="tpu_custom_call" | custom-call | tf_op jit(solution)/shard_map/pack/pallas_call | solution.py:211
  5.8 0.0 copy-start
  5.8 0.0 collective-permute-start
  5.8 3.3 %collective-permute-start.1 = (bf16[336,128]{1,0:T(8,128)(2,1)S(1)}, bf16[336,128]{1,0:T(8,128)(2,1)S(1)}, u32[]{:S(2)}, u32[]{:S(2)}) collective-permute-start(bf16[336,128]{1,0:T(8,128)(2,1)S(1)} %get-tuple-element.31), channel_id=1, source_target_pairs={{0,112},{16,0},{32,16},{48,32},{64,48},{80,64},{96,80},{112,96},{1... | collective-permute-start | bytes 258056 | tf_op jit(solution)/shard_map/ppermute | solution.py:706
  9.1 0.2 collective-permute-start.2
  9.3 1.8 %collective-permute-start.3 = (bf16[336,128]{1,0:T(8,128)(2,1)S(1)}, bf16[336,128]{1,0:T(8,128)(2,1)S(1)}, u32[]{:S(2)}, u32[]{:S(2)}) collective-permute-start(bf16[336,128]{1,0:T(8,128)(2,1)S(1)} %get-tuple-element.33), channel_id=1, source_target_pairs={{0,12},{4,0},{8,4},{12,8},{1,13},{5,1},{9,5},{13,9},{2,14},{6,2},{... | collective-permute-start | bytes 258056 | tf_op jit(solution)/shard_map/ppermute | solution.py:706
  11.1 0.0 collective-permute-start.4
  11.1 0.1 collective-permute-done.first_arrived.a0
  11.3 1.9 %collective-permute-start.5 = (bf16[336,128]{1,0:T(8,128)(2,1)S(1)}, bf16[336,128]{1,0:T(8,128)(2,1)S(1)}, u32[]{:S(2)}, u32[]{:S(2)}) collective-permute-start(bf16[336,128]{1,0:T(8,128)(2,1)S(1)} %get-tuple-element.35), channel_id=1, source_target_pairs={{0,3},{1,0},{2,1},{3,2},{4,7},{5,4},{6,5},{7,6},{8,11},{9,8},{10,9... | collective-permute-start | bytes 258056 | tf_op jit(solution)/shard_map/ppermute | solution.py:706
  13.2 0.0 copy-done.2
  13.2 0.0 copy-done.1
  13.2 1.8 %jacobians.1._.jac_in = f32[512,1024]{1,0:T(8,128)S(1)} custom-call(s32[8,128]{1,0:T(8,128)S(1)} %get-tuple-element.36.spots, bf16[1024,512]{1,0:T(8,128)(2,1)S(1)} %copy-done.1, bf16[512,512]{1,0:T(8,128)(2,1)S(1)} %copy-done.2, bf16[336,128]{1,0:T(8,128)(2,1)S(1)} %collective-permute-done.first_arrived.a0), custom_call_target="tpu_custom_call" | custom-call | flops 2000000000 | bytes 1000000 | tf_op jit(solution)/shard_map/jacobians/pallas_call | solution.py:234
  15.0 0.0 copy-done
  15.0 0.0 copy-start.3
  15.0 1.8 %place.1.rows = f32[1040,16,128]{2,1,0:T(8,128)S(1)} custom-call(s32[1024]{0:T(1024)S(1)} %bitcast.15, bf16[1024,16,128]{2,1,0:T(8,128)(2,1)S(1)} %bitcast.11, f32[512,1024]{1,0:T(8,128)S(1)} %jacobians.1._.jac_in), custom_call_target="tpu_custom_call" | custom-call | flops 2000000000 | bytes 1000000 | tf_op jit(solution)/shard_map/place/pallas_call | solution.py:234
  16.8 0.0 copy-start.4
  16.8 0.0 collective-permute-done.1.a1
  16.8 0.0 collective-permute-done.2.a2
  16.8 0.0 collective-permute-done.3.a3
  16.9 0.0 collective-permute-done.4.a4
  16.9 0.1 collective-permute-done.5.a5
  17.0 0.0 copy-done.3
  17.0 5.3 %brick.1 = (bf16[512,1024]{1,0:T(8,128)(2,1)S(1)}, bf16[512,1024]{1,0:T(8,128)(2,1)S(1)}, bf16[512,1024]{1,0:T(8,128)(2,1)S(1)}, bf16[512,1024]{1,0:T(8,128)(2,1)S(1)}, f32[1040,16,128]{2,1,0:T(8,128)S(1)}) custom-call(bf16[336,128]{1,0:T(8,128)(2,1)S(1)} %collective-permute-done.first_arrived.a0, ...), custom_call_target="tpu_custom_call", output_to_operand_aliasing={{4}: (9, {})} | custom-call | bytes 1000000 | tf_op jit(solution)/shard_map/brick/pallas_call | solution.py:234
  22.3 0.0 copy-done.4
  22.3 7.1 %filters.1 = (f32[8192,128]{1,0:T(8,128)S(1)}, f32[1280,128]{1,0:T(8,128)S(1)}, f32[640,128]{1,0:T(8,128)S(1)}, bf16[4,5760]{1,0:T(4,128)(2,1)S(1)}, bf16[4,5760]{1,0:T(4,128)(2,1)S(1)}) custom-call(bf16[512,1024]{1,0:T(8,128)(2,1)S(1)} %get-tuple-element.37.u0, bf16[512,1024]{1,0:T(8,128)(2,1)S(1)} %get-tuple-element.38.u1, ...), custom_call_target="tpu_custom_call" | custom-call | bytes 1000000 | tf_op jit(solution)/shard_map/filters/pallas_call | solution.py:234
  29.4 1.3 %collective-permute-start.6 = (bf16[4,5760]{1,0:T(4,128)(2,1)S(1)}, bf16[4,5760]{1,0:T(4,128)(2,1)S(1)}, u32[]{:S(2)}, u32[]{:S(2)}) collective-permute-start(bf16[4,5760]{1,0:T(4,128)(2,1)S(1)} %get-tuple-element.44), channel_id=1, source_target_pairs={{0,1},{1,2},{2,3},{3,0},{4,5},{5,6},{6,7},{7,4},{8,9},{9,10},{10,1... | collective-permute-start | bytes 138248 | tf_op jit(solution)/shard_map/ppermute | solution.py:706
  30.7 0.8 %collective-permute-start.7 = (bf16[4,5760]{1,0:T(4,128)(2,1)S(1)}, bf16[4,5760]{1,0:T(4,128)(2,1)S(1)}, u32[]{:S(2)}, u32[]{:S(2)}) collective-permute-start(bf16[4,5760]{1,0:T(4,128)(2,1)S(1)} %get-tuple-element.45), channel_id=1, source_target_pairs={{0,3},{1,0},{2,1},{3,2},{4,7},{5,4},{6,5},{7,6},{8,11},{9,8},{10,9... | collective-permute-start | bytes 138248 | tf_op jit(solution)/shard_map/ppermute | solution.py:706
  31.5 0.0 copy-start.6
  31.5 0.0 copy-start.7
  31.5 2.1 %first_a.1 = (f32[3072,128]{1,0:T(8,128)S(1)}, f32[768,128]{1,0:T(8,128)S(1)}) custom-call(f32[8192,128]{1,0:T(8,128)S(1)} %get-tuple-element.41.wide), custom_call_target="tpu_custom_call" | custom-call | flops 3000000000 | bytes 1000000 | tf_op jit(solution)/shard_map/first_a/pallas_call | solution.py:234
  33.6 0.0 collective-permute-done.6.zl.from_low
  33.6 2.4 %collective-permute-done.7.zh.from_high = bf16[4,5760]{1,0:T(4,128)(2,1)S(1)} collective-permute-done((bf16[4,5760]{1,0:T(4,128)(2,1)S(1)}, bf16[4,5760]{1,0:T(4,128)(2,1)S(1)}, u32[]{:S(2)}, u32[]{:S(2)}) %collective-permute-start.7) | collective-permute-done | bytes 46112 | tf_op jit(solution)/shard_map/ppermute | solution.py:706
  36.0 0.0 copy-done.6
  36.0 0.0 copy-done.7
  36.0 0.3 y_edges.1
  36.3 1.8 %collective-permute-start.8 = (bf16[224,128]{1,0:T(8,128)(2,1)S(1)}, bf16[224,128]{1,0:T(8,128)(2,1)S(1)}, u32[]{:S(2)}, u32[]{:S(2)}) collective-permute-start(bf16[224,128]{1,0:T(8,128)(2,1)S(1)} %get-tuple-element.50), channel_id=1, source_target_pairs={{0,4},{4,8},{8,12},{12,0},{1,5},{5,9},{9,13},{13,1},{2,6},{6,10},{... | collective-permute-start | bytes 172040 | tf_op jit(solution)/shard_map/ppermute | solution.py:706
  38.1 0.3 collective-permute-start.9
  38.4 0.5 z_main.1
  38.9 1.6 %collective-permute-done.8.yl = bf16[224,128]{1,0:T(8,128)(2,1)S(1)} collective-permute-done((bf16[224,128]{1,0:T(8,128)(2,1)S(1)}, bf16[224,128]{1,0:T(8,128)(2,1)S(1)}, u32[]{:S(2)}, u32[]{:S(2)}) %collective-permute-start.8) | collective-permute-done | bytes 57376 | tf_op jit(solution)/shard_map/ppermute | solution.py:706
  40.6 2.9 %collective-permute-done.9.yh = bf16[224,128]{1,0:T(8,128)(2,1)S(1)} collective-permute-done((bf16[224,128]{1,0:T(8,128)(2,1)S(1)}, bf16[224,128]{1,0:T(8,128)(2,1)S(1)}, u32[]{:S(2)}, u32[]{:S(2)}) %collective-permute-start.9) | collective-permute-done | bytes 57376 | tf_op jit(solution)/shard_map/ppermute | solution.py:706
  43.5 0.5 %x_edges.1 = (f32[3072,128]{1,0:T(8,128)S(1)}, f32[1280,128]{1,0:T(8,128)S(1)}, bf16[704,128]{1,0:T(8,128)(2,1)S(1)}, bf16[704,128]{1,0:T(8,128)(2,1)S(1)}) custom-call(f32[3072,128]{1,0:T(8,128)S(1)} %get-tuple-element.46.sa_in, f32[1280,128]{1,0:T(8,128)S(1)} %get-tuple-element.47.sc_in, bf16[224,128]{1,0:T(8,128)(2,1)S(1)} %collective-permute-done.8.yl, ...), custom_call_target="tpu_custom_call" | custom-call | bytes 1000000 | tf_op jit(solution)/shard_map/x_edges/pallas_call | solution.py:234
  44.0 0.0 collective-permute-start.10
  44.1 2.9 %collective-permute-start.11 = (bf16[704,128]{1,0:T(8,128)(2,1)S(1)}, bf16[704,128]{1,0:T(8,128)(2,1)S(1)}, u32[]{:S(2)}, u32[]{:S(2)}) collective-permute-start(bf16[704,128]{1,0:T(8,128)(2,1)S(1)} %get-tuple-element.55), channel_id=1, source_target_pairs={{0,112},{16,0},{32,16},{48,32},{64,48},{80,64},{96,80},{112,96},{1... | collective-permute-start | bytes 540680 | tf_op jit(solution)/shard_map/ppermute | solution.py:706
  47.0 0.8 %inside.1._ = f32[4,8,64,128]{3,2,1,0:T(8,128)} custom-call(f32[48,64,128]{2,1,0:T(8,128)S(1)} %bitcast.12), custom_call_target="tpu_custom_call" | custom-call | flops 2000000000 | bytes 1000000 | tf_op jit(solution)/shard_map/inside/pallas_call | solution.py:234
  47.8 2.3 %collective-permute-done.10.xl = bf16[704,128]{1,0:T(8,128)(2,1)S(1)} collective-permute-done((bf16[704,128]{1,0:T(8,128)(2,1)S(1)}, bf16[704,128]{1,0:T(8,128)(2,1)S(1)}, u32[]{:S(2)}, u32[]{:S(2)}) %collective-permute-start.10) | collective-permute-done | bytes 180256 | tf_op jit(solution)/shard_map/ppermute | solution.py:706
  50.2 0.0 collective-permute-done.11.xh
  50.2 1.0 %final.1 = (f32[4,4,32,64]{3,2,1,0:T(8,128)}, f32[4,8,64,128]{3,2,1,0:T(8,128)}) custom-call(f32[48,64,128]{2,1,0:T(8,128)S(1)} %bitcast.13, f32[1280,128]{1,0:T(8,128)S(1)} %get-tuple-element.53.sc, bf16[704,128]{1,0:T(8,128)(2,1)S(1)} %collective-permute-done.10.xl, ...), custom_call_target="tpu_custom_call", output_to_operand_aliasing={{1}: (4, {})} | custom-call | bytes 1000000 | tf_op jit(solution)/shard_map/final/pallas_call | solution.py:234
Async XLA Ops:
  0.6 12.5 %copy-start.2 = (bf16[512,512]{1,0:T(8,128)(2,1)S(1)}, bf16[512,512]{1,0:T(8,128)(2,1)}, u32[]{:S(2)}) copy-start(bf16[512,512]{1,0:T(8,128)(2,1)} %constant.10.clone.order) | copy-start | bytes 1572868
  0.6 12.5 %copy-start.1 = (bf16[1024,512]{1,0:T(8,128)(2,1)S(1)}, bf16[1024,512]{1,0:T(8,128)(2,1)}, u32[]{:S(2)}) copy-start(bf16[1024,512]{1,0:T(8,128)(2,1)} %jac.1) | copy-start | bytes 3145732
  0.7 0.8 %copy-start.5 = (s32[1024]{0:T(1024)S(1)}, s32[1024]{0:T(1024)}, u32[]{:S(2)}) copy-start(s32[1024]{0:T(1024)} %param.11) | copy-start | bytes 12292
  5.8 9.2 %copy-start = (bf16[1024,4,512]{2,1,0:T(4,128)(2,1)S(1)}, bf16[1024,4,512]{2,1,0:T(4,128)(2,1)}, u32[]{:S(2)}) copy-start(bf16[1024,4,512]{2,1,0:T(4,128)(2,1)} %param.9) | copy-start | bytes 12582916
  5.8 5.5 %collective-permute-start = (bf16[336,128]{1,0:T(8,128)(2,1)S(1)}, bf16[336,128]{1,0:T(8,128)(2,1)S(1)}, u32[]{:S(2)}, u32[]{:S(2)}) collective-permute-start(bf16[336,128]{1,0:T(8,128)(2,1)S(1)} %get-tuple-element.30), channel_id=1, source_target_pairs={{0,16},{16,32},{32,48},{48,64},{64,80},{80,96},{96,112},{112,0},{1... | collective-permute-start | bytes 258056 | tf_op jit(solution)/shard_map/ppermute | solution.py:706
  5.8 11.0 %collective-permute-start.1 = (bf16[336,128]{1,0:T(8,128)(2,1)S(1)}, bf16[336,128]{1,0:T(8,128)(2,1)S(1)}, u32[]{:S(2)}, u32[]{:S(2)}) collective-permute-start(bf16[336,128]{1,0:T(8,128)(2,1)S(1)} %get-tuple-element.31), channel_id=1, source_target_pairs={{0,112},{16,0},{32,16},{48,32},{64,48},{80,64},{96,80},{112,96},{1... | collective-permute-start | bytes 258056 | tf_op jit(solution)/shard_map/ppermute | solution.py:706
  9.1 7.7 %collective-permute-start.2 = (bf16[336,128]{1,0:T(8,128)(2,1)S(1)}, bf16[336,128]{1,0:T(8,128)(2,1)S(1)}, u32[]{:S(2)}, u32[]{:S(2)}) collective-permute-start(bf16[336,128]{1,0:T(8,128)(2,1)S(1)} %get-tuple-element.32), channel_id=1, source_target_pairs={{0,4},{4,8},{8,12},{12,0},{1,5},{5,9},{9,13},{13,1},{2,6},{6,10},{... | collective-permute-start | bytes 258056 | tf_op jit(solution)/shard_map/ppermute | solution.py:706
  9.3 7.5 %collective-permute-start.3 = (bf16[336,128]{1,0:T(8,128)(2,1)S(1)}, bf16[336,128]{1,0:T(8,128)(2,1)S(1)}, u32[]{:S(2)}, u32[]{:S(2)}) collective-permute-start(bf16[336,128]{1,0:T(8,128)(2,1)S(1)} %get-tuple-element.33), channel_id=1, source_target_pairs={{0,12},{4,0},{8,4},{12,8},{1,13},{5,1},{9,5},{13,9},{2,14},{6,2},{... | collective-permute-start | bytes 258056 | tf_op jit(solution)/shard_map/ppermute | solution.py:706
  11.1 5.7 %collective-permute-start.4 = (bf16[336,128]{1,0:T(8,128)(2,1)S(1)}, bf16[336,128]{1,0:T(8,128)(2,1)S(1)}, u32[]{:S(2)}, u32[]{:S(2)}) collective-permute-start(bf16[336,128]{1,0:T(8,128)(2,1)S(1)} %get-tuple-element.34), channel_id=1, source_target_pairs={{0,1},{1,2},{2,3},{3,0},{4,5},{5,6},{6,7},{7,4},{8,9},{9,10},{10,1... | collective-permute-start | bytes 258056 | tf_op jit(solution)/shard_map/ppermute | solution.py:706
  11.3 5.7 %collective-permute-start.5 = (bf16[336,128]{1,0:T(8,128)(2,1)S(1)}, bf16[336,128]{1,0:T(8,128)(2,1)S(1)}, u32[]{:S(2)}, u32[]{:S(2)}) collective-permute-start(bf16[336,128]{1,0:T(8,128)(2,1)S(1)} %get-tuple-element.35), channel_id=1, source_target_pairs={{0,3},{1,0},{2,1},{3,2},{4,7},{5,4},{6,5},{7,6},{8,11},{9,8},{10,9... | collective-permute-start | bytes 258056 | tf_op jit(solution)/shard_map/ppermute | solution.py:706
  15.0 1.9 %copy-start.3 = (bf16[512,512]{1,0:T(8,128)(2,1)S(1)}, bf16[512,512]{1,0:T(8,128)(2,1)}, u32[]{:S(2)}) copy-start(bf16[512,512]{1,0:T(8,128)(2,1)} %constant.11.clone.table) | copy-start | bytes 1572868
  16.8 5.5 %copy-start.4 = (bf16[3,256,256]{2,1,0:T(8,128)(2,1)S(1)}, bf16[3,256,256]{2,1,0:T(8,128)(2,1)}, u32[]{:S(2)}) copy-start(bf16[3,256,256]{2,1,0:T(8,128)(2,1)} %constant.12.clone.depths) | copy-start | bytes 1179652
  29.4 4.2 %collective-permute-start.6 = (bf16[4,5760]{1,0:T(4,128)(2,1)S(1)}, bf16[4,5760]{1,0:T(4,128)(2,1)S(1)}, u32[]{:S(2)}, u32[]{:S(2)}) collective-permute-start(bf16[4,5760]{1,0:T(4,128)(2,1)S(1)} %get-tuple-element.44), channel_id=1, source_target_pairs={{0,1},{1,2},{2,3},{3,0},{4,5},{5,6},{6,7},{7,4},{8,9},{9,10},{10,1... | collective-permute-start | bytes 138248 | tf_op jit(solution)/shard_map/ppermute | solution.py:706
  30.7 5.3 %collective-permute-start.7 = (bf16[4,5760]{1,0:T(4,128)(2,1)S(1)}, bf16[4,5760]{1,0:T(4,128)(2,1)S(1)}, u32[]{:S(2)}, u32[]{:S(2)}) collective-permute-start(bf16[4,5760]{1,0:T(4,128)(2,1)S(1)} %get-tuple-element.45), channel_id=1, source_target_pairs={{0,3},{1,0},{2,1},{3,2},{4,7},{5,4},{6,5},{7,6},{8,11},{9,8},{10,9... | collective-permute-start | bytes 138248 | tf_op jit(solution)/shard_map/ppermute | solution.py:706
  31.5 4.5 %copy-start.6 = (bf16[8,128]{1,0:T(8,128)(2,1)S(1)}, bf16[8,128]{1,0:T(8,128)(2,1)}, u32[]{:S(2)}) copy-start(bf16[8,128]{1,0:T(8,128)(2,1)} %constant.14.clone.spread_c) | copy-start | bytes 6148
  31.5 4.5 %copy-start.7 = (bf16[8,128]{1,0:T(8,128)(2,1)S(1)}, bf16[8,128]{1,0:T(8,128)(2,1)}, u32[]{:S(2)}) copy-start(bf16[8,128]{1,0:T(8,128)(2,1)} %constant.13.clone.spread_a) | copy-start | bytes 6148
  36.3 4.2 %collective-permute-start.8 = (bf16[224,128]{1,0:T(8,128)(2,1)S(1)}, bf16[224,128]{1,0:T(8,128)(2,1)S(1)}, u32[]{:S(2)}, u32[]{:S(2)}) collective-permute-start(bf16[224,128]{1,0:T(8,128)(2,1)S(1)} %get-tuple-element.50), channel_id=1, source_target_pairs={{0,4},{4,8},{8,12},{12,0},{1,5},{5,9},{9,13},{13,1},{2,6},{6,10},{... | collective-permute-start | bytes 172040 | tf_op jit(solution)/shard_map/ppermute | solution.py:706
  38.1 5.4 %collective-permute-start.9 = (bf16[224,128]{1,0:T(8,128)(2,1)S(1)}, bf16[224,128]{1,0:T(8,128)(2,1)S(1)}, u32[]{:S(2)}, u32[]{:S(2)}) collective-permute-start(bf16[224,128]{1,0:T(8,128)(2,1)S(1)} %get-tuple-element.51), channel_id=1, source_target_pairs={{0,12},{4,0},{8,4},{12,8},{1,13},{5,1},{9,5},{13,9},{2,14},{6,2},{... | collective-permute-start | bytes 172040 | tf_op jit(solution)/shard_map/ppermute | solution.py:706
  44.0 6.1 %collective-permute-start.10 = (bf16[704,128]{1,0:T(8,128)(2,1)S(1)}, bf16[704,128]{1,0:T(8,128)(2,1)S(1)}, u32[]{:S(2)}, u32[]{:S(2)}) collective-permute-start(bf16[704,128]{1,0:T(8,128)(2,1)S(1)} %get-tuple-element.54), channel_id=1, source_target_pairs={{0,16},{16,32},{32,48},{48,64},{64,80},{80,96},{96,112},{112,0},{1... | collective-permute-start | bytes 540680 | tf_op jit(solution)/shard_map/ppermute | solution.py:706
  44.1 6.1 %collective-permute-start.11 = (bf16[704,128]{1,0:T(8,128)(2,1)S(1)}, bf16[704,128]{1,0:T(8,128)(2,1)S(1)}, u32[]{:S(2)}, u32[]{:S(2)}) collective-permute-start(bf16[704,128]{1,0:T(8,128)(2,1)S(1)} %get-tuple-element.55), channel_id=1, source_target_pairs={{0,112},{16,0},{32,16},{48,32},{64,48},{80,64},{96,80},{112,96},{1... | collective-permute-start | bytes 540680 | tf_op jit(solution)/shard_map/ppermute | solution.py:706

commit v6 on v5

--- a/solution.py
+++ b/solution.py
@@ -23,8 +23,8 @@
     ]
 )
 
-SHIFTS = (("gx", 1), ("gx", -1), ("gy", 1), ("gy", -1), ("gz", 1), ("gz", -1))
-STEPS = (16, -16, 4, -4, 1, -1)
+SHIFTS = (('gz', 1), ('gz', -1), ('gy', 1), ('gy', -1), ('gx', 1), ('gx', -1))
+STEPS = (1, -1, 4, -4, 16, -16)
 PAYLOAD = 336
 
 
@@ -273,7 +273,20 @@
     lax.fori_loop(0, 32, place, 0)
 
 
-def brick_kernel(a0, a1, a2, a3, a4, a5, order, table, jac_in, rows, u0, u1, u2, u3, _,
+def regroup(values):
+    lane = lax.broadcasted_iota(jnp.int32, values[0].shape, 1)
+    v = list(values)
+    for bit, pairs in ((32, ((0, 1), (2, 3))), (64, ((0, 2), (1, 3)))):
+        mask = (lane & bit) != 0
+        for a, b in pairs:
+            v[a], v[b] = (
+                jnp.where(mask, pltpu.roll(v[b], bit, 1), v[a]),
+                jnp.where(mask, v[b], pltpu.roll(v[a], 128 - bit, 1)),
+            )
+    return v
+
+
+def brick_kernel(a0, a1, a2, a3, a4, a5, order, table, jac_in, rows, lhs, _,
                  jac_t, spot_v, spot_s, sem):
     arrays = (a0, a1, a2, a3, a4, a5)
     tags = jnp.zeros((8, 128), F32)
@@ -303,16 +316,22 @@
         for e in range(16):
             rows[spot_s[0, d * 16 + e]] = arrays[d][e * 16 : e * 16 + 16, :].astype(F32)
     flat = rows.reshape(1040 * 16, 128)
-    for f, out in enumerate((u0, u1, u2, u3)):
-        for n in range(4):
+    for n in range(4):
+        for f in range(4):
             pieces = [
                 flat[pl.ds(n * 4096 + c * 4 + f, 256, stride=16), :].astype(BF16)
                 for c in range(4)
             ]
             values = nt(table[...], jnp.concatenate(pieces, axis=1))
-            out[:, n * 256 : n * 256 + 256] = (
-                values * jac_t[:, n * 256 : n * 256 + 256]
-            ).astype(BF16)
+            values = (values * jac_t[:, n * 256 : n * 256 + 256]).astype(BF16)
+            for half in range(2):
+                ex, t = n // 2, n % 2 * 2 + half
+                part = values[:, half * 128 : half * 128 + 128]
+                for h in range(2):
+                    blocks = regroup([part[k * 64 : k * 64 + 64] for k in range(h * 4, h * 4 + 4)])
+                    for e in range(4):
+                        at = ((t * 4 + f) * 4 + e) * 128 + ex * 64
+                        lhs[at : at + 64, h * 128 : h * 128 + 128] = blocks[e]
 
 
 def own_elements(spots, fields_elems, jac, first_arrived):
@@ -342,8 +361,10 @@
     vmem = pl.BlockSpec(memory_space=pltpu.VMEM)
     return local_call(
         brick_kernel,
-        [jax.ShapeDtypeStruct((512, 1024), BF16)] * 4
-        + [jax.ShapeDtypeStruct((1040, 16, 128), F32)],
+        [
+            jax.ShapeDtypeStruct((8192, 256), BF16),
+            jax.ShapeDtypeStruct((1040, 16, 128), F32),
+        ],
         [vmem] * 10,
         [*arrived, jnp.asarray(point_order()), jnp.asarray(interp_table()), jac_t, rows],
         "brick",
@@ -353,9 +374,9 @@
             pltpu.SMEM((8, 128), jnp.int32),
             pltpu.SemaphoreType.DMA,
         ],
-        aliases={9: 4},
+        aliases={9: 1},
         limit=36,
-    )[:4]
+    )[0]
 
 
 def halve(values, outputs, shift):
@@ -443,7 +464,7 @@
     lax.fori_loop(0, 48, first, 0, unroll=4)
 
 
-def filter_kernel(u0, u1, u2, u3, depths, wide_a, main_c, edge_c, to_low, to_high,
+def filter_kernel(lhs, depths, wide_a, main_c, edge_c, to_low, to_high,
                   depth, wide_b, yb, mb, yc, pbz, pcz, sem):
     x_low, x_high, y_low, y_high = inner_sides()
     _, _, iz = brick_place()
@@ -455,34 +476,9 @@
     copy.wait()
 
     def quarter(t, carry):
-        lane = lax.broadcasted_iota(jnp.int32, (64, 128), 1)
-        odd = (lane & 32) != 0
-        upper = (lane & 64) != 0
         for f in range(4):
-            pieces = [[], [], [], []]
-            for ex in range(2):
-                total = (u0, u1, u2, u3)[f][
-                    :, pl.ds(pl.multiple_of(ex * 512 + t * 128, 128), 128)
-                ]
-                regrouped = []
-                for h in range(2):
-                    v = [total[(h * 4 + k) * 64 : (h * 4 + k) * 64 + 64] for k in range(4)]
-                    for a, b in ((0, 1), (2, 3)):
-                        v[a], v[b] = (
-                            jnp.where(odd, pltpu.roll(v[b], 32, 1), v[a]),
-                            jnp.where(odd, v[b], pltpu.roll(v[a], 96, 1)),
-                        )
-                    for a, b in ((0, 2), (1, 3)):
-                        v[a], v[b] = (
-                            jnp.where(upper, pltpu.roll(v[b], 64, 1), v[a]),
-                            jnp.where(upper, v[b], pltpu.roll(v[a], 64, 1)),
-                        )
-                    regrouped.append(v)
-                for e in range(4):
-                    pieces[e].append(
-                        jnp.concatenate([regrouped[0][e], regrouped[1][e]], axis=1)
-                    )
-            operand = jnp.concatenate([p for e in range(4) for p in pieces[e]], axis=0)
+            start = pl.multiple_of(t * 2048 + f * 512, 512)
+            operand = lhs[pl.ds(start, 512), :]
             both = nn(operand, depth[...])
             wide_a[pl.ds(pl.multiple_of(t * 2048 + f * 512, 512), 512), :] = both[:, 0:128]
             wide_b[f * 512 : f * 512 + 512, :] = both[:, 128:256]
@@ -546,7 +542,7 @@
         ref[:, 3840:5760] = coarse[at : at + 4].astype(BF16)
 
 
-def filters(uniform_t):
+def filters(uniform):
     vmem = pl.BlockSpec(memory_space=pltpu.VMEM)
     return local_call(
         filter_kernel,
@@ -557,8 +553,8 @@
             jax.ShapeDtypeStruct((4, 5760), BF16),
             jax.ShapeDtypeStruct((4, 5760), BF16),
         ],
-        [vmem] * 4 + [pl.BlockSpec(memory_space=pltpu.HBM)],
-        [*uniform_t, jnp.asarray(depth_tables())],
+        [vmem, pl.BlockSpec(memory_space=pltpu.HBM)],
+        [uniform, jnp.asarray(depth_tables())],
         "filters",
         scratch=[
             pltpu.VMEM((256, 256), BF16),
@@ -629,7 +625,38 @@
     sc[...] = main_c[...] + tn(lanes, spread_c[...])
 
 
-def x_edges_kernel(sa_in, sc_in, yl, yh, sa, sc, to_low, to_high, fl, fh):
+def x_edges_kernel(sa, sc, yl, yh, to_low, to_high, fl, fh, pa, pc):
+    fl[...] = yl[...].astype(F32)
+    fh[...] = yh[...].astype(F32)
+    for ref, xa, xc in ((to_low, 0, 0), (to_high, 10, 7)):
+        for f in range(4):
+            first = f * 12 + xa
+            pa[...] = sa[first * 64 : first * 64 + 128, :]
+            for x in range(2):
+                for r in range(2):
+                    row = r * 48 + first + x
+                    low, high = x * 64 + r, x * 64 + 62 + r
+                    pa[low : low + 1, :] += fl[row : row + 1, :]
+                    pa[high : high + 1, :] += fh[row : row + 1, :]
+            ref[f * 128 : f * 128 + 128, :] = pa[...].astype(BF16)
+            first = f * 10 + xc
+            at = f % 2 * 96
+            pc[at : at + 96, :] = sc[first * 32 : first * 32 + 96, :]
+            for x in range(3):
+                for r in range(3):
+                    row = 96 + r * 40 + first + x
+                    low, high = at + x * 32 + r, at + x * 32 + 29 + r
+                    pc[low : low + 1, :] += fl[row : row + 1, :]
+                    pc[high : high + 1, :] += fh[row : row + 1, :]
+            if f % 2 == 1:
+                lane = lax.broadcasted_iota(jnp.int32, (96, 128), 1)
+                start = 512 + f // 2 * 96
+                ref[start : start + 96, :] = jnp.where(
+                    lane < 64, pc[0:96, :], pltpu.roll(pc[96:192, :], 64, 1)
+                ).astype(BF16)
+
+
+def inside_kernel(sa_in, sc_in, yl, yh, mid, sa, sc, fl, fh, sems):
     sa[...] = sa_in[...]
     sc[...] = sc_in[...]
     fl[...] = yl[...].astype(F32)
@@ -640,26 +667,10 @@
     for r in range(3):
         sc[pl.ds(r, 40, stride=32), :] += fl[96 + r * 40 : 136 + r * 40, :]
         sc[pl.ds(29 + r, 40, stride=32), :] += fh[96 + r * 40 : 136 + r * 40, :]
-    for ref, xa, xc in ((to_low, 0, 0), (to_high, 10, 7)):
-        for f in range(4):
-            ref[f * 128 : f * 128 + 128, :] = sa[
-                (f * 12 + xa) * 64 : (f * 12 + xa) * 64 + 128, :
-            ].astype(BF16)
-        for pair in range(2):
-            left, right = (
-                sc[(f * 10 + xc) * 32 : (f * 10 + xc) * 32 + 96, :]
-                for f in (2 * pair, 2 * pair + 1)
-            )
-            lane = lax.broadcasted_iota(jnp.int32, (96, 128), 1)
-            ref[512 + pair * 96 : 608 + pair * 96, :] = jnp.where(
-                lane < 64, left, pltpu.roll(right, 64, 1)
-            ).astype(BF16)
-
-
-def inside_kernel(sa, mid, sems):
+    planes = sa.reshape(48, 64, 128)
     copies = [
         pltpu.make_async_copy(
-            sa.at[pl.ds(f * 12 + 4, 4)], mid.at[f].at[pl.ds(2, 4)], sems.at[f]
+            planes.at[pl.ds(f * 12 + 4, 4)], mid.at[f].at[pl.ds(2, 4)], sems.at[f]
         )
         for f in range(4)
     ]
@@ -716,8 +727,8 @@
     *payloads, spots = pack(home_tile, jacobian, fields_rows)
     arrived = [shifted(p, *move) for p, move in zip(payloads, SHIFTS)]
     rows, jac_t = own_elements(spots, fields_elems, jacobian, arrived[0])
-    uniform_t = all_elements(rows, jac_t, arrived)
-    wide_a, main_c, edge_c, z_low, z_high = filters(uniform_t)
+    uniform = all_elements(rows, jac_t, arrived)
+    wide_a, main_c, edge_c, z_low, z_high = filters(uniform)
     from_z_low = shifted(z_high, "gz", 1)
     from_z_high = shifted(z_low, "gz", -1)
     main_a, edge_a = first_a(wide_a)
@@ -745,34 +756,42 @@
         "z_main",
         flops=2_000_000_000,
     )
-    sum_a, sum_c, x_low, x_high = local_call(
+    x_low, x_high = local_call(
         x_edges_kernel,
-        shapes + [jax.ShapeDtypeStruct((704, 128), BF16)] * 2,
+        [jax.ShapeDtypeStruct((704, 128), BF16)] * 2,
         [vmem] * 4,
         [sum_a, sum_c, from_y_low, from_y_high],
         "x_edges",
-        scratch=[pltpu.VMEM((224, 128), F32), pltpu.VMEM((224, 128), F32)],
+        scratch=[
+            pltpu.VMEM((224, 128), F32),
+            pltpu.VMEM((224, 128), F32),
+            pltpu.VMEM((128, 128), F32),
+            pltpu.VMEM((192, 128), F32),
+        ],
     )
     from_x_low = shifted(x_high, "gx", 1)
     from_x_high = shifted(x_low, "gx", -1)
     hbm = pl.BlockSpec(memory_space=pltpu.HBM)
-    planes = sum_a.reshape(48, 64, 128)
     mid_shape = jax.ShapeDtypeStruct((4, 8, 64, 128), F32)
-    [mid] = local_call(
+    mid, sum_a, sum_c = local_call(
         inside_kernel,
-        [mid_shape],
-        [vmem],
-        [planes],
+        [mid_shape] + shapes,
+        [vmem] * 4,
+        [sum_a, sum_c, from_y_low, from_y_high],
         "inside",
-        out_specs=[hbm],
-        scratch=[pltpu.SemaphoreType.DMA((4,))],
+        out_specs=[hbm, vmem, vmem],
+        scratch=[
+            pltpu.VMEM((224, 128), F32),
+            pltpu.VMEM((224, 128), F32),
+            pltpu.SemaphoreType.DMA((4,)),
+        ],
         flops=2_000_000_000,
     )
     coarse, mid = local_call(
         final_kernel,
         [jax.ShapeDtypeStruct((4, 4, 32, 64), F32), mid_shape],
         [vmem] * 4 + [hbm],
-        [planes, sum_c, from_x_low, from_x_high, mid],
+        [sum_a.reshape(48, 64, 128), sum_c, from_x_low, from_x_high, mid],
         "final",
         out_specs=[hbm, hbm],
         scratch=[

time: 51.4 us -> 49.2 us (0.957)
  Pallas kernels: 25.6 us -> 23.8 us
    pallas_call x9, Pallas kernels: 20.9 us -> 19.5 us  [local_call(): pl.pallas_call(kernel, out_shape=list(outs), in_specs=specs, out_specs=ou...]
  transfers between devices with their start and end apart: 12 -> 12, of which waited for: 6 -> 5; matrix products, arithmetic and copies ran while one was open for 0% -> 0% of each run, Pallas kernels for 14% -> 15%
where the time goes in v6:
time: 49.2 us; the launch traced here: 48.6 us
  Pallas kernels  23.8 us (48%)
  starting transfers between devices  14.2 us (29%)
  waiting for transfers between devices  9 us (18%)
  between operations  0.84 us (2%)
  local copies, waits for them, and re-layouts  0.83 us (2%)
    pallas_call x9, Pallas kernels, local_call(): pl.pallas_call(kernel, out_shape=list(outs), in_specs=specs, out_specs=ou...  19.5 us
    ppermute x12, starting transfers between devices, shifted(): return lax.ppermute(x, axis, [(i, (i + by) % size) for i in range(size)])  14.2 us
    ppermute x12, waiting for transfers between devices, shifted(): return lax.ppermute(x, axis, [(i, (i + by) % size) for i in range(size)])  9 us
    pallas_call x1, Pallas kernels, pack(): pl.pallas_call(pack_kernel, out_shape=[jax.ShapeDtypeStruct((PAYLOAD, 128...  3.91 us
  transfers between devices with their start and end apart: 12, of which 5 were waited for; matrix products, arithmetic and copies ran while one was open for 0% of the time, Pallas kernels for 15%

profile of v6, /device:TPU:30, one launch (start us, length us, event | category | flops | bytes accessed | tf_op | source)
XLA Modules:
  0.0 48.6 jit_solution(16707604418526593534)
XLA Ops:
  0.6 0.0 copy-start.2
  0.6 0.0 copy-start.1
  0.7 0.0 copy-start.5
  0.7 0.8 %copy-done.5 = s32[1024]{0:T(1024)S(1)} copy-done((s32[1024]{0:T(1024)S(1)}, s32[1024]{0:T(1024)}, u32[]{:S(2)}) %copy-start.5) | copy-done | bytes 4120
  1.5 3.9 %pack.1 = (bf16[336,128]{1,0:T(8,128)(2,1)S(1)}, bf16[336,128]{1,0:T(8,128)(2,1)S(1)}, bf16[336,128]{1,0:T(8,128)(2,1)S(1)}, bf16[336,128]{1,0:T(8,128)(2,1)S(1)...) custom-call(s32[8,128]{1,0:T(8,128)S(1)} %bitcast.13, bf16[1024,512]{1,0:T(8,128)(2,1)} %jac.1, ...), custom_call_target="tpu_custom_call" | custom-call | tf_op jit(solution)/shard_map/pack/pallas_call | solution.py:211
  5.4 0.0 copy-start
  5.4 0.3 collective-permute-start
  5.7 1.8 %collective-permute-start.1 = (bf16[336,128]{1,0:T(8,128)(2,1)S(1)}, bf16[336,128]{1,0:T(8,128)(2,1)S(1)}, u32[]{:S(2)}, u32[]{:S(2)}) collective-permute-start(bf16[336,128]{1,0:T(8,128)(2,1)S(1)} %get-tuple-element.29), channel_id=1, source_target_pairs={{0,3},{1,0},{2,1},{3,2},{4,7},{5,4},{6,5},{7,6},{8,11},{9,8},{10,9... | collective-permute-start | bytes 258056 | tf_op jit(solution)/shard_map/ppermute | solution.py:717
  7.5 0.3 collective-permute-start.2
  7.8 1.7 %collective-permute-start.3 = (bf16[336,128]{1,0:T(8,128)(2,1)S(1)}, bf16[336,128]{1,0:T(8,128)(2,1)S(1)}, u32[]{:S(2)}, u32[]{:S(2)}) collective-permute-start(bf16[336,128]{1,0:T(8,128)(2,1)S(1)} %get-tuple-element.31), channel_id=1, source_target_pairs={{0,12},{4,0},{8,4},{12,8},{1,13},{5,1},{9,5},{13,9},{2,14},{6,2},{... | collective-permute-start | bytes 258056 | tf_op jit(solution)/shard_map/ppermute | solution.py:717
  9.5 0.0 collective-permute-start.4
  9.5 0.4 collective-permute-done.first_arrived.a0
  9.9 2.9 %collective-permute-start.5 = (bf16[336,128]{1,0:T(8,128)(2,1)S(1)}, bf16[336,128]{1,0:T(8,128)(2,1)S(1)}, u32[]{:S(2)}, u32[]{:S(2)}) collective-permute-start(bf16[336,128]{1,0:T(8,128)(2,1)S(1)} %get-tuple-element.33), channel_id=1, source_target_pairs={{0,112},{16,0},{32,16},{48,32},{64,48},{80,64},{96,80},{112,96},{1... | collective-permute-start | bytes 258056 | tf_op jit(solution)/shard_map/ppermute | solution.py:717
  12.8 0.0 copy-done.2
  12.8 0.0 copy-done.1
  12.8 1.8 %jacobians.1._.jac_in = f32[512,1024]{1,0:T(8,128)S(1)} custom-call(s32[8,128]{1,0:T(8,128)S(1)} %get-tuple-element.34.spots, bf16[1024,512]{1,0:T(8,128)(2,1)S(1)} %copy-done.1, bf16[512,512]{1,0:T(8,128)(2,1)S(1)} %copy-done.2, bf16[336,128]{1,0:T(8,128)(2,1)S(1)} %collective-permute-done.first_arrived.a0), custom_call_target="tpu_custom_call" | custom-call | flops 2000000000 | bytes 1000000 | tf_op jit(solution)/shard_map/jacobians/pallas_call | solution.py:234
  14.7 0.0 copy-done
  14.7 0.0 copy-start.3
  14.7 1.8 %place.1.rows = f32[1040,16,128]{2,1,0:T(8,128)S(1)} custom-call(s32[1024]{0:T(1024)S(1)} %bitcast.14, bf16[1024,16,128]{2,1,0:T(8,128)(2,1)S(1)} %bitcast.11, f32[512,1024]{1,0:T(8,128)S(1)} %jacobians.1._.jac_in), custom_call_target="tpu_custom_call" | custom-call | flops 2000000000 | bytes 1000000 | tf_op jit(solution)/shard_map/place/pallas_call | solution.py:234
  16.5 0.0 copy-start.4
  16.5 0.0 collective-permute-done.1.a1
  16.5 0.0 collective-permute-done.2.a2
  16.5 0.0 collective-permute-done.3.a3
  16.5 0.0 collective-permute-done.4.a4
  16.5 0.0 collective-permute-done.5.a5
  16.5 0.0 copy-done.3
  16.6 6.0 %brick.1 = (bf16[8192,256]{1,0:T(8,128)(2,1)S(1)}, f32[1040,16,128]{2,1,0:T(8,128)S(1)}) custom-call(bf16[336,128]{1,0:T(8,128)(2,1)S(1)} %collective-permute-done.first_arrived.a0, bf16[336,128]{1,0:T(8,128)(2,1)S(1)} %collective-permute-done.1.a1, bf16[336,128]{1,0:T(8,128)(2,1)S(1)} %collective-permute-done.2.a2, ...), custom_call_target="tpu_custom_call", output_to_operand_aliasing={{1}: (9, {})} | custom-call | bytes 1000000 | tf_op jit(solution)/shard_map/brick/pallas_call | solution.py:234
  22.6 0.0 copy-done.4
  22.6 5.0 %filters.1 = (f32[8192,128]{1,0:T(8,128)S(1)}, f32[1280,128]{1,0:T(8,128)S(1)}, f32[640,128]{1,0:T(8,128)S(1)}, bf16[4,5760]{1,0:T(4,128)(2,1)S(1)}, bf16[4,5760]{1,0:T(4,128)(2,1)S(1)}) custom-call(bf16[8192,256]{1,0:T(8,128)(2,1)S(1)} %get-tuple-element.35.lhs, bf16[3,256,256]{2,1,0:T(8,128)(2,1)S(1)} %copy-done.4), custom_call_target="tpu_custom_call" | custom-call | bytes 1000000 | tf_op jit(solution)/shard_map/filters/pallas_call | solution.py:234
  27.6 1.9 %collective-permute-start.6 = (bf16[4,5760]{1,0:T(4,128)(2,1)S(1)}, bf16[4,5760]{1,0:T(4,128)(2,1)S(1)}, u32[]{:S(2)}, u32[]{:S(2)}) collective-permute-start(bf16[4,5760]{1,0:T(4,128)(2,1)S(1)} %get-tuple-element.39), channel_id=1, source_target_pairs={{0,1},{1,2},{2,3},{3,0},{4,5},{5,6},{6,7},{7,4},{8,9},{9,10},{10,1... | collective-permute-start | bytes 138248 | tf_op jit(solution)/shard_map/ppermute | solution.py:717
  29.5 0.2 collective-permute-start.7
  29.7 0.0 copy-start.6
  29.7 0.0 copy-start.7
  29.7 2.1 %first_a.1 = (f32[3072,128]{1,0:T(8,128)S(1)}, f32[768,128]{1,0:T(8,128)S(1)}) custom-call(f32[8192,128]{1,0:T(8,128)S(1)} %get-tuple-element.36.wide), custom_call_target="tpu_custom_call" | custom-call | flops 3000000000 | bytes 1000000 | tf_op jit(solution)/shard_map/first_a/pallas_call | solution.py:234
  31.8 0.0 collective-permute-done.6.zl.from_low
  31.8 3.0 %collective-permute-done.7.zh.from_high = bf16[4,5760]{1,0:T(4,128)(2,1)S(1)} collective-permute-done((bf16[4,5760]{1,0:T(4,128)(2,1)S(1)}, bf16[4,5760]{1,0:T(4,128)(2,1)S(1)}, u32[]{:S(2)}, u32[]{:S(2)}) %collective-permute-start.7) | collective-permute-done | bytes 46112 | tf_op jit(solution)/shard_map/ppermute | solution.py:717
  34.8 0.0 copy-done.6
  34.8 0.0 copy-done.7
  34.8 0.3 y_edges.1
  35.1 0.8 %collective-permute-start.8 = (bf16[224,128]{1,0:T(8,128)(2,1)S(1)}, bf16[224,128]{1,0:T(8,128)(2,1)S(1)}, u32[]{:S(2)}, u32[]{:S(2)}) collective-permute-start(bf16[224,128]{1,0:T(8,128)(2,1)S(1)} %get-tuple-element.45), channel_id=1, source_target_pairs={{0,4},{4,8},{8,12},{12,0},{1,5},{5,9},{9,13},{13,1},{2,6},{6,10},{... | collective-permute-start | bytes 172040 | tf_op jit(solution)/shard_map/ppermute | solution.py:717
  35.9 1.3 %collective-permute-start.9 = (bf16[224,128]{1,0:T(8,128)(2,1)S(1)}, bf16[224,128]{1,0:T(8,128)(2,1)S(1)}, u32[]{:S(2)}, u32[]{:S(2)}) collective-permute-start(bf16[224,128]{1,0:T(8,128)(2,1)S(1)} %get-tuple-element.46), channel_id=1, source_target_pairs={{0,12},{4,0},{8,4},{12,8},{1,13},{5,1},{9,5},{13,9},{2,14},{6,2},{... | collective-permute-start | bytes 172040 | tf_op jit(solution)/shard_map/ppermute | solution.py:717
  37.2 0.5 %z_main.1 = (f32[3072,128]{1,0:T(8,128)S(1)}, f32[1280,128]{1,0:T(8,128)S(1)}) custom-call(f32[3072,128]{1,0:T(8,128)S(1)} %get-tuple-element.37.main_a, f32[1280,128]{1,0:T(8,128)S(1)} %get-tuple-element.38.main_c, bf16[4,5760]{1,0:T(4,128)(2,1)S(1)} %collective-permute-done.6.zl.from_low, bf16[4,5760]{1,0:T(4,128)(2,1)S(1)} %collective-permute-done.7.zh.from_high, ...), custom_call_target="tpu_custom_call" | custom-call | flops 2000000000 | bytes 1000000 | tf_op jit(solution)/shard_map/z_main/pallas_call | solution.py:234
  37.7 1.6 %collective-permute-done.8.yl = bf16[224,128]{1,0:T(8,128)(2,1)S(1)} collective-permute-done((bf16[224,128]{1,0:T(8,128)(2,1)S(1)}, bf16[224,128]{1,0:T(8,128)(2,1)S(1)}, u32[]{:S(2)}, u32[]{:S(2)}) %collective-permute-start.8) | collective-permute-done | bytes 57376 | tf_op jit(solution)/shard_map/ppermute | solution.py:717
  39.4 1.9 %collective-permute-done.9.yh = bf16[224,128]{1,0:T(8,128)(2,1)S(1)} collective-permute-done((bf16[224,128]{1,0:T(8,128)(2,1)S(1)}, bf16[224,128]{1,0:T(8,128)(2,1)S(1)}, u32[]{:S(2)}, u32[]{:S(2)}) %collective-permute-start.9) | collective-permute-done | bytes 57376 | tf_op jit(solution)/shard_map/ppermute | solution.py:717
  41.3 0.2 x_edges.1
  41.5 0.0 collective-permute-start.10
  41.5 2.9 %collective-permute-start.11 = (bf16[704,128]{1,0:T(8,128)(2,1)S(1)}, bf16[704,128]{1,0:T(8,128)(2,1)S(1)}, u32[]{:S(2)}, u32[]{:S(2)}) collective-permute-start(bf16[704,128]{1,0:T(8,128)(2,1)S(1)} %get-tuple-element.50), channel_id=1, source_target_pairs={{0,112},{16,0},{32,16},{48,32},{64,48},{80,64},{96,80},{112,96},{1... | collective-permute-start | bytes 540680 | tf_op jit(solution)/shard_map/ppermute | solution.py:717
  44.5 1.2 %inside.1 = (f32[4,8,64,128]{3,2,1,0:T(8,128)}, f32[3072,128]{1,0:T(8,128)S(1)}, f32[1280,128]{1,0:T(8,128)S(1)}) custom-call(f32[3072,128]{1,0:T(8,128)S(1)} %get-tuple-element.41.sa_in.sa, f32[1280,128]{1,0:T(8,128)S(1)} %get-tuple-element.42.sc_in.sc, bf16[224,128]{1,0:T(8,128)(2,1)S(1)} %collective-permute-done.8.yl, ...), custom_call_target="tpu_custom_call" | custom-call | flops 2000000000 | bytes 1000000 | tf_op jit(solution)/shard_map/inside/pallas_call | solution.py:234
  45.6 2.0 %collective-permute-done.10.xl = bf16[704,128]{1,0:T(8,128)(2,1)S(1)} collective-permute-done((bf16[704,128]{1,0:T(8,128)(2,1)S(1)}, bf16[704,128]{1,0:T(8,128)(2,1)S(1)}, u32[]{:S(2)}, u32[]{:S(2)}) %collective-permute-start.10) | collective-permute-done | bytes 180256 | tf_op jit(solution)/shard_map/ppermute | solution.py:717
  47.6 0.0 collective-permute-done.11.xh
  47.7 1.0 %final.1 = (f32[4,4,32,64]{3,2,1,0:T(8,128)}, f32[4,8,64,128]{3,2,1,0:T(8,128)}) custom-call(f32[48,64,128]{2,1,0:T(8,128)S(1)} %bitcast.12, f32[1280,128]{1,0:T(8,128)S(1)} %get-tuple-element.48.sc, bf16[704,128]{1,0:T(8,128)(2,1)S(1)} %collective-permute-done.10.xl, ...), custom_call_target="tpu_custom_call", output_to_operand_aliasing={{1}: (4, {})} | custom-call | bytes 1000000 | tf_op jit(solution)/shard_map/final/pallas_call | solution.py:234
Async XLA Ops:
  0.6 12.2 %copy-start.2 = (bf16[512,512]{1,0:T(8,128)(2,1)S(1)}, bf16[512,512]{1,0:T(8,128)(2,1)}, u32[]{:S(2)}) copy-start(bf16[512,512]{1,0:T(8,128)(2,1)} %constant.10.clone.order) | copy-start | bytes 1572868
  0.6 12.2 %copy-start.1 = (bf16[1024,512]{1,0:T(8,128)(2,1)S(1)}, bf16[1024,512]{1,0:T(8,128)(2,1)}, u32[]{:S(2)}) copy-start(bf16[1024,512]{1,0:T(8,128)(2,1)} %jac.1) | copy-start | bytes 3145732
  0.7 0.8 %copy-start.5 = (s32[1024]{0:T(1024)S(1)}, s32[1024]{0:T(1024)}, u32[]{:S(2)}) copy-start(s32[1024]{0:T(1024)} %param.11) | copy-start | bytes 12292
  5.4 9.3 %copy-start = (bf16[1024,4,512]{2,1,0:T(4,128)(2,1)S(1)}, bf16[1024,4,512]{2,1,0:T(4,128)(2,1)}, u32[]{:S(2)}) copy-start(bf16[1024,4,512]{2,1,0:T(4,128)(2,1)} %param.9) | copy-start | bytes 12582916
  5.4 4.6 %collective-permute-start = (bf16[336,128]{1,0:T(8,128)(2,1)S(1)}, bf16[336,128]{1,0:T(8,128)(2,1)S(1)}, u32[]{:S(2)}, u32[]{:S(2)}) collective-permute-start(bf16[336,128]{1,0:T(8,128)(2,1)S(1)} %get-tuple-element.28), channel_id=1, source_target_pairs={{0,1},{1,2},{2,3},{3,0},{4,5},{5,6},{6,7},{7,4},{8,9},{9,10},{10,1... | collective-permute-start | bytes 258056 | tf_op jit(solution)/shard_map/ppermute | solution.py:717
  5.7 10.8 %collective-permute-start.1 = (bf16[336,128]{1,0:T(8,128)(2,1)S(1)}, bf16[336,128]{1,0:T(8,128)(2,1)S(1)}, u32[]{:S(2)}, u32[]{:S(2)}) collective-permute-start(bf16[336,128]{1,0:T(8,128)(2,1)S(1)} %get-tuple-element.29), channel_id=1, source_target_pairs={{0,3},{1,0},{2,1},{3,2},{4,7},{5,4},{6,5},{7,6},{8,11},{9,8},{10,9... | collective-permute-start | bytes 258056 | tf_op jit(solution)/shard_map/ppermute | solution.py:717
  7.5 9.0 %collective-permute-start.2 = (bf16[336,128]{1,0:T(8,128)(2,1)S(1)}, bf16[336,128]{1,0:T(8,128)(2,1)S(1)}, u32[]{:S(2)}, u32[]{:S(2)}) collective-permute-start(bf16[336,128]{1,0:T(8,128)(2,1)S(1)} %get-tuple-element.30), channel_id=1, source_target_pairs={{0,4},{4,8},{8,12},{12,0},{1,5},{5,9},{9,13},{13,1},{2,6},{6,10},{... | collective-permute-start | bytes 258056 | tf_op jit(solution)/shard_map/ppermute | solution.py:717
  7.8 8.7 %collective-permute-start.3 = (bf16[336,128]{1,0:T(8,128)(2,1)S(1)}, bf16[336,128]{1,0:T(8,128)(2,1)S(1)}, u32[]{:S(2)}, u32[]{:S(2)}) collective-permute-start(bf16[336,128]{1,0:T(8,128)(2,1)S(1)} %get-tuple-element.31), channel_id=1, source_target_pairs={{0,12},{4,0},{8,4},{12,8},{1,13},{5,1},{9,5},{13,9},{2,14},{6,2},{... | collective-permute-start | bytes 258056 | tf_op jit(solution)/shard_map/ppermute | solution.py:717
  9.5 7.0 %collective-permute-start.4 = (bf16[336,128]{1,0:T(8,128)(2,1)S(1)}, bf16[336,128]{1,0:T(8,128)(2,1)S(1)}, u32[]{:S(2)}, u32[]{:S(2)}) collective-permute-start(bf16[336,128]{1,0:T(8,128)(2,1)S(1)} %get-tuple-element.32), channel_id=1, source_target_pairs={{0,16},{16,32},{32,48},{48,64},{64,80},{80,96},{96,112},{112,0},{1... | collective-permute-start | bytes 258056 | tf_op jit(solution)/shard_map/ppermute | solution.py:717
  9.9 6.6 %collective-permute-start.5 = (bf16[336,128]{1,0:T(8,128)(2,1)S(1)}, bf16[336,128]{1,0:T(8,128)(2,1)S(1)}, u32[]{:S(2)}, u32[]{:S(2)}) collective-permute-start(bf16[336,128]{1,0:T(8,128)(2,1)S(1)} %get-tuple-element.33), channel_id=1, source_target_pairs={{0,112},{16,0},{32,16},{48,32},{64,48},{80,64},{96,80},{112,96},{1... | collective-permute-start | bytes 258056 | tf_op jit(solution)/shard_map/ppermute | solution.py:717
  14.7 1.9 %copy-start.3 = (bf16[512,512]{1,0:T(8,128)(2,1)S(1)}, bf16[512,512]{1,0:T(8,128)(2,1)}, u32[]{:S(2)}) copy-start(bf16[512,512]{1,0:T(8,128)(2,1)} %constant.11.clone.table) | copy-start | bytes 1572868
  16.5 6.1 %copy-start.4 = (bf16[3,256,256]{2,1,0:T(8,128)(2,1)S(1)}, bf16[3,256,256]{2,1,0:T(8,128)(2,1)}, u32[]{:S(2)}) copy-start(bf16[3,256,256]{2,1,0:T(8,128)(2,1)} %constant.12.clone.depths) | copy-start | bytes 1179652
  27.6 4.2 %collective-permute-start.6 = (bf16[4,5760]{1,0:T(4,128)(2,1)S(1)}, bf16[4,5760]{1,0:T(4,128)(2,1)S(1)}, u32[]{:S(2)}, u32[]{:S(2)}) collective-permute-start(bf16[4,5760]{1,0:T(4,128)(2,1)S(1)} %get-tuple-element.39), channel_id=1, source_target_pairs={{0,1},{1,2},{2,3},{3,0},{4,5},{5,6},{6,7},{7,4},{8,9},{9,10},{10,1... | collective-permute-start | bytes 138248 | tf_op jit(solution)/shard_map/ppermute | solution.py:717
  29.5 5.3 %collective-permute-start.7 = (bf16[4,5760]{1,0:T(4,128)(2,1)S(1)}, bf16[4,5760]{1,0:T(4,128)(2,1)S(1)}, u32[]{:S(2)}, u32[]{:S(2)}) collective-permute-start(bf16[4,5760]{1,0:T(4,128)(2,1)S(1)} %get-tuple-element.40), channel_id=1, source_target_pairs={{0,3},{1,0},{2,1},{3,2},{4,7},{5,4},{6,5},{7,6},{8,11},{9,8},{10,9... | collective-permute-start | bytes 138248 | tf_op jit(solution)/shard_map/ppermute | solution.py:717
  29.7 5.1 %copy-start.6 = (bf16[8,128]{1,0:T(8,128)(2,1)S(1)}, bf16[8,128]{1,0:T(8,128)(2,1)}, u32[]{:S(2)}) copy-start(bf16[8,128]{1,0:T(8,128)(2,1)} %constant.14.clone.spread_c) | copy-start | bytes 6148
  29.7 5.1 %copy-start.7 = (bf16[8,128]{1,0:T(8,128)(2,1)S(1)}, bf16[8,128]{1,0:T(8,128)(2,1)}, u32[]{:S(2)}) copy-start(bf16[8,128]{1,0:T(8,128)(2,1)} %constant.13.clone.spread_a) | copy-start | bytes 6148
  35.1 4.2 %collective-permute-start.8 = (bf16[224,128]{1,0:T(8,128)(2,1)S(1)}, bf16[224,128]{1,0:T(8,128)(2,1)S(1)}, u32[]{:S(2)}, u32[]{:S(2)}) collective-permute-start(bf16[224,128]{1,0:T(8,128)(2,1)S(1)} %get-tuple-element.45), channel_id=1, source_target_pairs={{0,4},{4,8},{8,12},{12,0},{1,5},{5,9},{9,13},{13,1},{2,6},{6,10},{... | collective-permute-start | bytes 172040 | tf_op jit(solution)/shard_map/ppermute | solution.py:717
  35.9 5.4 %collective-permute-start.9 = (bf16[224,128]{1,0:T(8,128)(2,1)S(1)}, bf16[224,128]{1,0:T(8,128)(2,1)S(1)}, u32[]{:S(2)}, u32[]{:S(2)}) collective-permute-start(bf16[224,128]{1,0:T(8,128)(2,1)S(1)} %get-tuple-element.46), channel_id=1, source_target_pairs={{0,12},{4,0},{8,4},{12,8},{1,13},{5,1},{9,5},{13,9},{2,14},{6,2},{... | collective-permute-start | bytes 172040 | tf_op jit(solution)/shard_map/ppermute | solution.py:717
  41.5 6.1 %collective-permute-start.10 = (bf16[704,128]{1,0:T(8,128)(2,1)S(1)}, bf16[704,128]{1,0:T(8,128)(2,1)S(1)}, u32[]{:S(2)}, u32[]{:S(2)}) collective-permute-start(bf16[704,128]{1,0:T(8,128)(2,1)S(1)} %get-tuple-element.49), channel_id=1, source_target_pairs={{0,16},{16,32},{32,48},{48,64},{64,80},{80,96},{96,112},{112,0},{1... | collective-permute-start | bytes 540680 | tf_op jit(solution)/shard_map/ppermute | solution.py:717
  41.5 6.1 %collective-permute-start.11 = (bf16[704,128]{1,0:T(8,128)(2,1)S(1)}, bf16[704,128]{1,0:T(8,128)(2,1)S(1)}, u32[]{:S(2)}, u32[]{:S(2)}) collective-permute-start(bf16[704,128]{1,0:T(8,128)(2,1)S(1)} %get-tuple-element.50), channel_id=1, source_target_pairs={{0,112},{16,0},{32,16},{48,32},{64,48},{80,64},{96,80},{112,96},{1... | collective-permute-start | bytes 540680 | tf_op jit(solution)/shard_map/ppermute | solution.py:717

commit v7 on v6

--- a/solution.py
+++ b/solution.py
@@ -264,13 +264,13 @@
 
 def place_kernel(spots, fields, _, rows):
     def place(e, carry):
-        targets = [spots[e * 32 + u] for u in range(32)]
-        values = [fields[e * 32 + u] for u in range(32)]
-        for u in range(32):
+        targets = [spots[e * 64 + u] for u in range(64)]
+        values = [fields[e * 64 + u] for u in range(64)]
+        for u in range(64):
             rows[targets[u]] = values[u].astype(F32)
         return carry
 
-    lax.fori_loop(0, 32, place, 0)
+    lax.fori_loop(0, 16, place, 0)
 
 
 def regroup(values):
@@ -461,7 +461,7 @@
         main_a[pl.ds(pl.multiple_of(q * 64, 64), 64), :] = middle
         return carry
 
-    lax.fori_loop(0, 48, first, 0, unroll=4)
+    lax.fori_loop(0, 48, first, 0, unroll=16)
 
 
 def filter_kernel(lhs, depths, wide_a, main_c, edge_c, to_low, to_high,
@@ -487,7 +487,7 @@
                 first_x(wide_b, f * 512, f, e, t, yb, x_low, x_high)
         return carry
 
-    lax.fori_loop(0, 4, quarter, 0)
+    lax.fori_loop(0, 4, quarter, 0, unroll=4)
 
     def first(q, carry):
         low, middle, high = along_y(yb, q * 176, 80, y_low, y_high)
@@ -501,7 +501,7 @@
         pbz[pl.ds(pl.multiple_of(768 + q * 64, 64), 64), :] = middle.astype(BF16)
         return carry
 
-    lax.fori_loop(0, 48, first, 0, unroll=4)
+    lax.fori_loop(0, 48, first, 0, unroll=16)
 
     def second_x(v, carry):
         for f in range(4):
@@ -513,7 +513,7 @@
                 yc[pl.ds(pl.multiple_of(at, 8), 8), :] = value
         return carry
 
-    lax.fori_loop(0, 10, second_x, 0, unroll=2)
+    lax.fori_loop(0, 10, second_x, 0, unroll=10)
 
     def second(q, carry):
         low, middle, high = along_y(yc, q * 112, 48, y_low, y_high)
@@ -526,7 +526,7 @@
         pcz[pl.ds(pl.multiple_of(640 + q * 32, 32), 32), :] = middle.astype(BF16)
         return carry
 
-    lax.fori_loop(0, 40, second, 0, unroll=4)
+    lax.fori_loop(0, 40, second, 0, unroll=20)
     row = lax.broadcasted_iota(jnp.int32, (16, 128), 0)
     lane = lax.broadcasted_iota(jnp.int32, (16, 128), 1)
 

time: 49.2 us -> 48.8 us (level)
  waiting for transfers between devices: 9 us -> 9.74 us
  Pallas kernels: 23.8 us -> 23.2 us
    ppermute x12, waiting for transfers between devices: 9 us -> 9.74 us  [shifted(): return lax.ppermute(x, axis, [(i, (i + by) % size) for i in range(size)])]
    pallas_call x9, Pallas kernels: 19.5 us -> 18.8 us  [local_call(): pl.pallas_call(kernel, out_shape=list(outs), in_specs=specs, out_specs=ou...]
where the time goes in v7:
time: 48.8 us; the launch traced here: 48.6 us
  Pallas kernels  23.2 us (48%)
  starting transfers between devices  13.8 us (28%)
  waiting for transfers between devices  9.74 us (20%)
  between operations  1 us (2%)
  local copies, waits for them, and re-layouts  0.83 us (2%)
    pallas_call x9, Pallas kernels, local_call(): pl.pallas_call(kernel, out_shape=list(outs), in_specs=specs, out_specs=ou...  18.8 us
    ppermute x12, starting transfers between devices, shifted(): return lax.ppermute(x, axis, [(i, (i + by) % size) for i in range(size)])  13.8 us
    ppermute x12, waiting for transfers between devices, shifted(): return lax.ppermute(x, axis, [(i, (i + by) % size) for i in range(size)])  9.74 us
    pallas_call x1, Pallas kernels, pack(): pl.pallas_call(pack_kernel, out_shape=[jax.ShapeDtypeStruct((PAYLOAD, 128...  4.09 us
  transfers between devices with their start and end apart: 12, of which 5 were waited for; matrix products, arithmetic and copies ran while one was open for 0% of the time, Pallas kernels for 15%

profile of v7, /device:TPU:30, one launch (start us, length us, event | category | flops | bytes accessed | tf_op | source)
XLA Modules:
  0.0 48.6 jit_solution(8753694922670229811)
XLA Ops:
  0.6 0.0 copy-start.2
  0.6 0.0 copy-start.1
  0.7 0.0 copy-start.5
  0.7 0.8 %copy-done.5 = s32[1024]{0:T(1024)S(1)} copy-done((s32[1024]{0:T(1024)S(1)}, s32[1024]{0:T(1024)}, u32[]{:S(2)}) %copy-start.5) | copy-done | bytes 4120
  1.5 4.1 %pack.1 = (bf16[336,128]{1,0:T(8,128)(2,1)S(1)}, bf16[336,128]{1,0:T(8,128)(2,1)S(1)}, bf16[336,128]{1,0:T(8,128)(2,1)S(1)}, bf16[336,128]{1,0:T(8,128)(2,1)S(1)...) custom-call(s32[8,128]{1,0:T(8,128)S(1)} %bitcast.13, bf16[1024,512]{1,0:T(8,128)(2,1)} %jac.1, ...), custom_call_target="tpu_custom_call" | custom-call | tf_op jit(solution)/shard_map/pack/pallas_call | solution.py:211
  5.6 0.0 copy-start
  5.6 0.3 collective-permute-start
  5.9 1.8 %collective-permute-start.1 = (bf16[336,128]{1,0:T(8,128)(2,1)S(1)}, bf16[336,128]{1,0:T(8,128)(2,1)S(1)}, u32[]{:S(2)}, u32[]{:S(2)}) collective-permute-start(bf16[336,128]{1,0:T(8,128)(2,1)S(1)} %get-tuple-element.29), channel_id=1, source_target_pairs={{0,3},{1,0},{2,1},{3,2},{4,7},{5,4},{6,5},{7,6},{8,11},{9,8},{10,9... | collective-permute-start | bytes 258056 | tf_op jit(solution)/shard_map/ppermute | solution.py:717
  7.7 0.6 %collective-permute-start.2 = (bf16[336,128]{1,0:T(8,128)(2,1)S(1)}, bf16[336,128]{1,0:T(8,128)(2,1)S(1)}, u32[]{:S(2)}, u32[]{:S(2)}) collective-permute-start(bf16[336,128]{1,0:T(8,128)(2,1)S(1)} %get-tuple-element.30), channel_id=1, source_target_pairs={{0,4},{4,8},{8,12},{12,0},{1,5},{5,9},{9,13},{13,1},{2,6},{6,10},{... | collective-permute-start | bytes 258056 | tf_op jit(solution)/shard_map/ppermute | solution.py:717
  8.3 1.4 %collective-permute-start.3 = (bf16[336,128]{1,0:T(8,128)(2,1)S(1)}, bf16[336,128]{1,0:T(8,128)(2,1)S(1)}, u32[]{:S(2)}, u32[]{:S(2)}) collective-permute-start(bf16[336,128]{1,0:T(8,128)(2,1)S(1)} %get-tuple-element.31), channel_id=1, source_target_pairs={{0,12},{4,0},{8,4},{12,8},{1,13},{5,1},{9,5},{13,9},{2,14},{6,2},{... | collective-permute-start | bytes 258056 | tf_op jit(solution)/shard_map/ppermute | solution.py:717
  9.7 0.0 collective-permute-start.4
  9.7 0.4 collective-permute-done.first_arrived.a0
  10.1 2.6 %collective-permute-start.5 = (bf16[336,128]{1,0:T(8,128)(2,1)S(1)}, bf16[336,128]{1,0:T(8,128)(2,1)S(1)}, u32[]{:S(2)}, u32[]{:S(2)}) collective-permute-start(bf16[336,128]{1,0:T(8,128)(2,1)S(1)} %get-tuple-element.33), channel_id=1, source_target_pairs={{0,112},{16,0},{32,16},{48,32},{64,48},{80,64},{96,80},{112,96},{1... | collective-permute-start | bytes 258056 | tf_op jit(solution)/shard_map/ppermute | solution.py:717
  12.7 0.0 copy-done.2
  12.7 0.0 copy-done.1
  12.7 1.8 %jacobians.1._.jac_in = f32[512,1024]{1,0:T(8,128)S(1)} custom-call(s32[8,128]{1,0:T(8,128)S(1)} %get-tuple-element.34.spots, bf16[1024,512]{1,0:T(8,128)(2,1)S(1)} %copy-done.1, bf16[512,512]{1,0:T(8,128)(2,1)S(1)} %copy-done.2, bf16[336,128]{1,0:T(8,128)(2,1)S(1)} %collective-permute-done.first_arrived.a0), custom_call_target="tpu_custom_call" | custom-call | flops 2000000000 | bytes 1000000 | tf_op jit(solution)/shard_map/jacobians/pallas_call | solution.py:234
  14.5 0.0 copy-done
  14.5 0.0 copy-start.3
  14.5 1.8 %place.1.rows = f32[1040,16,128]{2,1,0:T(8,128)S(1)} custom-call(s32[1024]{0:T(1024)S(1)} %bitcast.14, bf16[1024,16,128]{2,1,0:T(8,128)(2,1)S(1)} %bitcast.11, f32[512,1024]{1,0:T(8,128)S(1)} %jacobians.1._.jac_in), custom_call_target="tpu_custom_call" | custom-call | flops 2000000000 | bytes 1000000 | tf_op jit(solution)/shard_map/place/pallas_call | solution.py:234
  16.3 0.0 copy-start.4
  16.3 0.0 collective-permute-done.1.a1
  16.3 0.0 collective-permute-done.2.a2
  16.3 0.0 collective-permute-done.3.a3
  16.3 0.0 collective-permute-done.4.a4
  16.4 0.0 collective-permute-done.5.a5
  16.4 0.0 copy-done.3
  16.4 6.0 %brick.1 = (bf16[8192,256]{1,0:T(8,128)(2,1)S(1)}, f32[1040,16,128]{2,1,0:T(8,128)S(1)}) custom-call(bf16[336,128]{1,0:T(8,128)(2,1)S(1)} %collective-permute-done.first_arrived.a0, bf16[336,128]{1,0:T(8,128)(2,1)S(1)} %collective-permute-done.1.a1, bf16[336,128]{1,0:T(8,128)(2,1)S(1)} %collective-permute-done.2.a2, ...), custom_call_target="tpu_custom_call", output_to_operand_aliasing={{1}: (9, {})} | custom-call | bytes 1000000 | tf_op jit(solution)/shard_map/brick/pallas_call | solution.py:234
  22.4 0.0 copy-done.4
  22.4 4.3 %filters.1 = (f32[8192,128]{1,0:T(8,128)S(1)}, f32[1280,128]{1,0:T(8,128)S(1)}, f32[640,128]{1,0:T(8,128)S(1)}, bf16[4,5760]{1,0:T(4,128)(2,1)S(1)}, bf16[4,5760]{1,0:T(4,128)(2,1)S(1)}) custom-call(bf16[8192,256]{1,0:T(8,128)(2,1)S(1)} %get-tuple-element.35.lhs, bf16[3,256,256]{2,1,0:T(8,128)(2,1)S(1)} %copy-done.4), custom_call_target="tpu_custom_call" | custom-call | bytes 1000000 | tf_op jit(solution)/shard_map/filters/pallas_call | solution.py:234
  26.7 1.5 %collective-permute-start.6 = (bf16[4,5760]{1,0:T(4,128)(2,1)S(1)}, bf16[4,5760]{1,0:T(4,128)(2,1)S(1)}, u32[]{:S(2)}, u32[]{:S(2)}) collective-permute-start(bf16[4,5760]{1,0:T(4,128)(2,1)S(1)} %get-tuple-element.39), channel_id=1, source_target_pairs={{0,1},{1,2},{2,3},{3,0},{4,5},{5,6},{6,7},{7,4},{8,9},{9,10},{10,1... | collective-permute-start | bytes 138248 | tf_op jit(solution)/shard_map/ppermute | solution.py:717
  28.2 0.6 %collective-permute-start.7 = (bf16[4,5760]{1,0:T(4,128)(2,1)S(1)}, bf16[4,5760]{1,0:T(4,128)(2,1)S(1)}, u32[]{:S(2)}, u32[]{:S(2)}) collective-permute-start(bf16[4,5760]{1,0:T(4,128)(2,1)S(1)} %get-tuple-element.40), channel_id=1, source_target_pairs={{0,3},{1,0},{2,1},{3,2},{4,7},{5,4},{6,5},{7,6},{8,11},{9,8},{10,9... | collective-permute-start | bytes 138248 | tf_op jit(solution)/shard_map/ppermute | solution.py:717
  28.8 0.0 copy-start.6
  28.8 0.0 copy-start.7
  28.8 2.0 %first_a.1 = (f32[3072,128]{1,0:T(8,128)S(1)}, f32[768,128]{1,0:T(8,128)S(1)}) custom-call(f32[8192,128]{1,0:T(8,128)S(1)} %get-tuple-element.36.wide), custom_call_target="tpu_custom_call" | custom-call | flops 3000000000 | bytes 1000000 | tf_op jit(solution)/shard_map/first_a/pallas_call | solution.py:234
  30.9 0.0 collective-permute-done.6.zl.from_low
  30.9 2.6 %collective-permute-done.7.zh.from_high = bf16[4,5760]{1,0:T(4,128)(2,1)S(1)} collective-permute-done((bf16[4,5760]{1,0:T(4,128)(2,1)S(1)}, bf16[4,5760]{1,0:T(4,128)(2,1)S(1)}, u32[]{:S(2)}, u32[]{:S(2)}) %collective-permute-start.7) | collective-permute-done | bytes 46112 | tf_op jit(solution)/shard_map/ppermute | solution.py:717
  33.5 0.0 copy-done.6
  33.5 0.0 copy-done.7
  33.5 0.3 y_edges.1
  33.8 1.9 %collective-permute-start.8 = (bf16[224,128]{1,0:T(8,128)(2,1)S(1)}, bf16[224,128]{1,0:T(8,128)(2,1)S(1)}, u32[]{:S(2)}, u32[]{:S(2)}) collective-permute-start(bf16[224,128]{1,0:T(8,128)(2,1)S(1)} %get-tuple-element.45), channel_id=1, source_target_pairs={{0,4},{4,8},{8,12},{12,0},{1,5},{5,9},{9,13},{13,1},{2,6},{6,10},{... | collective-permute-start | bytes 172040 | tf_op jit(solution)/shard_map/ppermute | solution.py:717
  35.7 0.2 collective-permute-start.9
  35.9 0.5 %z_main.1 = (f32[3072,128]{1,0:T(8,128)S(1)}, f32[1280,128]{1,0:T(8,128)S(1)}) custom-call(f32[3072,128]{1,0:T(8,128)S(1)} %get-tuple-element.37.main_a, f32[1280,128]{1,0:T(8,128)S(1)} %get-tuple-element.38.main_c, bf16[4,5760]{1,0:T(4,128)(2,1)S(1)} %collective-permute-done.6.zl.from_low, bf16[4,5760]{1,0:T(4,128)(2,1)S(1)} %collective-permute-done.7.zh.from_high, ...), custom_call_target="tpu_custom_call" | custom-call | flops 2000000000 | bytes 1000000 | tf_op jit(solution)/shard_map/z_main/pallas_call | solution.py:234
  36.4 1.6 %collective-permute-done.8.yl = bf16[224,128]{1,0:T(8,128)(2,1)S(1)} collective-permute-done((bf16[224,128]{1,0:T(8,128)(2,1)S(1)}, bf16[224,128]{1,0:T(8,128)(2,1)S(1)}, u32[]{:S(2)}, u32[]{:S(2)}) %collective-permute-start.8) | collective-permute-done | bytes 57376 | tf_op jit(solution)/shard_map/ppermute | solution.py:717
  38.0 3.1 %collective-permute-done.9.yh = bf16[224,128]{1,0:T(8,128)(2,1)S(1)} collective-permute-done((bf16[224,128]{1,0:T(8,128)(2,1)S(1)}, bf16[224,128]{1,0:T(8,128)(2,1)S(1)}, u32[]{:S(2)}, u32[]{:S(2)}) %collective-permute-start.9) | collective-permute-done | bytes 57376 | tf_op jit(solution)/shard_map/ppermute | solution.py:717
  41.1 0.2 x_edges.1
  41.4 0.0 collective-permute-start.10
  41.4 2.9 %collective-permute-start.11 = (bf16[704,128]{1,0:T(8,128)(2,1)S(1)}, bf16[704,128]{1,0:T(8,128)(2,1)S(1)}, u32[]{:S(2)}, u32[]{:S(2)}) collective-permute-start(bf16[704,128]{1,0:T(8,128)(2,1)S(1)} %get-tuple-element.50), channel_id=1, source_target_pairs={{0,112},{16,0},{32,16},{48,32},{64,48},{80,64},{96,80},{112,96},{1... | collective-permute-start | bytes 540680 | tf_op jit(solution)/shard_map/ppermute | solution.py:717
  44.3 1.2 %inside.1 = (f32[4,8,64,128]{3,2,1,0:T(8,128)}, f32[3072,128]{1,0:T(8,128)S(1)}, f32[1280,128]{1,0:T(8,128)S(1)}) custom-call(f32[3072,128]{1,0:T(8,128)S(1)} %get-tuple-element.41.sa_in.sa, f32[1280,128]{1,0:T(8,128)S(1)} %get-tuple-element.42.sc_in.sc, bf16[224,128]{1,0:T(8,128)(2,1)S(1)} %collective-permute-done.8.yl, ...), custom_call_target="tpu_custom_call" | custom-call | flops 2000000000 | bytes 1000000 | tf_op jit(solution)/shard_map/inside/pallas_call | solution.py:234
  45.5 2.0 %collective-permute-done.10.xl = bf16[704,128]{1,0:T(8,128)(2,1)S(1)} collective-permute-done((bf16[704,128]{1,0:T(8,128)(2,1)S(1)}, bf16[704,128]{1,0:T(8,128)(2,1)S(1)}, u32[]{:S(2)}, u32[]{:S(2)}) %collective-permute-start.10) | collective-permute-done | bytes 180256 | tf_op jit(solution)/shard_map/ppermute | solution.py:717
  47.5 0.0 collective-permute-done.11.xh
  47.5 1.0 %final.1 = (f32[4,4,32,64]{3,2,1,0:T(8,128)}, f32[4,8,64,128]{3,2,1,0:T(8,128)}) custom-call(f32[48,64,128]{2,1,0:T(8,128)S(1)} %bitcast.12, f32[1280,128]{1,0:T(8,128)S(1)} %get-tuple-element.48.sc, bf16[704,128]{1,0:T(8,128)(2,1)S(1)} %collective-permute-done.10.xl, ...), custom_call_target="tpu_custom_call", output_to_operand_aliasing={{1}: (4, {})} | custom-call | bytes 1000000 | tf_op jit(solution)/shard_map/final/pallas_call | solution.py:234
Async XLA Ops:
  0.6 12.1 %copy-start.2 = (bf16[512,512]{1,0:T(8,128)(2,1)S(1)}, bf16[512,512]{1,0:T(8,128)(2,1)}, u32[]{:S(2)}) copy-start(bf16[512,512]{1,0:T(8,128)(2,1)} %constant.10.clone.order) | copy-start | bytes 1572868
  0.6 12.0 %copy-start.1 = (bf16[1024,512]{1,0:T(8,128)(2,1)S(1)}, bf16[1024,512]{1,0:T(8,128)(2,1)}, u32[]{:S(2)}) copy-start(bf16[1024,512]{1,0:T(8,128)(2,1)} %jac.1) | copy-start | bytes 3145732
  0.7 0.8 %copy-start.5 = (s32[1024]{0:T(1024)S(1)}, s32[1024]{0:T(1024)}, u32[]{:S(2)}) copy-start(s32[1024]{0:T(1024)} %param.11) | copy-start | bytes 12292
  5.6 9.0 %copy-start = (bf16[1024,4,512]{2,1,0:T(4,128)(2,1)S(1)}, bf16[1024,4,512]{2,1,0:T(4,128)(2,1)}, u32[]{:S(2)}) copy-start(bf16[1024,4,512]{2,1,0:T(4,128)(2,1)} %param.9) | copy-start | bytes 12582916
  5.6 4.6 %collective-permute-start = (bf16[336,128]{1,0:T(8,128)(2,1)S(1)}, bf16[336,128]{1,0:T(8,128)(2,1)S(1)}, u32[]{:S(2)}, u32[]{:S(2)}) collective-permute-start(bf16[336,128]{1,0:T(8,128)(2,1)S(1)} %get-tuple-element.28), channel_id=1, source_target_pairs={{0,1},{1,2},{2,3},{3,0},{4,5},{5,6},{6,7},{7,4},{8,9},{9,10},{10,1... | collective-permute-start | bytes 258056 | tf_op jit(solution)/shard_map/ppermute | solution.py:717
  5.9 10.5 %collective-permute-start.1 = (bf16[336,128]{1,0:T(8,128)(2,1)S(1)}, bf16[336,128]{1,0:T(8,128)(2,1)S(1)}, u32[]{:S(2)}, u32[]{:S(2)}) collective-permute-start(bf16[336,128]{1,0:T(8,128)(2,1)S(1)} %get-tuple-element.29), channel_id=1, source_target_pairs={{0,3},{1,0},{2,1},{3,2},{4,7},{5,4},{6,5},{7,6},{8,11},{9,8},{10,9... | collective-permute-start | bytes 258056 | tf_op jit(solution)/shard_map/ppermute | solution.py:717
  7.7 8.7 %collective-permute-start.2 = (bf16[336,128]{1,0:T(8,128)(2,1)S(1)}, bf16[336,128]{1,0:T(8,128)(2,1)S(1)}, u32[]{:S(2)}, u32[]{:S(2)}) collective-permute-start(bf16[336,128]{1,0:T(8,128)(2,1)S(1)} %get-tuple-element.30), channel_id=1, source_target_pairs={{0,4},{4,8},{8,12},{12,0},{1,5},{5,9},{9,13},{13,1},{2,6},{6,10},{... | collective-permute-start | bytes 258056 | tf_op jit(solution)/shard_map/ppermute | solution.py:717
  8.3 8.1 %collective-permute-start.3 = (bf16[336,128]{1,0:T(8,128)(2,1)S(1)}, bf16[336,128]{1,0:T(8,128)(2,1)S(1)}, u32[]{:S(2)}, u32[]{:S(2)}) collective-permute-start(bf16[336,128]{1,0:T(8,128)(2,1)S(1)} %get-tuple-element.31), channel_id=1, source_target_pairs={{0,12},{4,0},{8,4},{12,8},{1,13},{5,1},{9,5},{13,9},{2,14},{6,2},{... | collective-permute-start | bytes 258056 | tf_op jit(solution)/shard_map/ppermute | solution.py:717
  9.7 6.7 %collective-permute-start.4 = (bf16[336,128]{1,0:T(8,128)(2,1)S(1)}, bf16[336,128]{1,0:T(8,128)(2,1)S(1)}, u32[]{:S(2)}, u32[]{:S(2)}) collective-permute-start(bf16[336,128]{1,0:T(8,128)(2,1)S(1)} %get-tuple-element.32), channel_id=1, source_target_pairs={{0,16},{16,32},{32,48},{48,64},{64,80},{80,96},{96,112},{112,0},{1... | collective-permute-start | bytes 258056 | tf_op jit(solution)/shard_map/ppermute | solution.py:717
  10.1 6.2 %collective-permute-start.5 = (bf16[336,128]{1,0:T(8,128)(2,1)S(1)}, bf16[336,128]{1,0:T(8,128)(2,1)S(1)}, u32[]{:S(2)}, u32[]{:S(2)}) collective-permute-start(bf16[336,128]{1,0:T(8,128)(2,1)S(1)} %get-tuple-element.33), channel_id=1, source_target_pairs={{0,112},{16,0},{32,16},{48,32},{64,48},{80,64},{96,80},{112,96},{1... | collective-permute-start | bytes 258056 | tf_op jit(solution)/shard_map/ppermute | solution.py:717
  14.5 1.8 %copy-start.3 = (bf16[512,512]{1,0:T(8,128)(2,1)S(1)}, bf16[512,512]{1,0:T(8,128)(2,1)}, u32[]{:S(2)}) copy-start(bf16[512,512]{1,0:T(8,128)(2,1)} %constant.11.clone.table) | copy-start | bytes 1572868
  16.3 6.1 %copy-start.4 = (bf16[3,256,256]{2,1,0:T(8,128)(2,1)S(1)}, bf16[3,256,256]{2,1,0:T(8,128)(2,1)}, u32[]{:S(2)}) copy-start(bf16[3,256,256]{2,1,0:T(8,128)(2,1)} %constant.12.clone.depths) | copy-start | bytes 1179652
  26.7 4.1 %collective-permute-start.6 = (bf16[4,5760]{1,0:T(4,128)(2,1)S(1)}, bf16[4,5760]{1,0:T(4,128)(2,1)S(1)}, u32[]{:S(2)}, u32[]{:S(2)}) collective-permute-start(bf16[4,5760]{1,0:T(4,128)(2,1)S(1)} %get-tuple-element.39), channel_id=1, source_target_pairs={{0,1},{1,2},{2,3},{3,0},{4,5},{5,6},{6,7},{7,4},{8,9},{9,10},{10,1... | collective-permute-start | bytes 138248 | tf_op jit(solution)/shard_map/ppermute | solution.py:717
  28.2 5.3 %collective-permute-start.7 = (bf16[4,5760]{1,0:T(4,128)(2,1)S(1)}, bf16[4,5760]{1,0:T(4,128)(2,1)S(1)}, u32[]{:S(2)}, u32[]{:S(2)}) collective-permute-start(bf16[4,5760]{1,0:T(4,128)(2,1)S(1)} %get-tuple-element.40), channel_id=1, source_target_pairs={{0,3},{1,0},{2,1},{3,2},{4,7},{5,4},{6,5},{7,6},{8,11},{9,8},{10,9... | collective-permute-start | bytes 138248 | tf_op jit(solution)/shard_map/ppermute | solution.py:717
  28.8 4.7 %copy-start.6 = (bf16[8,128]{1,0:T(8,128)(2,1)S(1)}, bf16[8,128]{1,0:T(8,128)(2,1)}, u32[]{:S(2)}) copy-start(bf16[8,128]{1,0:T(8,128)(2,1)} %constant.14.clone.spread_c) | copy-start | bytes 6148
  28.8 4.7 %copy-start.7 = (bf16[8,128]{1,0:T(8,128)(2,1)S(1)}, bf16[8,128]{1,0:T(8,128)(2,1)}, u32[]{:S(2)}) copy-start(bf16[8,128]{1,0:T(8,128)(2,1)} %constant.13.clone.spread_a) | copy-start | bytes 6148
  33.8 4.2 %collective-permute-start.8 = (bf16[224,128]{1,0:T(8,128)(2,1)S(1)}, bf16[224,128]{1,0:T(8,128)(2,1)S(1)}, u32[]{:S(2)}, u32[]{:S(2)}) collective-permute-start(bf16[224,128]{1,0:T(8,128)(2,1)S(1)} %get-tuple-element.45), channel_id=1, source_target_pairs={{0,4},{4,8},{8,12},{12,0},{1,5},{5,9},{9,13},{13,1},{2,6},{6,10},{... | collective-permute-start | bytes 172040 | tf_op jit(solution)/shard_map/ppermute | solution.py:717
  35.7 5.4 %collective-permute-start.9 = (bf16[224,128]{1,0:T(8,128)(2,1)S(1)}, bf16[224,128]{1,0:T(8,128)(2,1)S(1)}, u32[]{:S(2)}, u32[]{:S(2)}) collective-permute-start(bf16[224,128]{1,0:T(8,128)(2,1)S(1)} %get-tuple-element.46), channel_id=1, source_target_pairs={{0,12},{4,0},{8,4},{12,8},{1,13},{5,1},{9,5},{13,9},{2,14},{6,2},{... | collective-permute-start | bytes 172040 | tf_op jit(solution)/shard_map/ppermute | solution.py:717
  41.4 6.1 %collective-permute-start.10 = (bf16[704,128]{1,0:T(8,128)(2,1)S(1)}, bf16[704,128]{1,0:T(8,128)(2,1)S(1)}, u32[]{:S(2)}, u32[]{:S(2)}) collective-permute-start(bf16[704,128]{1,0:T(8,128)(2,1)S(1)} %get-tuple-element.49), channel_id=1, source_target_pairs={{0,16},{16,32},{32,48},{48,64},{64,80},{80,96},{96,112},{112,0},{1... | collective-permute-start | bytes 540680 | tf_op jit(solution)/shard_map/ppermute | solution.py:717
  41.4 6.1 %collective-permute-start.11 = (bf16[704,128]{1,0:T(8,128)(2,1)S(1)}, bf16[704,128]{1,0:T(8,128)(2,1)S(1)}, u32[]{:S(2)}, u32[]{:S(2)}) collective-permute-start(bf16[704,128]{1,0:T(8,128)(2,1)S(1)} %get-tuple-element.50), channel_id=1, source_target_pairs={{0,112},{16,0},{32,16},{48,32},{64,48},{80,64},{96,80},{112,96},{1... | collective-permute-start | bytes 540680 | tf_op jit(solution)/shard_map/ppermute | solution.py:717

commit v8 on v7

--- a/solution.py
+++ b/solution.py
@@ -422,7 +422,7 @@
         ref[pl.ds(base + size - width, width), :] = zero
         return carry
 
-    lax.fori_loop(0, count, pads, 0, unroll=4)
+    lax.fori_loop(0, count, pads, 0, unroll=count)
 
 
 def along_x(values, outputs, edge, x_low, x_high):
@@ -471,9 +471,9 @@
     place = jnp.where(iz == 0, 0, jnp.where(iz == 3, 2, 1))
     copy = pltpu.make_async_copy(depths.at[place], depth, sem)
     copy.start()
+    copy.wait()
     clear_pads(yb, 48, 176, 24)
     clear_pads(yc, 40, 112, 16)
-    copy.wait()
 
     def quarter(t, carry):
         for f in range(4):

time: 48.8 us -> 48.6 us (level)
  no operation moved by 1% of the time
where the time goes in v8:
time: 48.6 us; the launch traced here: 48.2 us
  Pallas kernels  23.1 us (48%)
  starting transfers between devices  13.8 us (28%)
  waiting for transfers between devices  9.48 us (20%)
  between operations  1 us (2%)
  local copies, waits for them, and re-layouts  0.83 us (2%)
    pallas_call x9, Pallas kernels, local_call(): pl.pallas_call(kernel, out_shape=list(outs), in_specs=specs, out_specs=ou...  18.6 us
    ppermute x12, starting transfers between devices, shifted(): return lax.ppermute(x, axis, [(i, (i + by) % size) for i in range(size)])  13.8 us
    ppermute x12, waiting for transfers between devices, shifted(): return lax.ppermute(x, axis, [(i, (i + by) % size) for i in range(size)])  9.48 us
    pallas_call x1, Pallas kernels, pack(): pl.pallas_call(pack_kernel, out_shape=[jax.ShapeDtypeStruct((PAYLOAD, 128...  4.09 us
  transfers between devices with their start and end apart: 12, of which 5 were waited for; matrix products, arithmetic and copies ran while one was open for 0% of the time, Pallas kernels for 15%

profile of v8, /device:TPU:30, one launch (start us, length us, event | category | flops | bytes accessed | tf_op | source)
XLA Modules:
  0.0 48.2 jit_solution(14574680240103688357)
XLA Ops:
  0.6 0.0 copy-start.2
  0.6 0.0 copy-start.1
  0.7 0.0 copy-start.5
  0.7 0.8 %copy-done.5 = s32[1024]{0:T(1024)S(1)} copy-done((s32[1024]{0:T(1024)S(1)}, s32[1024]{0:T(1024)}, u32[]{:S(2)}) %copy-start.5) | copy-done | bytes 4120
  1.5 4.1 %pack.1 = (bf16[336,128]{1,0:T(8,128)(2,1)S(1)}, bf16[336,128]{1,0:T(8,128)(2,1)S(1)}, bf16[336,128]{1,0:T(8,128)(2,1)S(1)}, bf16[336,128]{1,0:T(8,128)(2,1)S(1)...) custom-call(s32[8,128]{1,0:T(8,128)S(1)} %bitcast.13, bf16[1024,512]{1,0:T(8,128)(2,1)} %jac.1, ...), custom_call_target="tpu_custom_call" | custom-call | tf_op jit(solution)/shard_map/pack/pallas_call | solution.py:211
  5.6 0.0 copy-start
  5.6 0.6 %collective-permute-start = (bf16[336,128]{1,0:T(8,128)(2,1)S(1)}, bf16[336,128]{1,0:T(8,128)(2,1)S(1)}, u32[]{:S(2)}, u32[]{:S(2)}) collective-permute-start(bf16[336,128]{1,0:T(8,128)(2,1)S(1)} %get-tuple-element.28), channel_id=1, source_target_pairs={{0,1},{1,2},{2,3},{3,0},{4,5},{5,6},{6,7},{7,4},{8,9},{9,10},{10,1... | collective-permute-start | bytes 258056 | tf_op jit(solution)/shard_map/ppermute | solution.py:717
  6.2 1.5 %collective-permute-start.1 = (bf16[336,128]{1,0:T(8,128)(2,1)S(1)}, bf16[336,128]{1,0:T(8,128)(2,1)S(1)}, u32[]{:S(2)}, u32[]{:S(2)}) collective-permute-start(bf16[336,128]{1,0:T(8,128)(2,1)S(1)} %get-tuple-element.29), channel_id=1, source_target_pairs={{0,3},{1,0},{2,1},{3,2},{4,7},{5,4},{6,5},{7,6},{8,11},{9,8},{10,9... | collective-permute-start | bytes 258056 | tf_op jit(solution)/shard_map/ppermute | solution.py:717
  7.7 0.2 collective-permute-start.2
  7.9 1.8 %collective-permute-start.3 = (bf16[336,128]{1,0:T(8,128)(2,1)S(1)}, bf16[336,128]{1,0:T(8,128)(2,1)S(1)}, u32[]{:S(2)}, u32[]{:S(2)}) collective-permute-start(bf16[336,128]{1,0:T(8,128)(2,1)S(1)} %get-tuple-element.31), channel_id=1, source_target_pairs={{0,12},{4,0},{8,4},{12,8},{1,13},{5,1},{9,5},{13,9},{2,14},{6,2},{... | collective-permute-start | bytes 258056 | tf_op jit(solution)/shard_map/ppermute | solution.py:717
  9.7 0.0 collective-permute-start.4
  9.7 0.4 collective-permute-done.first_arrived.a0
  10.1 2.5 %collective-permute-start.5 = (bf16[336,128]{1,0:T(8,128)(2,1)S(1)}, bf16[336,128]{1,0:T(8,128)(2,1)S(1)}, u32[]{:S(2)}, u32[]{:S(2)}) collective-permute-start(bf16[336,128]{1,0:T(8,128)(2,1)S(1)} %get-tuple-element.33), channel_id=1, source_target_pairs={{0,112},{16,0},{32,16},{48,32},{64,48},{80,64},{96,80},{112,96},{1... | collective-permute-start | bytes 258056 | tf_op jit(solution)/shard_map/ppermute | solution.py:717
  12.7 0.0 copy-done.2
  12.7 0.0 copy-done.1
  12.7 1.8 %jacobians.1._.jac_in = f32[512,1024]{1,0:T(8,128)S(1)} custom-call(s32[8,128]{1,0:T(8,128)S(1)} %get-tuple-element.34.spots, bf16[1024,512]{1,0:T(8,128)(2,1)S(1)} %copy-done.1, bf16[512,512]{1,0:T(8,128)(2,1)S(1)} %copy-done.2, bf16[336,128]{1,0:T(8,128)(2,1)S(1)} %collective-permute-done.first_arrived.a0), custom_call_target="tpu_custom_call" | custom-call | flops 2000000000 | bytes 1000000 | tf_op jit(solution)/shard_map/jacobians/pallas_call | solution.py:234
  14.5 0.0 copy-done
  14.5 0.0 copy-start.3
  14.5 1.8 %place.1.rows = f32[1040,16,128]{2,1,0:T(8,128)S(1)} custom-call(s32[1024]{0:T(1024)S(1)} %bitcast.14, bf16[1024,16,128]{2,1,0:T(8,128)(2,1)S(1)} %bitcast.11, f32[512,1024]{1,0:T(8,128)S(1)} %jacobians.1._.jac_in), custom_call_target="tpu_custom_call" | custom-call | flops 2000000000 | bytes 1000000 | tf_op jit(solution)/shard_map/place/pallas_call | solution.py:234
  16.3 0.0 copy-start.4
  16.3 0.0 collective-permute-done.1.a1
  16.3 0.0 collective-permute-done.2.a2
  16.3 0.0 collective-permute-done.3.a3
  16.3 0.0 collective-permute-done.4.a4
  16.3 0.0 collective-permute-done.5.a5
  16.3 0.0 copy-done.3
  16.3 6.0 %brick.1 = (bf16[8192,256]{1,0:T(8,128)(2,1)S(1)}, f32[1040,16,128]{2,1,0:T(8,128)S(1)}) custom-call(bf16[336,128]{1,0:T(8,128)(2,1)S(1)} %collective-permute-done.first_arrived.a0, bf16[336,128]{1,0:T(8,128)(2,1)S(1)} %collective-permute-done.1.a1, bf16[336,128]{1,0:T(8,128)(2,1)S(1)} %collective-permute-done.2.a2, ...), custom_call_target="tpu_custom_call", output_to_operand_aliasing={{1}: (9, {})} | custom-call | bytes 1000000 | tf_op jit(solution)/shard_map/brick/pallas_call | solution.py:234
  22.4 0.0 copy-done.4
  22.4 4.1 %filters.1 = (f32[8192,128]{1,0:T(8,128)S(1)}, f32[1280,128]{1,0:T(8,128)S(1)}, f32[640,128]{1,0:T(8,128)S(1)}, bf16[4,5760]{1,0:T(4,128)(2,1)S(1)}, bf16[4,5760]{1,0:T(4,128)(2,1)S(1)}) custom-call(bf16[8192,256]{1,0:T(8,128)(2,1)S(1)} %get-tuple-element.35.lhs, bf16[3,256,256]{2,1,0:T(8,128)(2,1)S(1)} %copy-done.4), custom_call_target="tpu_custom_call" | custom-call | bytes 1000000 | tf_op jit(solution)/shard_map/filters/pallas_call | solution.py:234
  26.5 1.8 %collective-permute-start.6 = (bf16[4,5760]{1,0:T(4,128)(2,1)S(1)}, bf16[4,5760]{1,0:T(4,128)(2,1)S(1)}, u32[]{:S(2)}, u32[]{:S(2)}) collective-permute-start(bf16[4,5760]{1,0:T(4,128)(2,1)S(1)} %get-tuple-element.39), channel_id=1, source_target_pairs={{0,1},{1,2},{2,3},{3,0},{4,5},{5,6},{6,7},{7,4},{8,9},{9,10},{10,1... | collective-permute-start | bytes 138248 | tf_op jit(solution)/shard_map/ppermute | solution.py:717
  28.4 0.3 collective-permute-start.7
  28.6 0.0 copy-start.6
  28.6 0.0 copy-start.7
  28.6 2.0 %first_a.1 = (f32[3072,128]{1,0:T(8,128)S(1)}, f32[768,128]{1,0:T(8,128)S(1)}) custom-call(f32[8192,128]{1,0:T(8,128)S(1)} %get-tuple-element.36.wide), custom_call_target="tpu_custom_call" | custom-call | flops 3000000000 | bytes 1000000 | tf_op jit(solution)/shard_map/first_a/pallas_call | solution.py:234
  30.7 0.0 collective-permute-done.6.zl.from_low
  30.7 3.0 %collective-permute-done.7.zh.from_high = bf16[4,5760]{1,0:T(4,128)(2,1)S(1)} collective-permute-done((bf16[4,5760]{1,0:T(4,128)(2,1)S(1)}, bf16[4,5760]{1,0:T(4,128)(2,1)S(1)}, u32[]{:S(2)}, u32[]{:S(2)}) %collective-permute-start.7) | collective-permute-done | bytes 46112 | tf_op jit(solution)/shard_map/ppermute | solution.py:717
  33.6 0.0 copy-done.6
  33.6 0.0 copy-done.7
  33.6 0.3 y_edges.1
  34.0 1.3 %collective-permute-start.8 = (bf16[224,128]{1,0:T(8,128)(2,1)S(1)}, bf16[224,128]{1,0:T(8,128)(2,1)S(1)}, u32[]{:S(2)}, u32[]{:S(2)}) collective-permute-start(bf16[224,128]{1,0:T(8,128)(2,1)S(1)} %get-tuple-element.45), channel_id=1, source_target_pairs={{0,4},{4,8},{8,12},{12,0},{1,5},{5,9},{9,13},{13,1},{2,6},{6,10},{... | collective-permute-start | bytes 172040 | tf_op jit(solution)/shard_map/ppermute | solution.py:717
  35.3 0.8 %collective-permute-start.9 = (bf16[224,128]{1,0:T(8,128)(2,1)S(1)}, bf16[224,128]{1,0:T(8,128)(2,1)S(1)}, u32[]{:S(2)}, u32[]{:S(2)}) collective-permute-start(bf16[224,128]{1,0:T(8,128)(2,1)S(1)} %get-tuple-element.46), channel_id=1, source_target_pairs={{0,12},{4,0},{8,4},{12,8},{1,13},{5,1},{9,5},{13,9},{2,14},{6,2},{... | collective-permute-start | bytes 172040 | tf_op jit(solution)/shard_map/ppermute | solution.py:717
  36.1 0.5 %z_main.1 = (f32[3072,128]{1,0:T(8,128)S(1)}, f32[1280,128]{1,0:T(8,128)S(1)}) custom-call(f32[3072,128]{1,0:T(8,128)S(1)} %get-tuple-element.37.main_a, f32[1280,128]{1,0:T(8,128)S(1)} %get-tuple-element.38.main_c, bf16[4,5760]{1,0:T(4,128)(2,1)S(1)} %collective-permute-done.6.zl.from_low, bf16[4,5760]{1,0:T(4,128)(2,1)S(1)} %collective-permute-done.7.zh.from_high, ...), custom_call_target="tpu_custom_call" | custom-call | flops 2000000000 | bytes 1000000 | tf_op jit(solution)/shard_map/z_main/pallas_call | solution.py:234
  36.6 1.6 %collective-permute-done.8.yl = bf16[224,128]{1,0:T(8,128)(2,1)S(1)} collective-permute-done((bf16[224,128]{1,0:T(8,128)(2,1)S(1)}, bf16[224,128]{1,0:T(8,128)(2,1)S(1)}, u32[]{:S(2)}, u32[]{:S(2)}) %collective-permute-start.8) | collective-permute-done | bytes 57376 | tf_op jit(solution)/shard_map/ppermute | solution.py:717
  38.2 2.4 %collective-permute-done.9.yh = bf16[224,128]{1,0:T(8,128)(2,1)S(1)} collective-permute-done((bf16[224,128]{1,0:T(8,128)(2,1)S(1)}, bf16[224,128]{1,0:T(8,128)(2,1)S(1)}, u32[]{:S(2)}, u32[]{:S(2)}) %collective-permute-start.9) | collective-permute-done | bytes 57376 | tf_op jit(solution)/shard_map/ppermute | solution.py:717
  40.7 0.2 x_edges.1
  40.9 0.0 collective-permute-start.10
  40.9 2.9 %collective-permute-start.11 = (bf16[704,128]{1,0:T(8,128)(2,1)S(1)}, bf16[704,128]{1,0:T(8,128)(2,1)S(1)}, u32[]{:S(2)}, u32[]{:S(2)}) collective-permute-start(bf16[704,128]{1,0:T(8,128)(2,1)S(1)} %get-tuple-element.50), channel_id=1, source_target_pairs={{0,112},{16,0},{32,16},{48,32},{64,48},{80,64},{96,80},{112,96},{1... | collective-permute-start | bytes 540680 | tf_op jit(solution)/shard_map/ppermute | solution.py:717
  43.9 1.2 %inside.1 = (f32[4,8,64,128]{3,2,1,0:T(8,128)}, f32[3072,128]{1,0:T(8,128)S(1)}, f32[1280,128]{1,0:T(8,128)S(1)}) custom-call(f32[3072,128]{1,0:T(8,128)S(1)} %get-tuple-element.41.sa_in.sa, f32[1280,128]{1,0:T(8,128)S(1)} %get-tuple-element.42.sc_in.sc, bf16[224,128]{1,0:T(8,128)(2,1)S(1)} %collective-permute-done.8.yl, ...), custom_call_target="tpu_custom_call" | custom-call | flops 2000000000 | bytes 1000000 | tf_op jit(solution)/shard_map/inside/pallas_call | solution.py:234
  45.0 2.0 %collective-permute-done.10.xl = bf16[704,128]{1,0:T(8,128)(2,1)S(1)} collective-permute-done((bf16[704,128]{1,0:T(8,128)(2,1)S(1)}, bf16[704,128]{1,0:T(8,128)(2,1)S(1)}, u32[]{:S(2)}, u32[]{:S(2)}) %collective-permute-start.10) | collective-permute-done | bytes 180256 | tf_op jit(solution)/shard_map/ppermute | solution.py:717
  47.0 0.0 collective-permute-done.11.xh
  47.0 1.0 %final.1 = (f32[4,4,32,64]{3,2,1,0:T(8,128)}, f32[4,8,64,128]{3,2,1,0:T(8,128)}) custom-call(f32[48,64,128]{2,1,0:T(8,128)S(1)} %bitcast.12, f32[1280,128]{1,0:T(8,128)S(1)} %get-tuple-element.48.sc, bf16[704,128]{1,0:T(8,128)(2,1)S(1)} %collective-permute-done.10.xl, ...), custom_call_target="tpu_custom_call", output_to_operand_aliasing={{1}: (4, {})} | custom-call | bytes 1000000 | tf_op jit(solution)/shard_map/final/pallas_call | solution.py:234
Async XLA Ops:
  0.6 12.0 %copy-start.2 = (bf16[512,512]{1,0:T(8,128)(2,1)S(1)}, bf16[512,512]{1,0:T(8,128)(2,1)}, u32[]{:S(2)}) copy-start(bf16[512,512]{1,0:T(8,128)(2,1)} %constant.10.clone.order) | copy-start | bytes 1572868
  0.6 12.0 %copy-start.1 = (bf16[1024,512]{1,0:T(8,128)(2,1)S(1)}, bf16[1024,512]{1,0:T(8,128)(2,1)}, u32[]{:S(2)}) copy-start(bf16[1024,512]{1,0:T(8,128)(2,1)} %jac.1) | copy-start | bytes 3145732
  0.7 0.8 %copy-start.5 = (s32[1024]{0:T(1024)S(1)}, s32[1024]{0:T(1024)}, u32[]{:S(2)}) copy-start(s32[1024]{0:T(1024)} %param.11) | copy-start | bytes 12292
  5.6 8.9 %copy-start = (bf16[1024,4,512]{2,1,0:T(4,128)(2,1)S(1)}, bf16[1024,4,512]{2,1,0:T(4,128)(2,1)}, u32[]{:S(2)}) copy-start(bf16[1024,4,512]{2,1,0:T(4,128)(2,1)} %param.9) | copy-start | bytes 12582916
  5.6 4.6 %collective-permute-start = (bf16[336,128]{1,0:T(8,128)(2,1)S(1)}, bf16[336,128]{1,0:T(8,128)(2,1)S(1)}, u32[]{:S(2)}, u32[]{:S(2)}) collective-permute-start(bf16[336,128]{1,0:T(8,128)(2,1)S(1)} %get-tuple-element.28), channel_id=1, source_target_pairs={{0,1},{1,2},{2,3},{3,0},{4,5},{5,6},{6,7},{7,4},{8,9},{9,10},{10,1... | collective-permute-start | bytes 258056 | tf_op jit(solution)/shard_map/ppermute | solution.py:717
  6.2 10.1 %collective-permute-start.1 = (bf16[336,128]{1,0:T(8,128)(2,1)S(1)}, bf16[336,128]{1,0:T(8,128)(2,1)S(1)}, u32[]{:S(2)}, u32[]{:S(2)}) collective-permute-start(bf16[336,128]{1,0:T(8,128)(2,1)S(1)} %get-tuple-element.29), channel_id=1, source_target_pairs={{0,3},{1,0},{2,1},{3,2},{4,7},{5,4},{6,5},{7,6},{8,11},{9,8},{10,9... | collective-permute-start | bytes 258056 | tf_op jit(solution)/shard_map/ppermute | solution.py:717
  7.7 8.6 %collective-permute-start.2 = (bf16[336,128]{1,0:T(8,128)(2,1)S(1)}, bf16[336,128]{1,0:T(8,128)(2,1)S(1)}, u32[]{:S(2)}, u32[]{:S(2)}) collective-permute-start(bf16[336,128]{1,0:T(8,128)(2,1)S(1)} %get-tuple-element.30), channel_id=1, source_target_pairs={{0,4},{4,8},{8,12},{12,0},{1,5},{5,9},{9,13},{13,1},{2,6},{6,10},{... | collective-permute-start | bytes 258056 | tf_op jit(solution)/shard_map/ppermute | solution.py:717
  7.9 8.4 %collective-permute-start.3 = (bf16[336,128]{1,0:T(8,128)(2,1)S(1)}, bf16[336,128]{1,0:T(8,128)(2,1)S(1)}, u32[]{:S(2)}, u32[]{:S(2)}) collective-permute-start(bf16[336,128]{1,0:T(8,128)(2,1)S(1)} %get-tuple-element.31), channel_id=1, source_target_pairs={{0,12},{4,0},{8,4},{12,8},{1,13},{5,1},{9,5},{13,9},{2,14},{6,2},{... | collective-permute-start | bytes 258056 | tf_op jit(solution)/shard_map/ppermute | solution.py:717
  9.7 6.6 %collective-permute-start.4 = (bf16[336,128]{1,0:T(8,128)(2,1)S(1)}, bf16[336,128]{1,0:T(8,128)(2,1)S(1)}, u32[]{:S(2)}, u32[]{:S(2)}) collective-permute-start(bf16[336,128]{1,0:T(8,128)(2,1)S(1)} %get-tuple-element.32), channel_id=1, source_target_pairs={{0,16},{16,32},{32,48},{48,64},{64,80},{80,96},{96,112},{112,0},{1... | collective-permute-start | bytes 258056 | tf_op jit(solution)/shard_map/ppermute | solution.py:717
  10.1 6.2 %collective-permute-start.5 = (bf16[336,128]{1,0:T(8,128)(2,1)S(1)}, bf16[336,128]{1,0:T(8,128)(2,1)S(1)}, u32[]{:S(2)}, u32[]{:S(2)}) collective-permute-start(bf16[336,128]{1,0:T(8,128)(2,1)S(1)} %get-tuple-element.33), channel_id=1, source_target_pairs={{0,112},{16,0},{32,16},{48,32},{64,48},{80,64},{96,80},{112,96},{1... | collective-permute-start | bytes 258056 | tf_op jit(solution)/shard_map/ppermute | solution.py:717
  14.5 1.8 %copy-start.3 = (bf16[512,512]{1,0:T(8,128)(2,1)S(1)}, bf16[512,512]{1,0:T(8,128)(2,1)}, u32[]{:S(2)}) copy-start(bf16[512,512]{1,0:T(8,128)(2,1)} %constant.11.clone.table) | copy-start | bytes 1572868
  16.3 6.1 %copy-start.4 = (bf16[3,256,256]{2,1,0:T(8,128)(2,1)S(1)}, bf16[3,256,256]{2,1,0:T(8,128)(2,1)}, u32[]{:S(2)}) copy-start(bf16[3,256,256]{2,1,0:T(8,128)(2,1)} %constant.12.clone.depths) | copy-start | bytes 1179652
  26.5 4.1 %collective-permute-start.6 = (bf16[4,5760]{1,0:T(4,128)(2,1)S(1)}, bf16[4,5760]{1,0:T(4,128)(2,1)S(1)}, u32[]{:S(2)}, u32[]{:S(2)}) collective-permute-start(bf16[4,5760]{1,0:T(4,128)(2,1)S(1)} %get-tuple-element.39), channel_id=1, source_target_pairs={{0,1},{1,2},{2,3},{3,0},{4,5},{5,6},{6,7},{7,4},{8,9},{9,10},{10,1... | collective-permute-start | bytes 138248 | tf_op jit(solution)/shard_map/ppermute | solution.py:717
  28.4 5.3 %collective-permute-start.7 = (bf16[4,5760]{1,0:T(4,128)(2,1)S(1)}, bf16[4,5760]{1,0:T(4,128)(2,1)S(1)}, u32[]{:S(2)}, u32[]{:S(2)}) collective-permute-start(bf16[4,5760]{1,0:T(4,128)(2,1)S(1)} %get-tuple-element.40), channel_id=1, source_target_pairs={{0,3},{1,0},{2,1},{3,2},{4,7},{5,4},{6,5},{7,6},{8,11},{9,8},{10,9... | collective-permute-start | bytes 138248 | tf_op jit(solution)/shard_map/ppermute | solution.py:717
  28.6 5.0 %copy-start.6 = (bf16[8,128]{1,0:T(8,128)(2,1)S(1)}, bf16[8,128]{1,0:T(8,128)(2,1)}, u32[]{:S(2)}) copy-start(bf16[8,128]{1,0:T(8,128)(2,1)} %constant.14.clone.spread_c) | copy-start | bytes 6148
  28.6 5.0 %copy-start.7 = (bf16[8,128]{1,0:T(8,128)(2,1)S(1)}, bf16[8,128]{1,0:T(8,128)(2,1)}, u32[]{:S(2)}) copy-start(bf16[8,128]{1,0:T(8,128)(2,1)} %constant.13.clone.spread_a) | copy-start | bytes 6148
  34.0 4.2 %collective-permute-start.8 = (bf16[224,128]{1,0:T(8,128)(2,1)S(1)}, bf16[224,128]{1,0:T(8,128)(2,1)S(1)}, u32[]{:S(2)}, u32[]{:S(2)}) collective-permute-start(bf16[224,128]{1,0:T(8,128)(2,1)S(1)} %get-tuple-element.45), channel_id=1, source_target_pairs={{0,4},{4,8},{8,12},{12,0},{1,5},{5,9},{9,13},{13,1},{2,6},{6,10},{... | collective-permute-start | bytes 172040 | tf_op jit(solution)/shard_map/ppermute | solution.py:717
  35.3 5.4 %collective-permute-start.9 = (bf16[224,128]{1,0:T(8,128)(2,1)S(1)}, bf16[224,128]{1,0:T(8,128)(2,1)S(1)}, u32[]{:S(2)}, u32[]{:S(2)}) collective-permute-start(bf16[224,128]{1,0:T(8,128)(2,1)S(1)} %get-tuple-element.46), channel_id=1, source_target_pairs={{0,12},{4,0},{8,4},{12,8},{1,13},{5,1},{9,5},{13,9},{2,14},{6,2},{... | collective-permute-start | bytes 172040 | tf_op jit(solution)/shard_map/ppermute | solution.py:717
  40.9 6.1 %collective-permute-start.10 = (bf16[704,128]{1,0:T(8,128)(2,1)S(1)}, bf16[704,128]{1,0:T(8,128)(2,1)S(1)}, u32[]{:S(2)}, u32[]{:S(2)}) collective-permute-start(bf16[704,128]{1,0:T(8,128)(2,1)S(1)} %get-tuple-element.49), channel_id=1, source_target_pairs={{0,16},{16,32},{32,48},{48,64},{64,80},{80,96},{96,112},{112,0},{1... | collective-permute-start | bytes 540680 | tf_op jit(solution)/shard_map/ppermute | solution.py:717
  40.9 6.1 %collective-permute-start.11 = (bf16[704,128]{1,0:T(8,128)(2,1)S(1)}, bf16[704,128]{1,0:T(8,128)(2,1)S(1)}, u32[]{:S(2)}, u32[]{:S(2)}) collective-permute-start(bf16[704,128]{1,0:T(8,128)(2,1)S(1)} %get-tuple-element.50), channel_id=1, source_target_pairs={{0,112},{16,0},{32,16},{48,32},{64,48},{80,64},{96,80},{112,96},{1... | collective-permute-start | bytes 540680 | tf_op jit(solution)/shard_map/ppermute | solution.py:717
